TPU v7x, 1024 devices: a whole 4x4x32 slice. The times are simulated.
1024 devices in a mesh: dp: 8 (over x, core), node: 16 (over z_lo), local: 8 (over y, z_hi).
Axes of the slice: x: 4, y: 4, z: 32 (z_hi: 2, z_lo: 16; z = z_hi * 16 + z_lo), core: 2. Of those that a mesh axis runs over, the one named last changes fastest.
Arguments:
- grad_out: bfloat16 [16384, 2048], P(('dp', 'node', 'local')), may hold values from -6 to 6
- saved_pre: bfloat16 [16384, 8, 1536], P(('dp', 'node', 'local')), may hold values from -6 to 6
- gates: float32 [16384, 8], P(('dp', 'node', 'local')), may hold values from 0.1 to 1
- routes: int32 [16384, 8], P(('dp', 'node', 'local')), may hold values from 0 to 127, all different within a row; in each aligned block of 16 rows (0 to 15, 16 to 31, ...) at most 2 rows name the same one
- w_gate: bfloat16 [128, 2048, 768], P(('node', 'local')), may hold values from -0.125 to 0.125
- w_up: bfloat16 [128, 2048, 768], P(('node', 'local')), may hold values from -0.125 to 0.125
- w_down: bfloat16 [128, 768, 2048], P(('node', 'local')), may hold values from -0.21875 to 0.21875
Outputs:
- d_tokens: bfloat16 [16384, 2048], P(('dp', 'node', 'local'))
- d_gates: float32 [16384, 8], P(('dp', 'node', 'local'))
- d_down: bfloat16 [128, 768, 2048], P(('node', 'local'), 'dp')
Inputs may be any that keep to these rules, and one draw needn't show every extreme that they name: `routes`: within the rows of one device (aligned blocks of 16 tokens) no expert is named by more than 2 tokens, a bound that some block reaches.
All inputs are finite; a program needn't handle non-finite values.
Results may differ from a plain program's by a relative error of at most 0.017.
Values may be sent and summed in bfloat16 or wider, within the bound.
No kernel may reach another device: no remote copies, remote signals or barrier semaphores. Data moves between devices by JAX's collectives and lax.ppermute only.
A program may use at most 64 MiB of HBM per device.

v0:
```python
import jax
import jax.numpy as jnp
from jax import lax
from jax.sharding import PartitionSpec as P


def expert_rows(weight_rows, pre_rows, gate_weight, up_weight, down_weight):
    hidden_width = down_weight.shape[0]
    gate_pre = pre_rows[:, :hidden_width].astype(jnp.float32)
    up_pre = pre_rows[:, hidden_width:].astype(jnp.float32)
    sigmoid_gate = jax.nn.sigmoid(gate_pre)
    activated = gate_pre * sigmoid_gate
    hidden = (activated * up_pre).astype(jnp.bfloat16)
    hidden_grad = lax.dot_general(
        weight_rows, down_weight, (((1,), (1,)), ((), ())), preferred_element_type=jnp.float32
    )
    gate_dots = jnp.sum(hidden.astype(jnp.float32) * hidden_grad, axis=1).astype(jnp.bfloat16)
    gate_grad = (
        hidden_grad * up_pre * sigmoid_gate * (1.0 + gate_pre * (1.0 - sigmoid_gate))
    ).astype(jnp.bfloat16)
    up_grad = (hidden_grad * activated).astype(jnp.bfloat16)
    contract = (((1,), (1,)), ((), ()))
    route_grad = lax.dot_general(
        gate_grad, gate_weight, contract, preferred_element_type=jnp.float32
    )
    route_grad = route_grad + lax.dot_general(
        up_grad, up_weight, contract, preferred_element_type=jnp.float32
    )
    return (hidden, route_grad.astype(jnp.bfloat16), gate_dots)


def shards(grad_out, saved_pre, gates, routes, w_gate, w_up, w_down):
    tok_count, topk_count = routes.shape
    model_width = grad_out.shape[1]
    pre_width = saved_pre.shape[2]
    node_count = lax.axis_size("node")
    local_count = lax.axis_size("local")
    expert_count = node_count * local_count
    capacity = min(tok_count, max(2, 2 * tok_count * topk_count // expert_count))
    route_count = tok_count * topk_count
    slot_count = expert_count * capacity
    flat_routes = routes.reshape(route_count)
    onehot = (flat_routes[:, None] == jnp.arange(expert_count, dtype=jnp.int32)[None, :]).astype(
        jnp.int32
    )
    within = jnp.sum(jnp.cumsum(onehot, axis=0) * onehot, axis=1) - 1
    target = flat_routes * capacity + within
    weighted = (gates[:, :, None] * grad_out[:, None, :].astype(jnp.float32)).astype(jnp.bfloat16)
    weighted = weighted.reshape(route_count, model_width)
    pre_flat = saved_pre.reshape(route_count, pre_width)
    send_weighted = jnp.zeros((slot_count, model_width), jnp.bfloat16).at[target].set(weighted)
    send_weighted = send_weighted.reshape(node_count, local_count, capacity, model_width)
    send_pre = jnp.zeros((slot_count, pre_width), jnp.bfloat16).at[target].set(pre_flat)
    send_pre = send_pre.reshape(node_count, local_count, capacity, pre_width)
    recv_weighted, recv_pre = (
        lax.all_to_all(
            lax.all_to_all(send_weighted, "node", split_axis=0, concat_axis=0, tiled=True),
            "local",
            split_axis=1,
            concat_axis=1,
            tiled=True,
        ),
        lax.all_to_all(
            lax.all_to_all(send_pre, "node", split_axis=0, concat_axis=0, tiled=True),
            "local",
            split_axis=1,
            concat_axis=1,
            tiled=True,
        ),
    )
    weight_rows = recv_weighted.reshape(slot_count, model_width)
    pre_rows = recv_pre.reshape(slot_count, pre_width)
    hidden, route_grad, gate_dots = expert_rows(
        weight_rows, pre_rows, w_gate[0], w_up[0], w_down[0]
    )
    route_grad = route_grad.reshape(node_count, local_count, capacity, model_width)
    gate_dots = gate_dots.reshape(node_count, local_count, capacity)
    back_grad, back_dots = (
        lax.all_to_all(
            lax.all_to_all(route_grad, "node", split_axis=0, concat_axis=0, tiled=True),
            "local",
            split_axis=1,
            concat_axis=1,
            tiled=True,
        ),
        lax.all_to_all(
            lax.all_to_all(gate_dots, "node", split_axis=0, concat_axis=0, tiled=True),
            "local",
            split_axis=1,
            concat_axis=1,
            tiled=True,
        ),
    )
    d_down = lax.psum_scatter(
        lax.dot_general(
            hidden, weight_rows, (((0,), (0,)), ((), ())), preferred_element_type=jnp.float32
        ).astype(jnp.bfloat16),
        "dp",
        scatter_dimension=0,
        tiled=True,
    )
    returned_rows = back_grad.reshape(slot_count, model_width)[target]
    d_tokens = jnp.sum(
        returned_rows.reshape(tok_count, topk_count, model_width).astype(jnp.float32), axis=1
    ).astype(jnp.bfloat16)
    d_gates = (
        back_dots.reshape(slot_count)[target].reshape(tok_count, topk_count).astype(jnp.float32)
        / gates
    )
    return (d_tokens, d_gates, d_down[None])


def solution(mesh):
    in_specs = (
        P(("dp", "node", "local"), None),
        P(("dp", "node", "local"), None, None),
        P(("dp", "node", "local"), None),
        P(("dp", "node", "local"), None),
        P(("node", "local"), None, None),
        P(("node", "local"), None, None),
        P(("node", "local"), None, None),
    )
    out_specs = (
        P(("dp", "node", "local"), None),
        P(("dp", "node", "local"), None),
        P(("node", "local"), "dp", None),
    )
    return jax.shard_map(shards, mesh=mesh, in_specs=in_specs, out_specs=out_specs, check_vma=False)
```

profile of v0, /device:TPU:35, one launch (start us, length us, event | category | flops | bytes accessed | tf_op | source)
XLA Modules:
  0.0 720.1 jit_solution(3176341524251618266)
XLA Ops:
  7.2 0.8 broadcast_multiply_fusion
  8.0 0.9 copy.46
  9.3 0.2 reduce_window_sum.11
  9.5 0.2 select_reduce_fusion
  9.6 2.6 scatter_custom_fusion.1
  12.3 2.8 reshape.84
  15.1 25.3 %all-to-all-start.2 = ((bf16[16,8,2,1536]{3,2,1,0:T(2,128)(2,1)}), bf16[16,8,2,1536]{3,2,1,0:T(2,128)(2,1)}, u32[]{:S(2)}, u32[]{:S(2)}) async-start(bf16[16,8,2,1536]{3,2,1,0:T(2,128)(2,1)} %reshape.84), calls=%async_computation.2 | async-start | bytes 1572864 | tf_op jit(solution)/shard_map/all_to_all | solution.py:64
  40.6 2.6 scatter_custom_fusion
  43.2 2.5 reshape.81
  45.7 63.7 %all-to-all-done.2 = bf16[16,8,2,1536]{3,2,1,0:T(2,128)(2,1)} async-done(((bf16[16,8,2,1536]{3,2,1,0:T(2,128)(2,1)}), bf16[16,8,2,1536]{3,2,1,0:T(2,128)(2,1)}, u32[]{:S(2)}, u32[]{:S(2)}) %all-to-all-start.2) | async-done | bytes 786464 | tf_op jit(solution)/shard_map/all_to_all | solution.py:64
  109.5 16.2 %all-to-all-start = ((bf16[16,8,2,2048]{3,2,1,0:T(2,128)(2,1)}), bf16[16,8,2,2048]{3,2,1,0:T(2,128)(2,1)}, u32[]{:S(2)}, u32[]{:S(2)}) async-start(bf16[16,8,2,2048]{3,2,1,0:T(2,128)(2,1)} %reshape.81), calls=%async_computation | async-start | bytes 2097152 | tf_op jit(solution)/shard_map/all_to_all | solution.py:57
  125.7 2.6 copy.50
  128.3 87.2 %all-to-all-done = bf16[16,8,2,2048]{3,2,1,0:T(2,128)(2,1)} async-done(((bf16[16,8,2,2048]{3,2,1,0:T(2,128)(2,1)}), bf16[16,8,2,2048]{3,2,1,0:T(2,128)(2,1)}, u32[]{:S(2)}, u32[]{:S(2)}) %all-to-all-start) | async-done | bytes 1048608 | tf_op jit(solution)/shard_map/all_to_all | solution.py:57
  215.5 13.6 %all-to-all-start.3 = ((bf16[16,8,2,1536]{3,2,0,1:T(2,128)(2,1)}), bf16[16,8,2,1536]{3,2,0,1:T(2,128)(2,1)}, u32[]{:S(2)}, u32[]{:S(2)}) async-start(bf16[16,8,2,1536]{3,2,0,1:T(2,128)(2,1)} %copy.50), calls=%async_computation.3 | async-start | bytes 1572864 | tf_op jit(solution)/shard_map/all_to_all | solution.py:63
  229.0 3.0 copy.48
  232.1 107.5 %all-to-all-done.3 = bf16[16,8,2,1536]{3,2,0,1:T(2,128)(2,1)} async-done(((bf16[16,8,2,1536]{3,2,0,1:T(2,128)(2,1)}), bf16[16,8,2,1536]{3,2,0,1:T(2,128)(2,1)}, u32[]{:S(2)}, u32[]{:S(2)}) %all-to-all-start.3) | async-done | bytes 786464 | tf_op jit(solution)/shard_map/all_to_all | solution.py:63
  339.6 4.2 all-to-all-start.1
  343.9 2.7 copy.51
  346.6 3.0 reshape.85
  349.6 44.3 %all-to-all-done.1 = bf16[16,8,2,2048]{3,2,0,1:T(2,128)(2,1)} async-done(((bf16[16,8,2,2048]{3,2,0,1:T(2,128)(2,1)}), bf16[16,8,2,2048]{3,2,0,1:T(2,128)(2,1)}, u32[]{:S(2)}, u32[]{:S(2)}) %all-to-all-start.1) | async-done | bytes 1048608 | tf_op jit(solution)/shard_map/all_to_all | solution.py:56
  393.8 3.2 copy.49
  397.0 2.2 reshape.82
  399.2 4.3 multiply_reduce_fusion
  403.5 0.2 convert_element_type.61
  403.7 0.8 copy.54
  404.5 33.0 %all-to-all-start.6 = ((bf16[16,8,2]{1,2,0:T(2,128)(2,1)}), bf16[16,8,2]{1,2,0:T(2,128)(2,1)S(1)}, u32[]{:S(2)}, u32[]{:S(2)}) async-start(bf16[16,8,2]{1,2,0:T(2,128)(2,1)} %copy.54), calls=%async_computation.6 | async-start | bytes 16384 | tf_op jit(solution)/shard_map/all_to_all | solution.py:87
  437.5 2.4 fusion
  440.0 0.2 copy-done.5
  440.2 2.2 fusion.9
  442.3 2.5 reshape.86
  444.9 10.3 %all-to-all-done.6 = bf16[16,8,2]{1,2,0:T(2,128)(2,1)S(1)} async-done(((bf16[16,8,2]{1,2,0:T(2,128)(2,1)}), bf16[16,8,2]{1,2,0:T(2,128)(2,1)S(1)}, u32[]{:S(2)}, u32[]{:S(2)}) %all-to-all-start.6) | async-done | bytes 544 | tf_op jit(solution)/shard_map/all_to_all | solution.py:87
  455.1 8.7 %all-to-all-start.4 = ((bf16[16,8,2,2048]{3,2,1,0:T(2,128)(2,1)}), bf16[16,8,2,2048]{3,2,1,0:T(2,128)(2,1)}, u32[]{:S(2)}, u32[]{:S(2)}) async-start(bf16[16,8,2,2048]{3,2,1,0:T(2,128)(2,1)} %reshape.86), calls=%async_computation.4 | async-start | bytes 2097152 | tf_op jit(solution)/shard_map/all_to_all | solution.py:80
  463.8 0.7 copy.55
  464.5 89.1 %all-to-all-done.4 = bf16[16,8,2,2048]{3,2,1,0:T(2,128)(2,1)} async-done(((bf16[16,8,2,2048]{3,2,1,0:T(2,128)(2,1)}), bf16[16,8,2,2048]{3,2,1,0:T(2,128)(2,1)}, u32[]{:S(2)}, u32[]{:S(2)}) %all-to-all-start.4) | async-done | bytes 1048608 | tf_op jit(solution)/shard_map/all_to_all | solution.py:80
  553.6 8.2 %all-to-all-start.7 = ((bf16[16,8,2]{0,2,1:T(2,128)(2,1)}), bf16[16,8,2]{0,2,1:T(2,128)(2,1)S(1)}, u32[]{:S(2)}, u32[]{:S(2)}) async-start(bf16[16,8,2]{0,2,1:T(2,128)(2,1)} %copy.55), calls=%async_computation.7 | async-start | bytes 8192 | tf_op jit(solution)/shard_map/all_to_all | solution.py:86
  561.8 3.1 copy.52
  564.9 20.2 %all-to-all-done.7 = bf16[16,8,2]{0,2,1:T(2,128)(2,1)S(1)} async-done(((bf16[16,8,2]{0,2,1:T(2,128)(2,1)}), bf16[16,8,2]{0,2,1:T(2,128)(2,1)S(1)}, u32[]{:S(2)}, u32[]{:S(2)}) %all-to-all-start.7) | async-done | bytes 544 | tf_op jit(solution)/shard_map/all_to_all | solution.py:86
  585.1 4.2 all-to-all-start.5
  589.4 4.2 convolution_convert_fusion
  593.6 0.1 copy.56
  593.8 0.1 reshape.89
  593.9 1.2 gather_fusion.1
  595.3 0.7 copy.58
  596.0 106.2 %all-to-all-done.5 = bf16[16,8,2,2048]{3,2,0,1:T(2,128)(2,1)} async-done(((bf16[16,8,2,2048]{3,2,0,1:T(2,128)(2,1)}), bf16[16,8,2,2048]{3,2,0,1:T(2,128)(2,1)}, u32[]{:S(2)}, u32[]{:S(2)}) %all-to-all-start.5) | async-done | bytes 1048608 | tf_op jit(solution)/shard_map/all_to_all | solution.py:79
  702.2 3.2 copy.53
  705.4 2.2 reshape.87
  707.6 3.6 gather_fusion
  711.2 2.0 bitcast_reduce_fusion
  (25 shorter events, 0.7 us)
Async XLA Ops:
  7.2 430.3 %copy-start = (bf16[1,2048,768]{2,1,0:T(8,128)(2,1)S(1)}, bf16[1,2048,768]{2,1,0:T(8,128)(2,1)}, u32[]{:S(2)}) copy-start(bf16[1,2048,768]{2,1,0:T(8,128)(2,1)} %param.12) | copy-start | bytes 9437188
  7.2 33.3 %copy-start.3 = (f32[16,8]{0,1:T(8,128)S(1)}, f32[16,8]{0,1:T(8,128)}, u32[]{:S(2)}) copy-start(f32[16,8]{0,1:T(8,128)} %param.9) | copy-start | bytes 1540
  7.2 33.4 %copy-start.2 = (bf16[16,2048]{1,0:T(8,128)(2,1)S(1)}, bf16[16,2048]{1,0:T(8,128)(2,1)}, u32[]{:S(2)}) copy-start(bf16[16,2048]{1,0:T(8,128)(2,1)} %param.7) | copy-start | bytes 196612
  15.1 94.4 %all-to-all-start.2 = ((bf16[16,8,2,1536]{3,2,1,0:T(2,128)(2,1)}), bf16[16,8,2,1536]{3,2,1,0:T(2,128)(2,1)}, u32[]{:S(2)}, u32[]{:S(2)}) async-start(bf16[16,8,2,1536]{3,2,1,0:T(2,128)(2,1)} %reshape.84), calls=%async_computation.2 | async-start | bytes 1572864 | tf_op jit(solution)/shard_map/all_to_all | solution.py:64
  109.5 106.0 %all-to-all-start = ((bf16[16,8,2,2048]{3,2,1,0:T(2,128)(2,1)}), bf16[16,8,2,2048]{3,2,1,0:T(2,128)(2,1)}, u32[]{:S(2)}, u32[]{:S(2)}) async-start(bf16[16,8,2,2048]{3,2,1,0:T(2,128)(2,1)} %reshape.81), calls=%async_computation | async-start | bytes 2097152 | tf_op jit(solution)/shard_map/all_to_all | solution.py:57
  215.5 124.1 %all-to-all-start.3 = ((bf16[16,8,2,1536]{3,2,0,1:T(2,128)(2,1)}), bf16[16,8,2,1536]{3,2,0,1:T(2,128)(2,1)}, u32[]{:S(2)}, u32[]{:S(2)}) async-start(bf16[16,8,2,1536]{3,2,0,1:T(2,128)(2,1)} %copy.50), calls=%async_computation.3 | async-start | bytes 1572864 | tf_op jit(solution)/shard_map/all_to_all | solution.py:63
  339.6 54.2 %all-to-all-start.1 = ((bf16[16,8,2,2048]{3,2,0,1:T(2,128)(2,1)}), bf16[16,8,2,2048]{3,2,0,1:T(2,128)(2,1)}, u32[]{:S(2)}, u32[]{:S(2)}) async-start(bf16[16,8,2,2048]{3,2,0,1:T(2,128)(2,1)} %copy.48), calls=%async_computation.1 | async-start | bytes 2097152 | tf_op jit(solution)/shard_map/all_to_all | solution.py:56
  404.5 50.7 %all-to-all-start.6 = ((bf16[16,8,2]{1,2,0:T(2,128)(2,1)}), bf16[16,8,2]{1,2,0:T(2,128)(2,1)S(1)}, u32[]{:S(2)}, u32[]{:S(2)}) async-start(bf16[16,8,2]{1,2,0:T(2,128)(2,1)} %copy.54), calls=%async_computation.6 | async-start | bytes 16384 | tf_op jit(solution)/shard_map/all_to_all | solution.py:87
  437.5 2.4 copy-start.1
  437.5 2.5 copy-start.4
  437.5 2.7 copy-start.5
  455.1 98.5 %all-to-all-start.4 = ((bf16[16,8,2,2048]{3,2,1,0:T(2,128)(2,1)}), bf16[16,8,2,2048]{3,2,1,0:T(2,128)(2,1)}, u32[]{:S(2)}, u32[]{:S(2)}) async-start(bf16[16,8,2,2048]{3,2,1,0:T(2,128)(2,1)} %reshape.86), calls=%async_computation.4 | async-start | bytes 2097152 | tf_op jit(solution)/shard_map/all_to_all | solution.py:80
  553.6 31.5 %all-to-all-start.7 = ((bf16[16,8,2]{0,2,1:T(2,128)(2,1)}), bf16[16,8,2]{0,2,1:T(2,128)(2,1)S(1)}, u32[]{:S(2)}, u32[]{:S(2)}) async-start(bf16[16,8,2]{0,2,1:T(2,128)(2,1)} %copy.55), calls=%async_computation.7 | async-start | bytes 8192 | tf_op jit(solution)/shard_map/all_to_all | solution.py:86
  585.1 117.1 %all-to-all-start.5 = ((bf16[16,8,2,2048]{3,2,0,1:T(2,128)(2,1)}), bf16[16,8,2,2048]{3,2,0,1:T(2,128)(2,1)}, u32[]{:S(2)}, u32[]{:S(2)}) async-start(bf16[16,8,2,2048]{3,2,0,1:T(2,128)(2,1)} %copy.52), calls=%async_computation.5 | async-start | bytes 2097152 | tf_op jit(solution)/shard_map/all_to_all | solution.py:79
  589.3 123.9 %reduce-scatter.2.cloned.1.call-start = ((), (), s32[]{:S(2)}) async-start(), calls=%async_computation.9 | async-start | bytes 3538944 | tf_op jit(solution)/shard_map/reduce_scatter | solution.py:94
Sparse Core Ops, SparseCore 0:
  594.2 58.2 reduce-scatter.1
where the time goes:
time: 721 us; the launch traced here: 720 us
  waiting for transfers between devices  528 us (73%)
  starting transfers between devices  114 us (16%)
  local copies, waits for them, and re-layouts  44.7 us (6%)
  between operations  14.2 us (2%)
  matrix products  13.1 us (2%)
    all_to_all x1, waiting for transfers between devices, shards(): lax.all_to_all(lax.all_to_all(send_pre, 'node', split_axis=0, concat_axis...  108 us
    all_to_all x1, waiting for transfers between devices, shards(): lax.all_to_all(lax.all_to_all(route_grad, 'node', split_axis=0, concat_ax...  106 us
    all_to_all x1, waiting for transfers between devices, shards(): lax.all_to_all(route_grad, 'node', split_axis=0, concat_axis=0, tiled=True)  89.1 us
    all_to_all x1, waiting for transfers between devices, shards(): lax.all_to_all(send_weighted, 'node', split_axis=0, concat_axis=0, tiled=...  87.2 us
    all_to_all x1, waiting for transfers between devices, shards(): lax.all_to_all(send_pre, 'node', split_axis=0, concat_axis=0, tiled=True)  63.7 us
    all_to_all x1, waiting for transfers between devices, shards(): lax.all_to_all(lax.all_to_all(send_weighted, 'node', split_axis=0, concat...  44.3 us
    all_to_all x1, starting transfers between devices, shards(): lax.all_to_all(gate_dots, 'node', split_axis=0, concat_axis=0, tiled=True)  33 us
    all_to_all x1, starting transfers between devices, shards(): lax.all_to_all(send_pre, 'node', split_axis=0, concat_axis=0, tiled=True)  25.3 us
  transfers between devices with their start and end apart: 9, of which 8 were waited for; matrix products, arithmetic and copies ran while one was open for 6% of the time, Pallas kernels for 0%

commit v1 on v0

v1 whole, which is shorter than its diff:
```python
import jax
import jax.numpy as jnp
from jax import lax
from jax.sharding import Mesh, PartitionSpec as P

RING = ("node", "zh")
CAP = 2


def dot_rows(left, right, contract):
    return lax.dot_general(left, right, ((contract[:1], contract[1:]), ((), ())), preferred_element_type=jnp.float32)


def expert_of(ring_index, column):
    return (ring_index // 2) * 8 + column * 2 + ring_index % 2


def slot_masks(routes, experts):
    named = routes[..., None] == experts
    hits = jnp.any(named, axis=-2)
    counts = hits.astype(jnp.int32)
    before = jnp.cumsum(counts, axis=-2) - counts
    taken = hits[..., None] & (before[..., None] == jnp.arange(CAP, dtype=jnp.int32))
    return named, taken


def shards(grad_out, saved_pre, gates, routes, w_gate, w_up, w_down):
    tok, topk = routes.shape
    width = grad_out.shape[1]
    pre_width = saved_pre.shape[2]
    hidden_width = pre_width // 2
    ring = lax.axis_size("node") * lax.axis_size("zh")
    cols = lax.axis_size("y")
    me_y = lax.axis_index("y")
    f32, bf16 = jnp.float32, jnp.bfloat16
    ring_at = jnp.arange(ring, dtype=jnp.int32)

    gate_hi = lax.reduce_precision(gates, 8, 7)
    gate_mid = lax.reduce_precision(gates - gate_hi, 8, 7)
    gate_low = gates - gate_hi - gate_mid
    facts = jnp.concatenate([routes.astype(f32), gate_hi, gate_mid, gate_low], axis=1).astype(bf16)
    facts = jnp.pad(facts, ((0, 0), (0, 128 - 4 * topk)))
    payload = jnp.concatenate([grad_out, facts], axis=1)
    payload = jnp.broadcast_to(payload[None], (cols,) + payload.shape)
    column = lax.all_to_all(payload, "y", 0, 0, tiled=True)
    grad_col = column[:, :, :width].reshape(cols * tok, width)
    facts = column[:, :, width : width + 4 * topk].astype(f32)
    routes_col = facts[:, :, :topk].astype(jnp.int32)
    gates_col = facts[:, :, topk : 2 * topk] + facts[:, :, 2 * topk : 3 * topk] + facts[:, :, 3 * topk :]

    all_experts = expert_of(ring_at[None, :], jnp.arange(cols, dtype=jnp.int32)[:, None]).reshape(-1)
    named, taken = slot_masks(routes, all_experts)
    pick = named[..., None] & taken[:, None]
    pick = pick.reshape(tok * topk, cols * ring * CAP).astype(bf16)
    send_pre = dot_rows(pick, saved_pre.reshape(tok * topk, pre_width), (0, 0)).astype(bf16)
    pre_col = lax.all_to_all(send_pre.reshape(cols, ring * CAP, pre_width), "y", 0, 0, tiled=True)
    slots = cols * ring * CAP
    at = jnp.arange(slots, dtype=jnp.int32)
    origin = (at // CAP % cols) * (ring * CAP) + (at // (CAP * cols)) * CAP + at % CAP
    swap = (origin[:, None] == at[None, :]).astype(bf16)
    pre_ring = dot_rows(swap, pre_col.reshape(slots, pre_width), (1, 0)).astype(bf16)
    pre_ring = pre_ring.reshape(ring, cols * CAP, pre_width)

    mine = expert_of(ring_at, me_y)
    named_col, taken_col = slot_masks(routes_col, mine)
    gate_tok = jnp.sum(jnp.where(named_col, gates_col[..., None], 0.0), axis=2)
    gate_slot = jnp.sum(jnp.where(taken_col, gate_tok[..., None], 0.0), axis=1)
    gate_slot = gate_slot.transpose(1, 0, 2).reshape(slots, 1)
    same_col = jnp.arange(cols)[:, None] == jnp.arange(cols)[None, :]
    place = taken_col.transpose(2, 0, 3, 1)[:, :, :, None, :] & same_col[None, :, None, :, None]
    place = place.reshape(slots, cols * tok).astype(bf16)
    send_weighted = (dot_rows(place, grad_col, (1, 0)) * gate_slot).astype(bf16)
    send_weighted = send_weighted.reshape(ring, cols * CAP, width)

    weight_rows = lax.all_to_all(send_weighted, RING, 0, 0, tiled=True).reshape(slots, width)
    pre_rows = lax.all_to_all(pre_ring, RING, 0, 0, tiled=True).reshape(slots, pre_width)

    gate_pre = pre_rows[:, :hidden_width].astype(f32)
    up_pre = pre_rows[:, hidden_width:].astype(f32)
    sigmoid_gate = jax.nn.sigmoid(gate_pre)
    activated = gate_pre * sigmoid_gate
    hidden = (activated * up_pre).astype(bf16)
    partial = dot_rows(hidden, weight_rows, (0, 0)).astype(bf16)
    hidden_grad = dot_rows(weight_rows, w_down[0], (1, 1))
    gate_dots = jnp.sum(hidden.astype(f32) * hidden_grad, axis=1, keepdims=True).astype(bf16)
    gate_grad = (hidden_grad * up_pre * sigmoid_gate * (1.0 + gate_pre * (1.0 - sigmoid_gate))).astype(bf16)
    up_grad = (hidden_grad * activated).astype(bf16)
    d_down = lax.psum_scatter(partial, "dp", scatter_dimension=0, tiled=True)
    route_grad = dot_rows(gate_grad, w_gate[0], (1, 1)) + dot_rows(up_grad, w_up[0], (1, 1))
    back = jnp.concatenate([route_grad.astype(bf16), jnp.pad(gate_dots, ((0, 0), (0, 127)))], axis=1)
    back = lax.all_to_all(back.reshape(ring, cols * CAP, width + 128), RING, 0, 0, tiled=True)
    back = back.reshape(slots, width + 128)

    token_part = dot_rows(place, back[:, :width], (0, 0))
    dots = back[:, width].astype(f32).reshape(ring, cols, CAP).transpose(1, 0, 2)
    dots_tok = jnp.sum(jnp.where(taken_col, dots[:, None], 0.0), axis=3)
    dots_route = jnp.sum(jnp.where(named_col, dots_tok[:, :, None], 0.0), axis=3)
    dots_route = jnp.pad(dots_route.reshape(cols * tok, topk), ((0, 0), (0, 128 - topk)))
    home = jnp.concatenate([token_part, dots_route], axis=1).astype(bf16)
    home = lax.all_to_all(home.reshape(cols, tok, width + 128), "y", 0, 0, tiled=True)
    total = jnp.sum(home.astype(f32), axis=0)
    d_tokens = total[:, :width].astype(bf16)
    d_gates = total[:, width : width + topk] / gates
    return (d_tokens, d_gates, d_down[None])


def solution(mesh):
    devices = mesh.devices
    dp, node, local = devices.shape
    split = Mesh(devices.reshape(dp, node, local // 2, 2), ("dp", "node", "y", "zh"))
    owner = ("dp", "node", "y", "zh")
    expert = ("node", "y", "zh")
    in_specs = (
        P(owner, None),
        P(owner, None, None),
        P(owner, None),
        P(owner, None),
        P(expert, None, None),
        P(expert, None, None),
        P(expert, None, None),
    )
    out_specs = (P(owner, None), P(owner, None), P(expert, "dp", None))
    return jax.shard_map(shards, mesh=split, in_specs=in_specs, out_specs=out_specs, check_vma=False)
```

time: 721 us -> 419 us (0.58)
  the two profiles are of different devices: /device:TPU:35 before, /device:TPU:70 now
where the time goes in v1:
time: 419 us; the launch traced here: 418 us
  waiting for transfers between devices  201 us (48%)
  blocking collectives  112 us (27%)
  starting transfers between devices  46 us (11%)
  matrix products  20.8 us (5%)
  between operations  14.4 us (3%)
  other arithmetic  12.4 us (3%)
  local copies, waits for them, and re-layouts  12.1 us (3%)
    all_to_all x1, blocking collectives, shards(): lax.all_to_all(send_weighted, RING, 0, 0, tiled=True).reshape(slots, width)  112 us
    all_to_all x1, waiting for transfers between devices, shards(): lax.all_to_all(back.reshape(ring, cols * CAP, width + 128), RING, 0, 0, t...  106 us
    all_to_all x1, waiting for transfers between devices, shards(): lax.all_to_all(pre_ring, RING, 0, 0, tiled=True).reshape(slots, pre_width)  71.3 us
    all_to_all x1, starting transfers between devices, shards(): lax.all_to_all(pre_ring, RING, 0, 0, tiled=True).reshape(slots, pre_width)  28.2 us
    dot_general x8, matrix products, dot_rows(): lax.dot_general(left, right, ((contract[:1], contract[1:]), ((), ())), pr...  20.8 us
    all_to_all x1, waiting for transfers between devices, shards(): lax.all_to_all(send_pre.reshape(cols, ring * CAP, pre_width), 'y', 0, 0,...  12.2 us
  transfers between devices with their start and end apart: 6, of which 5 were waited for; matrix products, arithmetic and copies ran while one was open for 5% of the time, Pallas kernels for 0%

profile of v1, /device:TPU:70, one launch (start us, length us, event | category | flops | bytes accessed | tf_op | source)
XLA Modules:
  0.0 418.1 jit_solution(13973048165779603094)
XLA Ops:
  7.4 0.9 copy.52
  8.3 2.4 broadcast_compare_fusion
  10.8 0.6 convert_subtract_fusion.1
  11.4 0.8 copy.54
  12.3 0.1 compare_and_fusion
  12.4 1.9 broadcast_and_fusion
  14.3 2.1 and.200
  16.4 2.3 convolution_convert_fusion.1
  18.7 4.5 %all-to-all-start.2 = ((bf16[4,64,1536]{2,1,0:T(8,128)(2,1)}), bf16[4,64,1536]{2,1,0:T(8,128)(2,1)}, u32[]{:S(2)}, u32[]{:S(2)}) async-start(bf16[4,64,1536]{2,1,0:T(8,128)(2,1)} %bitcast.59), calls=%async_computation.2 | async-start | bytes 1572864 | tf_op jit(solution)/shard_map/all_to_all | solution.py:56
  23.3 12.2 %all-to-all-done.2 = bf16[4,64,1536]{2,1,0:T(8,128)(2,1)} async-done(((bf16[4,64,1536]{2,1,0:T(8,128)(2,1)}), bf16[4,64,1536]{2,1,0:T(8,128)(2,1)}, u32[]{:S(2)}, u32[]{:S(2)}) %all-to-all-start.2) | async-done | bytes 786464 | tf_op jit(solution)/shard_map/all_to_all | solution.py:56
  35.6 0.7 broadcast_in_dim.40
  36.3 3.5 all-to-all-start
  39.8 2.5 fusion.13
  42.2 4.2 %all-to-all-done = bf16[4,16,2176]{2,1,0:T(8,128)(2,1)S(1)} async-done(((bf16[4,16,2176]{2,1,0:T(8,128)(2,1)}), bf16[4,16,2176]{2,1,0:T(8,128)(2,1)S(1)}, u32[]{:S(2)}, u32[]{:S(2)}) %all-to-all-start) | async-done | bytes 278560 | tf_op jit(solution)/shard_map/all_to_all | solution.py:45
  46.5 28.2 %all-to-all-start.3 = ((bf16[32,8,1536]{2,1,0:T(8,128)(2,1)}), bf16[32,8,1536]{2,1,0:T(8,128)(2,1)}, u32[]{:S(2)}, u32[]{:S(2)}) async-start(bf16[32,8,1536]{2,1,0:T(8,128)(2,1)} %fusion.13), calls=%async_computation.3 | async-start | bytes 1572864 | tf_op jit(solution)/shard_map/all_to_all | solution.py:76
  74.7 0.5 iota_compare_fusion.5
  75.2 0.7 slice_add_fusion
  75.9 0.2 compare_reduce_fusion
  76.2 1.0 fusion.33
  77.2 0.6 copy-done.7
  77.8 0.7 copy.51
  78.5 1.5 mul.85
  80.1 0.6 bitcast_subtract_fusion
  80.7 0.8 copy.49
  81.6 0.1 copy.48
  81.7 0.1 compare_and_fusion.1
  81.8 0.9 broadcast_and_fusion.1
  82.7 0.8 and.188
  83.5 2.2 fusion.14
  85.7 71.3 %all-to-all-done.3 = bf16[32,8,1536]{2,1,0:T(8,128)(2,1)} async-done(((bf16[32,8,1536]{2,1,0:T(8,128)(2,1)}), bf16[32,8,1536]{2,1,0:T(8,128)(2,1)}, u32[]{:S(2)}, u32[]{:S(2)}) %all-to-all-start.3) | async-done | bytes 786464 | tf_op jit(solution)/shard_map/all_to_all | solution.py:76
  157.0 111.9 %all_to_all.30 = bf16[32,8,2048]{2,1,0:T(8,128)(2,1)S(1)} all-to-all(bf16[32,8,2048]{2,1,0:T(8,128)(2,1)} %fusion.14), channel_id=1, replica_groups=mesh['dp'=8,'node'=16,'y'=4,'zh'=2] {'node','zh'}, dimensions={0} | all-to-all | bytes 2097152 | tf_op jit(solution)/shard_map/all_to_all | solution.py:75
  268.8 3.7 multiply_reduce_fusion
  272.7 2.2 fusion
  274.9 2.3 fusion.10
  277.1 1.1 fusion.17
  278.2 6.4 %all-to-all-start.4 = ((bf16[32,8,2176]{2,1,0:T(8,128)(2,1)}), bf16[32,8,2176]{2,1,0:T(8,128)(2,1)}, u32[]{:S(2)}, u32[]{:S(2)}) async-start(bf16[32,8,2176]{2,1,0:T(8,128)(2,1)} %fusion.17), calls=%async_computation.4 | async-start | bytes 2228224 | tf_op jit(solution)/shard_map/all_to_all | solution.py:91
  284.6 4.3 %convolution_convert_fusion = bf16[768,2048]{1,0:T(8,128)(2,1)} fusion(bf16[32,8,2048]{2,1,0:T(8,128)(2,1)} %copy-done.1, bf16[256,1536]{1,0:T(8,128)(2,1)} %bitcast.13), kind=kOutput, calls=%fused_computation | convolution fusion | flops 808452096 | bytes 4980736 | tf_op jit(solution)/shard_map/dot_general | solution.py:11
  288.9 0.7 copy-done.6
  289.7 105.7 %all-to-all-done.4 = bf16[32,8,2176]{2,1,0:T(8,128)(2,1)} async-done(((bf16[32,8,2176]{2,1,0:T(8,128)(2,1)}), bf16[32,8,2176]{2,1,0:T(8,128)(2,1)}, u32[]{:S(2)}, u32[]{:S(2)}) %all-to-all-start.4) | async-done | bytes 1114144 | tf_op jit(solution)/shard_map/all_to_all | solution.py:91
  395.5 0.9 convert_reduce_fusion.1
  396.4 0.2 reshape.304
  396.7 0.3 fusion.34
  397.0 1.5 convolution_convert_fusion.3
  398.6 0.7 pad_maximum_fusion
  399.3 3.4 all-to-all-start.5
  402.8 7.0 %all-to-all-done.5 = bf16[4,16,2176]{2,1,0:T(8,128)(2,1)S(1)} async-done(((bf16[4,16,2176]{2,1,0:T(8,128)(2,1)}), bf16[4,16,2176]{2,1,0:T(8,128)(2,1)S(1)}, u32[]{:S(2)}, u32[]{:S(2)}) %all-to-all-start.5) | async-done | bytes 278560 | tf_op jit(solution)/shard_map/all_to_all | solution.py:100
  409.9 0.6 slice.94
  410.5 0.7 copy.58
  (61 shorter events, 1.1 us)
Async XLA Ops:
  7.2 265.5 %copy-start = (bf16[1,2048,768]{2,1,0:T(8,128)(2,1)S(1)}, bf16[1,2048,768]{2,1,0:T(8,128)(2,1)}, u32[]{:S(2)}) copy-start(bf16[1,2048,768]{2,1,0:T(8,128)(2,1)} %param.12) | copy-start | bytes 9437188
  11.4 11.9 %copy-start.9 = (bf16[16,2048]{1,0:T(8,128)(2,1)S(1)}, bf16[16,2048]{1,0:T(8,128)(2,1)}, u32[]{:S(2)}) copy-start(bf16[16,2048]{1,0:T(8,128)(2,1)} %param.7) | copy-start | bytes 196612
  12.4 10.8 %copy-start.11 = (f32[16,8]{0,1:T(8,128)S(1)}, f32[16,8]{0,1:T(8,128)}, u32[]{:S(2)}) copy-start(f32[16,8]{0,1:T(8,128)} %param.9) | copy-start | bytes 1540
  12.4 10.8 %copy-start.10 = (s32[16,8]{0,1:T(8,128)S(1)}, s32[16,8]{0,1:T(8,128)}, u32[]{:S(2)}) copy-start(s32[16,8]{0,1:T(8,128)} %param.10) | copy-start | bytes 1540
  18.7 16.9 %all-to-all-start.2 = ((bf16[4,64,1536]{2,1,0:T(8,128)(2,1)}), bf16[4,64,1536]{2,1,0:T(8,128)(2,1)}, u32[]{:S(2)}, u32[]{:S(2)}) async-start(bf16[4,64,1536]{2,1,0:T(8,128)(2,1)} %bitcast.59), calls=%async_computation.2 | async-start | bytes 1572864 | tf_op jit(solution)/shard_map/all_to_all | solution.py:56
  36.3 10.2 %all-to-all-start = ((bf16[4,16,2176]{2,1,0:T(8,128)(2,1)}), bf16[4,16,2176]{2,1,0:T(8,128)(2,1)S(1)}, u32[]{:S(2)}, u32[]{:S(2)}) async-start(bf16[4,16,2176]{2,1,0:T(8,128)(2,1)} %broadcast_in_dim.40), calls=%async_computation | async-start | bytes 557056 | tf_op jit(solution)/shard_map/all_to_all | solution.py:45
  46.5 110.5 %all-to-all-start.3 = ((bf16[32,8,1536]{2,1,0:T(8,128)(2,1)}), bf16[32,8,1536]{2,1,0:T(8,128)(2,1)}, u32[]{:S(2)}, u32[]{:S(2)}) async-start(bf16[32,8,1536]{2,1,0:T(8,128)(2,1)} %fusion.13), calls=%async_computation.3 | async-start | bytes 1572864 | tf_op jit(solution)/shard_map/all_to_all | solution.py:76
  75.2 6.3 %copy-start.13 = (s32[32]{0:T(128)}, s32[32]{0:T(128)S(1)}, u32[]{:S(2)}) copy-start(s32[32]{0:T(128)S(1)} %add_add_fusion.1) | copy-start | bytes 388
  75.9 5.7 %copy-start.2 = (s32[4,16,8]{2,1,0:T(8,128)}, s32[4,16,8]{2,1,0:T(8,128)S(1)}, u32[]{:S(2)}) copy-start(s32[4,16,8]{2,1,0:T(8,128)S(1)} %get-tuple-element.19) | copy-start | bytes 6148
  76.1 5.6 %copy-start.4 = (pred[4,16,32]{2,1,0:T(8,128)(4,1)}, pred[4,16,32]{2,1,0:T(8,128)(4,1)S(1)}, u32[]{:S(2)}) copy-start(pred[4,16,32]{2,1,0:T(8,128)(4,1)S(1)} %compare_reduce_fusion) | copy-start | bytes 6148
  77.2 0.6 copy-start.7
  268.8 3.7 copy-start.1
  272.7 2.2 copy-start.15
  278.2 117.3 %all-to-all-start.4 = ((bf16[32,8,2176]{2,1,0:T(8,128)(2,1)}), bf16[32,8,2176]{2,1,0:T(8,128)(2,1)}, u32[]{:S(2)}, u32[]{:S(2)}) async-start(bf16[32,8,2176]{2,1,0:T(8,128)(2,1)} %fusion.17), calls=%async_computation.4 | async-start | bytes 2228224 | tf_op jit(solution)/shard_map/all_to_all | solution.py:91
  284.6 126.6 %reduce-scatter.2.cloned.1.call-start = ((), (), s32[]{:S(2)}) async-start(), calls=%async_computation.7 | async-start | bytes 3538944 | tf_op jit(solution)/shard_map/reduce_scatter | solution.py:88
  288.9 0.8 copy-start.6
  288.9 107.8 %copy-start.5 = (pred[4,16,32]{2,1,0:T(8,128)(4,1)S(1)}, pred[4,16,32]{2,1,0:T(8,128)(4,1)}, u32[]{:S(2)}) copy-start(pred[4,16,32]{2,1,0:T(8,128)(4,1)} %copy-done.4) | copy-start | bytes 6148
  288.9 107.8 %copy-start.8 = (s32[4,16,32]{2,1,0:T(8,128)S(1)}, s32[4,16,32]{2,1,0:T(8,128)}, u32[]{:S(2)}) copy-start(s32[4,16,32]{2,1,0:T(8,128)} %copy-done.7) | copy-start | bytes 24580
  288.9 107.8 %copy-start.3 = (s32[4,16,8]{2,1,0:T(8,128)S(1)}, s32[4,16,8]{2,1,0:T(8,128)}, u32[]{:S(2)}) copy-start(s32[4,16,8]{2,1,0:T(8,128)} %copy-done.2) | copy-start | bytes 6148
  288.9 107.8 %copy-start.14 = (s32[32]{0:T(128)S(1)}, s32[32]{0:T(128)}, u32[]{:S(2)}) copy-start(s32[32]{0:T(128)} %copy-done.13) | copy-start | bytes 388
  288.9 113.8 %copy-start.12 = (f32[16,8]{0,1:T(8,128)S(1)}, f32[16,8]{0,1:T(8,128)}, u32[]{:S(2)}) copy-start(f32[16,8]{0,1:T(8,128)} %param.9) | copy-start | bytes 1540
  399.3 10.6 %all-to-all-start.5 = ((bf16[4,16,2176]{2,1,0:T(8,128)(2,1)}), bf16[4,16,2176]{2,1,0:T(8,128)(2,1)S(1)}, u32[]{:S(2)}, u32[]{:S(2)}) async-start(bf16[4,16,2176]{2,1,0:T(8,128)(2,1)} %pad_maximum_fusion), calls=%async_computation.5 | async-start | bytes 557056 | tf_op jit(solution)/shard_map/all_to_all | solution.py:100
Sparse Core Ops, SparseCore 0:
  289.4 48.8 reduce-scatter.1

commit v2 on v1

v2 whole, which is shorter than its diff:
```python
import jax
import jax.numpy as jnp
from jax import lax
from jax.sharding import Mesh, PartitionSpec as P

RING = ("node", "zh")
CAP = 2
RING_SIZE = 32
HALF = RING_SIZE // 2
REACH = 5
LEAP = 2 * REACH + 1


def dot_rows(left, right, contract):
    return lax.dot_general(left, right, ((contract[:1], contract[1:]), ((), ())), preferred_element_type=jnp.float32)


def ring_index(place):
    return (place % HALF) * 2 + place // HALF


def expert_of(place, column):
    return (place % HALF) * 8 + column * 2 + place // HALF


def shift(value, hops):
    pairs = [(ring_index(place), ring_index((place + hops) % RING_SIZE)) for place in range(RING_SIZE)]
    return lax.ppermute(value, RING, pairs)


def slot_masks(routes, experts):
    named = routes[..., None] == experts
    hits = jnp.any(named, axis=-2)
    counts = hits.astype(jnp.int32)
    before = jnp.cumsum(counts, axis=-2) - counts
    taken = hits[..., None] & (before[..., None] == jnp.arange(CAP, dtype=jnp.int32))
    return named, taken


def shards(grad_out, saved_pre, gates, routes, w_gate, w_up, w_down):
    tok, topk = routes.shape
    width = grad_out.shape[1]
    pre_width = saved_pre.shape[2]
    hidden_width = pre_width // 2
    ring = RING_SIZE
    cols = lax.axis_size("y")
    me_y = lax.axis_index("y")
    me_z = lax.axis_index("zh") * HALF + lax.axis_index("node")
    f32, bf16 = jnp.float32, jnp.bfloat16
    leaps = jnp.array([0, LEAP, -LEAP], jnp.int32)
    steps = jnp.arange(-REACH, REACH + 1, dtype=jnp.int32)
    hubs = 3
    spread = LEAP
    order = [d for r in range(1, REACH + 1) for d in (r, -r)]

    gate_hi = lax.reduce_precision(gates, 8, 7)
    gate_mid = lax.reduce_precision(gates - gate_hi, 8, 7)
    gate_low = gates - gate_hi - gate_mid
    facts = jnp.concatenate([routes.astype(f32), gate_hi, gate_mid, gate_low], axis=1).astype(bf16)
    facts = jnp.pad(facts, ((0, 0), (0, 128 - 4 * topk)))
    payload = jnp.concatenate([grad_out, facts], axis=1)
    held = jnp.stack([payload, shift(payload, LEAP), shift(payload, -LEAP)])

    ring_at = jnp.arange(ring, dtype=jnp.int32)
    place_of = ring_at % 2 * HALF + ring_at // 2
    all_experts = expert_of(place_of[None, :], jnp.arange(cols, dtype=jnp.int32)[:, None]).reshape(-1)
    named, taken = slot_masks(routes, all_experts)
    pick = named[..., None] & taken[:, None]
    pick = pick.reshape(tok * topk, cols * ring * CAP).astype(bf16)
    send_pre = dot_rows(pick, saved_pre.reshape(tok * topk, pre_width), (0, 0)).astype(bf16)
    pre_col = lax.all_to_all(send_pre.reshape(cols, ring * CAP, pre_width), "y", 0, 0, tiled=True)
    slots = cols * ring * CAP
    at = jnp.arange(slots, dtype=jnp.int32)
    origin = (at // CAP % cols) * (ring * CAP) + (at // (CAP * cols)) * CAP + at % CAP
    swap = (origin[:, None] == at[None, :]).astype(bf16)
    pre_ring = dot_rows(swap, pre_col.reshape(slots, pre_width), (1, 0)).astype(bf16)
    pre_ring = pre_ring.reshape(ring, cols * CAP, pre_width)

    column = jnp.broadcast_to(held.reshape(1, hubs * tok, width + 128), (cols, hubs * tok, width + 128))
    column = lax.all_to_all(column, "y", 0, 0, tiled=True)
    column, pre_ring = lax.optimization_barrier((column, pre_ring))
    pre_rows = lax.all_to_all(pre_ring, RING, 0, 0, tiled=True).reshape(slots, pre_width)

    grad_col = column[:, :, :width].reshape(cols * hubs * tok, width)
    facts = column[:, :, width : width + 4 * topk].astype(f32).reshape(cols, hubs, tok, 4 * topk)
    routes_col = facts[..., :topk].astype(jnp.int32)
    gates_col = facts[..., topk : 2 * topk] + facts[..., 2 * topk : 3 * topk] + facts[..., 3 * topk :]

    mine = expert_of((me_z + steps) % ring, me_y)
    named_col, taken_col = slot_masks(routes_col, mine)
    serves = ~((leaps[:, None] == -LEAP) & (steps[None, :] == -REACH))
    taken_col = taken_col & serves[None, :, None, :, None]
    gate_tok = jnp.sum(jnp.where(named_col, gates_col[..., None], 0.0), axis=3)
    gate_slot = jnp.sum(jnp.where(taken_col, gate_tok[..., None], 0.0), axis=2)
    rows = spread * hubs * cols * CAP
    block = hubs * cols * CAP
    gate_slot = gate_slot.transpose(2, 1, 0, 3).reshape(rows, 1)
    same_col = jnp.arange(cols)[:, None] == jnp.arange(cols)[None, :]
    same_hub = jnp.arange(hubs)[:, None] == jnp.arange(hubs)[None, :]
    same = same_hub[:, None, None, None, :] & same_col[None, :, None, :, None]
    place = taken_col.transpose(3, 1, 0, 4, 2)[:, :, :, :, None, None, :] & same[None, ..., None]
    place = place.reshape(rows, cols * hubs * tok).astype(bf16)
    weighted = (dot_rows(place, grad_col, (1, 0)) * gate_slot).astype(bf16)
    arrived = {0: weighted[REACH * block : (REACH + 1) * block]}
    for d in order:
        arrived[d] = shift(weighted[(d + REACH) * block : (d + REACH + 1) * block], d)
    weight_rows = jnp.concatenate([arrived[d] for d in range(-REACH, REACH + 1)], axis=0)

    from_place = (me_z - steps[:, None] - leaps[None, :]) % ring
    from_row = ring_index(from_place)[:, :, None] * (cols * CAP) + jnp.arange(cols * CAP, dtype=jnp.int32)
    from_row = jnp.where(serves.T[:, :, None], from_row, -1).reshape(rows)
    turn = (from_row[:, None] == at[None, :]).astype(bf16)
    pre = dot_rows(turn, pre_rows, (1, 0))
    gate_pre = pre[:, :hidden_width]
    up_pre = pre[:, hidden_width:]
    sigmoid_gate = jax.nn.sigmoid(gate_pre)
    activated = gate_pre * sigmoid_gate
    hidden = (activated * up_pre).astype(bf16)
    partial = dot_rows(hidden, weight_rows, (0, 0)).astype(bf16)
    hidden_grad = dot_rows(weight_rows, w_down[0], (1, 1))
    gate_dots = jnp.sum(hidden.astype(f32) * hidden_grad, axis=1, keepdims=True).astype(bf16)
    gate_grad = (hidden_grad * up_pre * sigmoid_gate * (1.0 + gate_pre * (1.0 - sigmoid_gate))).astype(bf16)
    up_grad = (hidden_grad * activated).astype(bf16)
    d_down = lax.psum_scatter(partial, "dp", scatter_dimension=0, tiled=True)
    route_grad = dot_rows(gate_grad, w_gate[0], (1, 1)) + dot_rows(up_grad, w_up[0], (1, 1))
    back = jnp.concatenate([route_grad.astype(bf16), jnp.pad(gate_dots, ((0, 0), (0, 127)))], axis=1)
    arrived = {0: back[REACH * block : (REACH + 1) * block]}
    for d in order:
        arrived[d] = shift(back[(d + REACH) * block : (d + REACH + 1) * block], -d)
    back = jnp.concatenate([arrived[d] for d in range(-REACH, REACH + 1)], axis=0)

    token_part = dot_rows(place, back[:, :width], (0, 0))
    dots = back[:, width].astype(f32).reshape(spread, hubs, cols, CAP).transpose(2, 1, 0, 3)
    dots_tok = jnp.sum(jnp.where(taken_col, dots[:, :, None], 0.0), axis=4)
    dots_route = jnp.sum(jnp.where(named_col, dots_tok[:, :, :, None], 0.0), axis=4)
    dots_route = jnp.pad(dots_route.reshape(cols * hubs * tok, topk), ((0, 0), (0, 128 - topk)))
    home = jnp.concatenate([token_part, dots_route], axis=1).astype(bf16)
    home = lax.all_to_all(home.reshape(cols, hubs * tok, width + 128), "y", 0, 0, tiled=True)
    home = jnp.sum(home.astype(f32), axis=0).reshape(hubs, tok, width + 128)
    from_up = shift(home[1].astype(bf16), -LEAP)
    from_down = shift(home[2].astype(bf16), LEAP)
    total = home[0] + from_up.astype(f32) + from_down.astype(f32)
    d_tokens = total[:, :width].astype(bf16)
    d_gates = total[:, width : width + topk] / gates
    return (d_tokens, d_gates, d_down[None])


def solution(mesh):
    devices = mesh.devices
    dp, node, local = devices.shape
    split = Mesh(devices.reshape(dp, node, local // 2, 2), ("dp", "node", "y", "zh"))
    owner = ("dp", "node", "y", "zh")
    expert = ("node", "y", "zh")
    in_specs = (
        P(owner, None),
        P(owner, None, None),
        P(owner, None),
        P(owner, None),
        P(expert, None, None),
        P(expert, None, None),
        P(expert, None, None),
    )
    out_specs = (P(owner, None), P(owner, None), P(expert, "dp", None))
    return jax.shard_map(shards, mesh=split, in_specs=in_specs, out_specs=out_specs, check_vma=False)
```

time: 419 us -> 414 us (0.988)
  the two profiles are of different devices: /device:TPU:70 before, /device:TPU:6 now
where the time goes in v2:
time: 414 us; the launch traced here: 412 us
  starting transfers between devices  198 us (48%)
  waiting for transfers between devices  118 us (29%)
  local copies, waits for them, and re-layouts  35.4 us (9%)
  matrix products  18.5 us (4%)
  between operations  14.7 us (4%)
  other arithmetic  14.4 us (3%)
  blocking collectives  12.3 us (3%)
    ppermute x24, starting transfers between devices, shift(): return lax.ppermute(value, RING, pairs)  159 us
    ppermute x24, waiting for transfers between devices, shift(): return lax.ppermute(value, RING, pairs)  110 us
    all_to_all x1, starting transfers between devices, shards(): lax.all_to_all(pre_ring, RING, 0, 0, tiled=True).reshape(slots, pre_width)  29.6 us
    dot_general x9, matrix products, dot_rows(): lax.dot_general(left, right, ((contract[:1], contract[1:]), ((), ())), pr...  18.5 us
    unnamed x54, local copies, waits for them, and re-layouts  15.8 us
    all_to_all x1, blocking collectives, shards(): lax.all_to_all(home.reshape(cols, hubs * tok, width + 128), 'y', 0, 0, ti...  12.3 us
    all_to_all x1, waiting for transfers between devices, shards(): column = lax.all_to_all(column, 'y', 0, 0, tiled=True)  8.65 us
  transfers between devices with their start and end apart: 28, of which 15 were waited for; matrix products, arithmetic and copies ran while one was open for 11% of the time, Pallas kernels for 0%

profile of v2, /device:TPU:6, one launch (start us, length us, event | category | flops | bytes accessed | tf_op | source)
XLA Modules:
  0.0 411.7 jit_solution(4306132757215152983)
XLA Ops:
  8.3 2.4 broadcast_compare_fusion
  11.1 1.9 broadcast_and_fusion.1
  13.0 2.1 and.343
  15.1 2.3 convolution_convert_fusion.1
  17.4 4.5 %all-to-all-start.1 = ((bf16[4,64,1536]{2,1,0:T(8,128)(2,1)}), bf16[4,64,1536]{2,1,0:T(8,128)(2,1)}, u32[]{:S(2)}, u32[]{:S(2)}) async-start(bf16[4,64,1536]{2,1,0:T(8,128)(2,1)} %bitcast.60), calls=%async_computation.1 | async-start | bytes 1572864 | tf_op jit(solution)/shard_map/all_to_all | solution.py:71
  22.0 19.8 %collective-permute-start = (bf16[16,2176]{1,0:T(8,128)(2,1)S(1)}, bf16[16,2176]{1,0:T(8,128)(2,1)S(1)}, u32[]{:S(2)}, u32[]{:S(2)}) collective-permute-start(bf16[16,2176]{1,0:T(8,128)(2,1)S(1)} %get-tuple-element.55), channel_id=1, source_target_pairs={{0,88},{8,96},{16,104},{24,112},{32,120},{40,1},{48,9},{56,17},{64... | collective-permute-start | bytes 208904 | tf_op jit(solution)/shard_map/ppermute | solution.py:28
  41.8 7.7 %collective-permute-start.1 = (bf16[16,2176]{1,0:T(8,128)(2,1)S(1)}, bf16[16,2176]{1,0:T(8,128)(2,1)S(1)}, u32[]{:S(2)}, u32[]{:S(2)}) collective-permute-start(bf16[16,2176]{1,0:T(8,128)(2,1)S(1)} %get-tuple-element.55), channel_id=1, source_target_pairs={{0,41},{8,49},{16,57},{24,65},{32,73},{40,81},{48,89},{56,97},{64,... | collective-permute-start | bytes 208904 | tf_op jit(solution)/shard_map/ppermute | solution.py:28
  50.5 9.5 %collective-permute-done.1 = bf16[16,2176]{1,0:T(8,128)(2,1)S(1)} collective-permute-done((bf16[16,2176]{1,0:T(8,128)(2,1)S(1)}, bf16[16,2176]{1,0:T(8,128)(2,1)S(1)}, u32[]{:S(2)}, u32[]{:S(2)}) %collective-permute-start.1) | collective-permute-done | bytes 69664 | tf_op jit(solution)/shard_map/ppermute | solution.py:28
  61.1 4.6 %all-to-all-start = ((bf16[4,48,2176]{2,1,0:T(8,128)(2,1)}), bf16[4,48,2176]{2,1,0:T(8,128)(2,1)}, u32[]{:S(2)}, u32[]{:S(2)}) async-start(bf16[4,48,2176]{2,1,0:T(8,128)(2,1)} %broadcast_in_dim.51), calls=%async_computation | async-start | bytes 1671168 | tf_op jit(solution)/shard_map/all_to_all | solution.py:80
  65.7 2.5 fusion.13
  68.2 8.7 %all-to-all-done = bf16[4,48,2176]{2,1,0:T(8,128)(2,1)} async-done(((bf16[4,48,2176]{2,1,0:T(8,128)(2,1)}), bf16[4,48,2176]{2,1,0:T(8,128)(2,1)}, u32[]{:S(2)}, u32[]{:S(2)}) %all-to-all-start) | async-done | bytes 835616 | tf_op jit(solution)/shard_map/all_to_all | solution.py:80
  76.8 29.6 %all-to-all-start.2 = ((bf16[32,8,1536]{2,1,0:T(8,128)(2,1)}), bf16[32,8,1536]{2,1,0:T(8,128)(2,1)}, u32[]{:S(2)}, u32[]{:S(2)}) async-start(bf16[32,8,1536]{2,1,0:T(8,128)(2,1)} %fusion.13), calls=%async_computation.2 | async-start | bytes 1572864 | tf_op jit(solution)/shard_map/all_to_all | solution.py:82
  108.6 2.2 slice.119
  120.2 2.7 and.361
  124.5 9.7 %collective-permute-start.2 = (bf16[24,2048]{1,0:T(8,128)(2,1)S(1)}, bf16[24,2048]{1,0:T(8,128)(2,1)S(1)}, u32[]{:S(2)}, u32[]{:S(2)}) collective-permute-start(bf16[24,2048]{1,0:T(8,128)(2,1)S(1)} %get-tuple-element.51), channel_id=1, source_target_pairs={{0,89},{8,97},{16,105},{24,113},{32,121},{40,0},{48,8},{56,16},{64... | collective-permute-start | bytes 294920 | tf_op jit(solution)/shard_map/ppermute | solution.py:28
  134.3 7.2 %collective-permute-start.3 = (bf16[24,2048]{1,0:T(8,128)(2,1)S(1)}, bf16[24,2048]{1,0:T(8,128)(2,1)S(1)}, u32[]{:S(2)}, u32[]{:S(2)}) collective-permute-start(bf16[24,2048]{1,0:T(8,128)(2,1)S(1)} %get-tuple-element.50), channel_id=1, source_target_pairs={{0,97},{8,105},{16,113},{24,121},{32,0},{40,8},{48,16},{56,24},{64... | collective-permute-start | bytes 294920 | tf_op jit(solution)/shard_map/ppermute | solution.py:28
  141.6 5.2 %collective-permute-start.4 = (bf16[24,2048]{1,0:T(8,128)(2,1)S(1)}, bf16[24,2048]{1,0:T(8,128)(2,1)S(1)}, u32[]{:S(2)}, u32[]{:S(2)}) collective-permute-start(bf16[24,2048]{1,0:T(8,128)(2,1)S(1)} %get-tuple-element.49), channel_id=1, source_target_pairs={{0,105},{8,113},{16,121},{24,0},{32,8},{40,16},{48,24},{56,32},{64... | collective-permute-start | bytes 294920 | tf_op jit(solution)/shard_map/ppermute | solution.py:28
  146.8 5.5 %collective-permute-start.5 = (bf16[24,2048]{1,0:T(8,128)(2,1)S(1)}, bf16[24,2048]{1,0:T(8,128)(2,1)S(1)}, u32[]{:S(2)}, u32[]{:S(2)}) collective-permute-start(bf16[24,2048]{1,0:T(8,128)(2,1)S(1)} %get-tuple-element.48), channel_id=1, source_target_pairs={{0,113},{8,121},{16,0},{24,8},{32,16},{40,24},{48,32},{56,40},{64,... | collective-permute-start | bytes 294920 | tf_op jit(solution)/shard_map/ppermute | solution.py:28
  152.2 3.4 collective-permute-start.6
  155.6 39.2 %collective-permute-done.2 = bf16[24,2048]{1,0:T(8,128)(2,1)S(1)} collective-permute-done((bf16[24,2048]{1,0:T(8,128)(2,1)S(1)}, bf16[24,2048]{1,0:T(8,128)(2,1)S(1)}, u32[]{:S(2)}, u32[]{:S(2)}) %collective-permute-start.2) | collective-permute-done | bytes 98336 | tf_op jit(solution)/shard_map/ppermute | solution.py:28
  196.6 7.2 %collective-permute-done.4 = bf16[24,2048]{1,0:T(8,128)(2,1)S(1)} collective-permute-done((bf16[24,2048]{1,0:T(8,128)(2,1)S(1)}, bf16[24,2048]{1,0:T(8,128)(2,1)S(1)}, u32[]{:S(2)}, u32[]{:S(2)}) %collective-permute-start.4) | collective-permute-done | bytes 98336 | tf_op jit(solution)/shard_map/ppermute | solution.py:28
  203.8 2.0 collective-permute-done.5
  207.8 3.4 collective-permute-start.7
  211.4 5.4 %collective-permute-start.8 = (bf16[24,2048]{1,0:T(8,128)(2,1)}, bf16[24,2048]{1,0:T(8,128)(2,1)S(1)}, u32[]{:S(2)}, u32[]{:S(2)}) collective-permute-start(bf16[24,2048]{1,0:T(8,128)(2,1)} %get-tuple-element.44), channel_id=1, source_target_pairs={{0,16},{8,24},{16,32},{24,40},{32,48},{40,56},{48,64},{56,72},{64,... | collective-permute-start | bytes 294920 | tf_op jit(solution)/shard_map/ppermute | solution.py:28
  216.8 5.9 %collective-permute-start.9 = (bf16[24,2048]{1,0:T(8,128)(2,1)}, bf16[24,2048]{1,0:T(8,128)(2,1)S(1)}, u32[]{:S(2)}, u32[]{:S(2)}) collective-permute-start(bf16[24,2048]{1,0:T(8,128)(2,1)} %get-tuple-element.43), channel_id=1, source_target_pairs={{0,24},{8,32},{16,40},{24,48},{32,56},{40,64},{48,72},{56,80},{64,... | collective-permute-start | bytes 294920 | tf_op jit(solution)/shard_map/ppermute | solution.py:28
  222.7 7.3 %collective-permute-start.10 = (bf16[24,2048]{1,0:T(8,128)(2,1)}, bf16[24,2048]{1,0:T(8,128)(2,1)S(1)}, u32[]{:S(2)}, u32[]{:S(2)}) collective-permute-start(bf16[24,2048]{1,0:T(8,128)(2,1)} %get-tuple-element.42), channel_id=1, source_target_pairs={{0,32},{8,40},{16,48},{24,56},{32,64},{40,72},{48,80},{56,88},{64,... | collective-permute-start | bytes 294920 | tf_op jit(solution)/shard_map/ppermute | solution.py:28
  230.1 8.8 %collective-permute-start.11 = (bf16[24,2048]{1,0:T(8,128)(2,1)S(1)}, bf16[24,2048]{1,0:T(8,128)(2,1)S(1)}, u32[]{:S(2)}, u32[]{:S(2)}) collective-permute-start(bf16[24,2048]{1,0:T(8,128)(2,1)S(1)} %get-tuple-element.41), channel_id=1, source_target_pairs={{0,40},{8,48},{16,56},{24,64},{32,72},{40,80},{48,88},{56,96},{64,... | collective-permute-start | bytes 294920 | tf_op jit(solution)/shard_map/ppermute | solution.py:28
  242.3 6.1 %collective-permute-done.11 = bf16[24,2048]{1,0:T(8,128)(2,1)S(1)} collective-permute-done((bf16[24,2048]{1,0:T(8,128)(2,1)S(1)}, bf16[24,2048]{1,0:T(8,128)(2,1)S(1)}, u32[]{:S(2)}, u32[]{:S(2)}) %collective-permute-start.11) | collective-permute-done | bytes 98336 | tf_op jit(solution)/shard_map/ppermute | solution.py:28
  250.8 3.1 multiply_reduce_fusion
  258.9 8.0 %collective-permute-start.12 = (bf16[24,2176]{1,0:T(8,128)(2,1)}, bf16[24,2176]{1,0:T(8,128)(2,1)S(1)}, u32[]{:S(2)}, u32[]{:S(2)}) collective-permute-start(bf16[24,2176]{1,0:T(8,128)(2,1)} %get-tuple-element.40), channel_id=1, source_target_pairs={{0,40},{8,48},{16,56},{24,64},{32,72},{40,80},{48,88},{56,96},{64,... | collective-permute-start | bytes 313352 | tf_op jit(solution)/shard_map/ppermute | solution.py:28
  266.9 3.5 convolution_convert_fusion
  270.4 7.6 %collective-permute-start.13 = (bf16[24,2176]{1,0:T(8,128)(2,1)}, bf16[24,2176]{1,0:T(8,128)(2,1)S(1)}, u32[]{:S(2)}, u32[]{:S(2)}) collective-permute-start(bf16[24,2176]{1,0:T(8,128)(2,1)} %get-tuple-element.39), channel_id=1, source_target_pairs={{0,32},{8,40},{16,48},{24,56},{32,64},{40,72},{48,80},{56,88},{64,... | collective-permute-start | bytes 313352 | tf_op jit(solution)/shard_map/ppermute | solution.py:28
  278.0 1.9 collective-permute-start.14
  280.0 7.5 %collective-permute-start.15 = (bf16[24,2176]{1,0:T(8,128)(2,1)}, bf16[24,2176]{1,0:T(8,128)(2,1)S(1)}, u32[]{:S(2)}, u32[]{:S(2)}) collective-permute-start(bf16[24,2176]{1,0:T(8,128)(2,1)} %get-tuple-element.37), channel_id=1, source_target_pairs={{0,16},{8,24},{16,32},{24,40},{32,48},{40,56},{48,64},{56,72},{64,... | collective-permute-start | bytes 313352 | tf_op jit(solution)/shard_map/ppermute | solution.py:28
  287.5 3.7 collective-permute-start.16
  294.4 4.3 %collective-permute-done.15 = bf16[24,2176]{1,0:T(8,128)(2,1)S(1)} collective-permute-done((bf16[24,2176]{1,0:T(8,128)(2,1)}, bf16[24,2176]{1,0:T(8,128)(2,1)S(1)}, u32[]{:S(2)}, u32[]{:S(2)}) %collective-permute-start.15) | collective-permute-done | bytes 104480 | tf_op jit(solution)/shard_map/ppermute | solution.py:28
  300.0 2.0 fusion.61
  301.9 3.5 collective-permute-start.17
  308.2 3.2 collective-permute-start.19
  311.5 8.3 %collective-permute-start.20 = (bf16[24,2176]{1,0:T(8,128)(2,1)}, bf16[24,2176]{1,0:T(8,128)(2,1)S(1)}, u32[]{:S(2)}, u32[]{:S(2)}) collective-permute-start(bf16[24,2176]{1,0:T(8,128)(2,1)} %get-tuple-element.31), channel_id=1, source_target_pairs={{0,97},{8,105},{16,113},{24,121},{32,0},{40,8},{48,16},{56,24},{64... | collective-permute-start | bytes 313352 | tf_op jit(solution)/shard_map/ppermute | solution.py:28
  319.8 7.1 %collective-permute-start.21 = (bf16[24,2176]{1,0:T(8,128)(2,1)S(1)}, bf16[24,2176]{1,0:T(8,128)(2,1)S(1)}, u32[]{:S(2)}, u32[]{:S(2)}) collective-permute-start(bf16[24,2176]{1,0:T(8,128)(2,1)S(1)} %get-tuple-element.30), channel_id=1, source_target_pairs={{0,89},{8,97},{16,105},{24,113},{32,121},{40,0},{48,8},{56,16},{64... | collective-permute-start | bytes 313352 | tf_op jit(solution)/shard_map/ppermute | solution.py:28
  329.8 2.3 collective-permute-done.20
  332.7 11.2 %collective-permute-done.21 = bf16[24,2176]{1,0:T(8,128)(2,1)S(1)} collective-permute-done((bf16[24,2176]{1,0:T(8,128)(2,1)S(1)}, bf16[24,2176]{1,0:T(8,128)(2,1)S(1)}, u32[]{:S(2)}, u32[]{:S(2)}) %collective-permute-start.21) | collective-permute-done | bytes 104480 | tf_op jit(solution)/shard_map/ppermute | solution.py:28
  348.5 12.3 %all_to_all.20 = bf16[4,48,2176]{2,1,0:T(8,128)(2,1)S(1)} all-to-all(bf16[4,48,2176]{2,1,0:T(8,128)(2,1)S(1)} %pad_maximum_fusion), channel_id=1, replica_groups=mesh['dp'=8,'node'=16,'y'=4,'zh'=2] {'y'}, dimensions={0} | all-to-all | bytes 1671168 | tf_op jit(solution)/shard_map/all_to_all | solution.py:138
  361.7 13.7 %collective-permute-start.22 = (bf16[16,2176]{1,0:T(8,128)(2,1)S(1)}, bf16[16,2176]{1,0:T(8,128)(2,1)S(1)}, u32[]{:S(2)}, u32[]{:S(2)}) collective-permute-start(bf16[16,2176]{1,0:T(8,128)(2,1)S(1)} %get-tuple-element.52), channel_id=1, source_target_pairs={{0,41},{8,49},{16,57},{24,65},{32,73},{40,81},{48,89},{56,97},{64,... | collective-permute-start | bytes 208904 | tf_op jit(solution)/shard_map/ppermute | solution.py:28
  375.4 3.5 collective-permute-start.23
  379.0 2.4 collective-permute-done.22
  381.5 21.2 %collective-permute-done.23 = bf16[16,2176]{1,0:T(8,128)(2,1)S(1)} collective-permute-done((bf16[16,2176]{1,0:T(8,128)(2,1)S(1)}, bf16[16,2176]{1,0:T(8,128)(2,1)S(1)}, u32[]{:S(2)}, u32[]{:S(2)}) %collective-permute-start.23) | collective-permute-done | bytes 69664 | tf_op jit(solution)/shard_map/ppermute | solution.py:28
  (151 shorter events, 50.0 us)
Async XLA Ops:
  7.2 246.8 %copy-start = (bf16[1,2048,768]{2,1,0:T(8,128)(2,1)S(1)}, bf16[1,2048,768]{2,1,0:T(8,128)(2,1)}, u32[]{:S(2)}) copy-start(bf16[1,2048,768]{2,1,0:T(8,128)(2,1)} %param.13) | copy-start | bytes 9437188
  15.1 6.8 %copy-start.5 = (s32[16,8]{0,1:T(8,128)S(1)}, s32[16,8]{0,1:T(8,128)}, u32[]{:S(2)}) copy-start(s32[16,8]{0,1:T(8,128)} %param.11) | copy-start | bytes 1540
  15.1 6.8 %copy-start.6 = (f32[16,8]{0,1:T(8,128)S(1)}, f32[16,8]{0,1:T(8,128)}, u32[]{:S(2)}) copy-start(f32[16,8]{0,1:T(8,128)} %param.10) | copy-start | bytes 1540
  15.1 6.9 %copy-start.4 = (bf16[16,2048]{1,0:T(8,128)(2,1)S(1)}, bf16[16,2048]{1,0:T(8,128)(2,1)}, u32[]{:S(2)}) copy-start(bf16[16,2048]{1,0:T(8,128)(2,1)} %param.8) | copy-start | bytes 196612
  17.4 42.6 %all-to-all-start.1 = ((bf16[4,64,1536]{2,1,0:T(8,128)(2,1)}), bf16[4,64,1536]{2,1,0:T(8,128)(2,1)}, u32[]{:S(2)}, u32[]{:S(2)}) async-start(bf16[4,64,1536]{2,1,0:T(8,128)(2,1)} %bitcast.60), calls=%async_computation.1 | async-start | bytes 1572864 | tf_op jit(solution)/shard_map/all_to_all | solution.py:71
  22.0 28.5 %collective-permute-start = (bf16[16,2176]{1,0:T(8,128)(2,1)S(1)}, bf16[16,2176]{1,0:T(8,128)(2,1)S(1)}, u32[]{:S(2)}, u32[]{:S(2)}) collective-permute-start(bf16[16,2176]{1,0:T(8,128)(2,1)S(1)} %get-tuple-element.55), channel_id=1, source_target_pairs={{0,88},{8,96},{16,104},{24,112},{32,120},{40,1},{48,9},{56,17},{64... | collective-permute-start | bytes 208904 | tf_op jit(solution)/shard_map/ppermute | solution.py:28
  41.8 18.2 %collective-permute-start.1 = (bf16[16,2176]{1,0:T(8,128)(2,1)S(1)}, bf16[16,2176]{1,0:T(8,128)(2,1)S(1)}, u32[]{:S(2)}, u32[]{:S(2)}) collective-permute-start(bf16[16,2176]{1,0:T(8,128)(2,1)S(1)} %get-tuple-element.55), channel_id=1, source_target_pairs={{0,41},{8,49},{16,57},{24,65},{32,73},{40,81},{48,89},{56,97},{64,... | collective-permute-start | bytes 208904 | tf_op jit(solution)/shard_map/ppermute | solution.py:28
  60.0 5.6 %copy-start.13 = (pred[3]{0:T(512)(128)(4,1)S(1)}, pred[3]{0:T(512)(128)(4,1)}, u32[]{:S(2)}) copy-start(pred[3]{0:T(512)(128)(4,1)} %constant.210) | copy-start | bytes 13
  61.1 15.8 %all-to-all-start = ((bf16[4,48,2176]{2,1,0:T(8,128)(2,1)}), bf16[4,48,2176]{2,1,0:T(8,128)(2,1)}, u32[]{:S(2)}, u32[]{:S(2)}) async-start(bf16[4,48,2176]{2,1,0:T(8,128)(2,1)} %broadcast_in_dim.51), calls=%async_computation | async-start | bytes 1671168 | tf_op jit(solution)/shard_map/all_to_all | solution.py:80
  65.7 50.4 %copy-start.9 = (pred[3,11]{1,0:T(4,128)(4,1)}, pred[3,11]{1,0:T(4,128)(4,1)S(1)}, u32[]{:S(2)}) copy-start(pred[3,11]{1,0:T(4,128)(4,1)S(1)} %and_not_fusion.1) | copy-start | bytes 103
  76.8 172.2 %all-to-all-start.2 = ((bf16[32,8,1536]{2,1,0:T(8,128)(2,1)}), bf16[32,8,1536]{2,1,0:T(8,128)(2,1)}, u32[]{:S(2)}, u32[]{:S(2)}) async-start(bf16[32,8,1536]{2,1,0:T(8,128)(2,1)} %fusion.13), calls=%async_computation.2 | async-start | bytes 1572864 | tf_op jit(solution)/shard_map/all_to_all | solution.py:82
  106.5 298.4 %reduce-scatter.2.cloned.1.call-start = ((), (), s32[]{:S(2)}) async-start(), calls=%async_computation.5 | async-start | bytes 3538944 | tf_op jit(solution)/shard_map/reduce_scatter | solution.py:124
  122.9 11.4 %copy-start.11 = (s32[11]{0:T(128)S(1)}, s32[11]{0:T(128)}, u32[]{:S(2)}) copy-start(s32[11]{0:T(128)} %get-tuple-element.65) | copy-start | bytes 136
  122.9 11.4 %copy-start.12 = (s32[3]{0:T(128)S(1)}, s32[3]{0:T(128)}, u32[]{:S(2)}) copy-start(s32[3]{0:T(128)} %constant.211) | copy-start | bytes 40
  124.5 70.3 %collective-permute-start.2 = (bf16[24,2048]{1,0:T(8,128)(2,1)S(1)}, bf16[24,2048]{1,0:T(8,128)(2,1)S(1)}, u32[]{:S(2)}, u32[]{:S(2)}) collective-permute-start(bf16[24,2048]{1,0:T(8,128)(2,1)S(1)} %get-tuple-element.51), channel_id=1, source_target_pairs={{0,89},{8,97},{16,105},{24,113},{32,121},{40,0},{48,8},{56,16},{64... | collective-permute-start | bytes 294920 | tf_op jit(solution)/shard_map/ppermute | solution.py:28
  134.3 62.3 %collective-permute-start.3 = (bf16[24,2048]{1,0:T(8,128)(2,1)S(1)}, bf16[24,2048]{1,0:T(8,128)(2,1)S(1)}, u32[]{:S(2)}, u32[]{:S(2)}) collective-permute-start(bf16[24,2048]{1,0:T(8,128)(2,1)S(1)} %get-tuple-element.50), channel_id=1, source_target_pairs={{0,97},{8,105},{16,113},{24,121},{32,0},{40,8},{48,16},{56,24},{64... | collective-permute-start | bytes 294920 | tf_op jit(solution)/shard_map/ppermute | solution.py:28
  141.6 62.2 %collective-permute-start.4 = (bf16[24,2048]{1,0:T(8,128)(2,1)S(1)}, bf16[24,2048]{1,0:T(8,128)(2,1)S(1)}, u32[]{:S(2)}, u32[]{:S(2)}) collective-permute-start(bf16[24,2048]{1,0:T(8,128)(2,1)S(1)} %get-tuple-element.49), channel_id=1, source_target_pairs={{0,105},{8,113},{16,121},{24,0},{32,8},{40,16},{48,24},{56,32},{64... | collective-permute-start | bytes 294920 | tf_op jit(solution)/shard_map/ppermute | solution.py:28
  146.8 59.0 %collective-permute-start.5 = (bf16[24,2048]{1,0:T(8,128)(2,1)S(1)}, bf16[24,2048]{1,0:T(8,128)(2,1)S(1)}, u32[]{:S(2)}, u32[]{:S(2)}) collective-permute-start(bf16[24,2048]{1,0:T(8,128)(2,1)S(1)} %get-tuple-element.48), channel_id=1, source_target_pairs={{0,113},{8,121},{16,0},{24,8},{32,16},{40,24},{48,32},{56,40},{64,... | collective-permute-start | bytes 294920 | tf_op jit(solution)/shard_map/ppermute | solution.py:28
  152.2 53.8 %collective-permute-start.6 = (bf16[24,2048]{1,0:T(8,128)(2,1)S(1)}, bf16[24,2048]{1,0:T(8,128)(2,1)S(1)}, u32[]{:S(2)}, u32[]{:S(2)}) collective-permute-start(bf16[24,2048]{1,0:T(8,128)(2,1)S(1)} %get-tuple-element.47), channel_id=1, source_target_pairs={{0,121},{8,0},{16,8},{24,16},{32,24},{40,32},{48,40},{56,48},{64,5... | collective-permute-start | bytes 294920 | tf_op jit(solution)/shard_map/ppermute | solution.py:28
  206.8 1.0 copy-start.7
  207.8 31.0 %collective-permute-start.7 = (bf16[24,2048]{1,0:T(8,128)(2,1)}, bf16[24,2048]{1,0:T(8,128)(2,1)}, u32[]{:S(2)}, u32[]{:S(2)}) collective-permute-start(bf16[24,2048]{1,0:T(8,128)(2,1)} %get-tuple-element.45), channel_id=1, source_target_pairs={{0,8},{8,16},{16,24},{24,32},{32,40},{40,48},{48,56},{56,64},{64,7... | collective-permute-start | bytes 294920 | tf_op jit(solution)/shard_map/ppermute | solution.py:28
  211.4 29.0 %collective-permute-start.8 = (bf16[24,2048]{1,0:T(8,128)(2,1)}, bf16[24,2048]{1,0:T(8,128)(2,1)S(1)}, u32[]{:S(2)}, u32[]{:S(2)}) collective-permute-start(bf16[24,2048]{1,0:T(8,128)(2,1)} %get-tuple-element.44), channel_id=1, source_target_pairs={{0,16},{8,24},{16,32},{24,40},{32,48},{40,56},{48,64},{56,72},{64,... | collective-permute-start | bytes 294920 | tf_op jit(solution)/shard_map/ppermute | solution.py:28
  216.8 24.2 %collective-permute-start.9 = (bf16[24,2048]{1,0:T(8,128)(2,1)}, bf16[24,2048]{1,0:T(8,128)(2,1)S(1)}, u32[]{:S(2)}, u32[]{:S(2)}) collective-permute-start(bf16[24,2048]{1,0:T(8,128)(2,1)} %get-tuple-element.43), channel_id=1, source_target_pairs={{0,24},{8,32},{16,40},{24,48},{32,56},{40,64},{48,72},{56,80},{64,... | collective-permute-start | bytes 294920 | tf_op jit(solution)/shard_map/ppermute | solution.py:28
  222.7 18.9 %collective-permute-start.10 = (bf16[24,2048]{1,0:T(8,128)(2,1)}, bf16[24,2048]{1,0:T(8,128)(2,1)S(1)}, u32[]{:S(2)}, u32[]{:S(2)}) collective-permute-start(bf16[24,2048]{1,0:T(8,128)(2,1)} %get-tuple-element.42), channel_id=1, source_target_pairs={{0,32},{8,40},{16,48},{24,56},{32,64},{40,72},{48,80},{56,88},{64,... | collective-permute-start | bytes 294920 | tf_op jit(solution)/shard_map/ppermute | solution.py:28
  230.1 18.4 %collective-permute-start.11 = (bf16[24,2048]{1,0:T(8,128)(2,1)S(1)}, bf16[24,2048]{1,0:T(8,128)(2,1)S(1)}, u32[]{:S(2)}, u32[]{:S(2)}) collective-permute-start(bf16[24,2048]{1,0:T(8,128)(2,1)S(1)} %get-tuple-element.41), channel_id=1, source_target_pairs={{0,40},{8,48},{16,56},{24,64},{32,72},{40,80},{48,88},{56,96},{64,... | collective-permute-start | bytes 294920 | tf_op jit(solution)/shard_map/ppermute | solution.py:28
  249.1 1.6 copy-start.8
  254.0 1.9 copy-start.14
  257.1 1.0 copy-start.1
  258.9 32.3 %collective-permute-start.12 = (bf16[24,2176]{1,0:T(8,128)(2,1)}, bf16[24,2176]{1,0:T(8,128)(2,1)S(1)}, u32[]{:S(2)}, u32[]{:S(2)}) collective-permute-start(bf16[24,2176]{1,0:T(8,128)(2,1)} %get-tuple-element.40), channel_id=1, source_target_pairs={{0,40},{8,48},{16,56},{24,64},{32,72},{40,80},{48,88},{56,96},{64,... | collective-permute-start | bytes 313352 | tf_op jit(solution)/shard_map/ppermute | solution.py:28
  270.4 21.5 %collective-permute-start.13 = (bf16[24,2176]{1,0:T(8,128)(2,1)}, bf16[24,2176]{1,0:T(8,128)(2,1)S(1)}, u32[]{:S(2)}, u32[]{:S(2)}) collective-permute-start(bf16[24,2176]{1,0:T(8,128)(2,1)} %get-tuple-element.39), channel_id=1, source_target_pairs={{0,32},{8,40},{16,48},{24,56},{32,64},{40,72},{48,80},{56,88},{64,... | collective-permute-start | bytes 313352 | tf_op jit(solution)/shard_map/ppermute | solution.py:28
  278.0 15.7 %collective-permute-start.14 = (bf16[24,2176]{1,0:T(8,128)(2,1)}, bf16[24,2176]{1,0:T(8,128)(2,1)S(1)}, u32[]{:S(2)}, u32[]{:S(2)}) collective-permute-start(bf16[24,2176]{1,0:T(8,128)(2,1)} %get-tuple-element.38), channel_id=1, source_target_pairs={{0,24},{8,32},{16,40},{24,48},{32,56},{40,64},{48,72},{56,80},{64,... | collective-permute-start | bytes 313352 | tf_op jit(solution)/shard_map/ppermute | solution.py:28
  280.0 18.7 %collective-permute-start.15 = (bf16[24,2176]{1,0:T(8,128)(2,1)}, bf16[24,2176]{1,0:T(8,128)(2,1)S(1)}, u32[]{:S(2)}, u32[]{:S(2)}) collective-permute-start(bf16[24,2176]{1,0:T(8,128)(2,1)} %get-tuple-element.37), channel_id=1, source_target_pairs={{0,16},{8,24},{16,32},{24,40},{32,48},{40,56},{48,64},{56,72},{64,... | collective-permute-start | bytes 313352 | tf_op jit(solution)/shard_map/ppermute | solution.py:28
  287.5 11.8 %collective-permute-start.16 = (bf16[24,2176]{1,0:T(8,128)(2,1)}, bf16[24,2176]{1,0:T(8,128)(2,1)S(1)}, u32[]{:S(2)}, u32[]{:S(2)}) collective-permute-start(bf16[24,2176]{1,0:T(8,128)(2,1)} %get-tuple-element.36), channel_id=1, source_target_pairs={{0,8},{8,16},{16,24},{24,32},{32,40},{40,48},{48,56},{56,64},{64,7... | collective-permute-start | bytes 313352 | tf_op jit(solution)/shard_map/ppermute | solution.py:28
  300.0 46.1 %copy-start.10 = (pred[3,11]{1,0:T(4,128)(4,1)S(1)}, pred[3,11]{1,0:T(4,128)(4,1)}, u32[]{:S(2)}) copy-start(pred[3,11]{1,0:T(4,128)(4,1)} %copy-done.9) | copy-start | bytes 103
  301.9 25.0 %collective-permute-start.17 = (bf16[24,2176]{1,0:T(8,128)(2,1)}, bf16[24,2176]{1,0:T(8,128)(2,1)}, u32[]{:S(2)}, u32[]{:S(2)}) collective-permute-start(bf16[24,2176]{1,0:T(8,128)(2,1)} %get-tuple-element.34), channel_id=1, source_target_pairs={{0,121},{8,0},{16,8},{24,16},{32,24},{40,32},{48,40},{56,48},{64,5... | collective-permute-start | bytes 313352 | tf_op jit(solution)/shard_map/ppermute | solution.py:28
  306.3 22.2 %collective-permute-start.18 = (bf16[24,2176]{1,0:T(8,128)(2,1)}, bf16[24,2176]{1,0:T(8,128)(2,1)S(1)}, u32[]{:S(2)}, u32[]{:S(2)}) collective-permute-start(bf16[24,2176]{1,0:T(8,128)(2,1)} %get-tuple-element.33), channel_id=1, source_target_pairs={{0,113},{8,121},{16,0},{24,8},{32,16},{40,24},{48,32},{56,40},{64,... | collective-permute-start | bytes 313352 | tf_op jit(solution)/shard_map/ppermute | solution.py:28
  308.2 20.9 %collective-permute-start.19 = (bf16[24,2176]{1,0:T(8,128)(2,1)}, bf16[24,2176]{1,0:T(8,128)(2,1)S(1)}, u32[]{:S(2)}, u32[]{:S(2)}) collective-permute-start(bf16[24,2176]{1,0:T(8,128)(2,1)} %get-tuple-element.32), channel_id=1, source_target_pairs={{0,105},{8,113},{16,121},{24,0},{32,8},{40,16},{48,24},{56,32},{64... | collective-permute-start | bytes 313352 | tf_op jit(solution)/shard_map/ppermute | solution.py:28
  311.5 20.6 %collective-permute-start.20 = (bf16[24,2176]{1,0:T(8,128)(2,1)}, bf16[24,2176]{1,0:T(8,128)(2,1)S(1)}, u32[]{:S(2)}, u32[]{:S(2)}) collective-permute-start(bf16[24,2176]{1,0:T(8,128)(2,1)} %get-tuple-element.31), channel_id=1, source_target_pairs={{0,97},{8,105},{16,113},{24,121},{32,0},{40,8},{48,16},{56,24},{64... | collective-permute-start | bytes 313352 | tf_op jit(solution)/shard_map/ppermute | solution.py:28
  319.8 24.1 %collective-permute-start.21 = (bf16[24,2176]{1,0:T(8,128)(2,1)S(1)}, bf16[24,2176]{1,0:T(8,128)(2,1)S(1)}, u32[]{:S(2)}, u32[]{:S(2)}) collective-permute-start(bf16[24,2176]{1,0:T(8,128)(2,1)S(1)} %get-tuple-element.30), channel_id=1, source_target_pairs={{0,89},{8,97},{16,105},{24,113},{32,121},{40,0},{48,8},{56,16},{64... | collective-permute-start | bytes 313352 | tf_op jit(solution)/shard_map/ppermute | solution.py:28
  343.9 2.7 copy-start.3
  360.9 0.7 copy-start.2
  361.7 19.8 %collective-permute-start.22 = (bf16[16,2176]{1,0:T(8,128)(2,1)S(1)}, bf16[16,2176]{1,0:T(8,128)(2,1)S(1)}, u32[]{:S(2)}, u32[]{:S(2)}) collective-permute-start(bf16[16,2176]{1,0:T(8,128)(2,1)S(1)} %get-tuple-element.52), channel_id=1, source_target_pairs={{0,41},{8,49},{16,57},{24,65},{32,73},{40,81},{48,89},{56,97},{64,... | collective-permute-start | bytes 208904 | tf_op jit(solution)/shard_map/ppermute | solution.py:28
  375.4 27.2 %collective-permute-start.23 = (bf16[16,2176]{1,0:T(8,128)(2,1)S(1)}, bf16[16,2176]{1,0:T(8,128)(2,1)S(1)}, u32[]{:S(2)}, u32[]{:S(2)}) collective-permute-start(bf16[16,2176]{1,0:T(8,128)(2,1)S(1)} %get-tuple-element.53), channel_id=1, source_target_pairs={{0,88},{8,96},{16,104},{24,112},{32,120},{40,1},{48,9},{56,17},{64... | collective-permute-start | bytes 208904 | tf_op jit(solution)/shard_map/ppermute | solution.py:28
Sparse Core Ops, SparseCore 0:
  270.5 43.0 reduce-scatter.1

commit v3 on v1

v3 whole, which is shorter than its diff:
```python
import functools

import jax
import jax.numpy as jnp
from jax import lax
from jax.experimental import pallas as pl
from jax.experimental.pallas import tpu as pltpu
from jax.sharding import Mesh, PartitionSpec as P

RING = ("node", "zh")
CAP = 2
COLS = 4
RING_SIZE = 32
SLOTS = COLS * RING_SIZE * CAP
FACTS = 128
VMEM_BYTES = 24 * 1024 * 1024
f32, bf16, i32 = jnp.float32, jnp.bfloat16, jnp.int32


def dot(left, right, contract=(1, 0)):
    dims = ((contract[:1], contract[1:]), ((), ()))
    return lax.dot_general(left, right, dims, preferred_element_type=f32)


def iota(shape, axis):
    return lax.broadcasted_iota(i32, shape, axis)


def expert_of(ring_index, column):
    return (ring_index // 2) * 8 + column * 2 + ring_index % 2


def one_hot(mask):
    return jnp.where(mask, 1.0, 0.0).astype(bf16)


def pack_kernel(routes_ref, gates_ref, grad_ref, pre_ref, out_ref):
    tok, topk = routes_ref.shape
    routes_of, width = tok * topk, pre_ref.shape[1]
    per_col = RING_SIZE * CAP
    routes = routes_ref[...].astype(f32).astype(bf16)
    row_tok, row_k = iota((routes_of, tok), 0) // topk, iota((routes_of, topk), 0) % topk
    spread = dot(one_hot(row_tok == iota((routes_of, tok), 1)), routes)
    named = jnp.sum(jnp.where(row_k == iota((routes_of, topk), 1), spread, 0.0), axis=1, keepdims=True)
    slot = iota((routes_of, SLOTS), 1)
    wanted = expert_of(slot % per_col // CAP, slot // per_col).astype(f32)
    hit = one_hot(named == wanted)
    pair = (routes_of, routes_of)
    earlier = one_hot(iota(pair, 1) // topk < iota(pair, 0) // topk)
    before = dot(earlier, hit)
    pick = jnp.where(before == (slot % CAP).astype(f32), hit.astype(f32), 0.0).astype(bf16)
    rows = dot(pick, pre_ref[...], (0, 0)).astype(bf16)
    gates = gates_ref[...]
    high = gates.astype(bf16)
    rest = gates - high.astype(f32)
    middle = rest.astype(bf16)
    low = (rest - middle.astype(f32)).astype(bf16)
    facts = jnp.zeros((tok, FACTS), f32)
    for at, part in enumerate((routes, high, middle, low)):
        seat = one_hot(iota((topk, FACTS), 1) == iota((topk, FACTS), 0) + at * topk)
        facts = facts + dot(part, seat)
    left = grad_ref.shape[1] - width
    for col in range(COLS):
        out_ref[col, :per_col, :] = rows[col * per_col : (col + 1) * per_col]
        out_ref[col, per_col : per_col + tok, :] = grad_ref[:, :width]
        out_ref[col, per_col + tok :, :left] = grad_ref[:, width:]
        out_ref[col, per_col + tok :, left : left + FACTS] = facts.astype(bf16)
        out_ref[col, per_col + tok :, left + FACTS :] = jnp.zeros((tok, width - left - FACTS), bf16)


def deal_kernel(col_ref, in_ref, out_ref, place_ref, facts_ref, *, tok, topk):
    width = in_ref.shape[2]
    per_col = RING_SIZE * CAP
    left = out_ref.shape[1] - 2 * width
    tokens = COLS * tok
    me = col_ref[0]
    facts = in_ref[:, per_col + tok :, left : left + FACTS].reshape(tokens, FACTS)
    facts_ref[...] = facts
    square = (FACTS, FACTS)
    turned = dot(one_hot(iota(square, 0) == iota(square, 1)), facts, (1, 1))
    gates = turned[topk : 2 * topk] + turned[2 * topk : 3 * topk] + turned[3 * topk : 4 * topk]
    shape = (SLOTS, tokens)
    slot, token = iota(shape, 0), iota(shape, 1)
    wanted = expert_of(slot // (COLS * CAP), me).astype(f32)
    hit = jnp.zeros(shape, f32)
    gate = jnp.zeros(shape, f32)
    for k in range(topk):
        match = turned[k : k + 1] == wanted
        hit = jnp.where(match, 1.0, hit)
        gate = jnp.where(match, gates[k : k + 1], gate)
    pair = (tokens, tokens)
    first, second = iota(pair, 0), iota(pair, 1)
    earlier = jnp.where(first // tok == second // tok, jnp.where(first < second, 1.0, 0.0), 0.0).astype(bf16)
    before = dot(hit.astype(bf16), earlier)
    same = jnp.where(slot % (COLS * CAP) // CAP == token // tok, hit, 0.0)
    place = jnp.where(before == (slot % CAP).astype(f32), same, 0.0)
    scale = jnp.sum(place * gate, axis=1, keepdims=True)
    place = place.astype(bf16)
    eye = one_hot(first == second)
    place_ref[...] = dot(eye, place, (1, 1)).astype(bf16)
    upper = in_ref[:, per_col : per_col + tok, :].reshape(tokens, width)
    lower = in_ref[:, per_col + tok :, :left].reshape(tokens, left)
    out_ref[:, :width] = (dot(place, upper) * scale).astype(bf16)
    out_ref[:, width : width + left] = (dot(place, lower) * scale).astype(bf16)
    square = (SLOTS, SLOTS)
    slot = iota(square, 0)
    origin = slot % (COLS * CAP) // CAP * per_col + slot // (COLS * CAP) * CAP + slot % CAP
    swap = one_hot(origin == iota(square, 1))
    pre = in_ref[:, :per_col, :].reshape(SLOTS, width)
    out_ref[:, width + left :] = dot(swap, pre).astype(bf16)


def join_kernel(col_ref, back_ref, place_ref, facts_ref, out_ref, *, topk):
    tokens = place_ref.shape[0]
    width = out_ref.shape[1] - FACTS
    me = col_ref[0]
    place = place_ref[...]
    out_ref[:, :width] = dot(place, back_ref[:, :width]).astype(bf16)
    lane = (8, FACTS)
    head = one_hot(iota(lane, 1) == iota(lane, 0))
    dots = dot(head, back_ref[:, width:], (1, 1))[0:1]
    held = place.astype(f32) * dots
    shape = (tokens, SLOTS)
    expert = expert_of(iota(shape, 1) // (COLS * CAP), me).astype(f32)
    facts = facts_ref[...].astype(f32)
    lanes = iota((tokens, FACTS), 1)
    result = jnp.zeros((tokens, FACTS), f32)
    for k in range(topk):
        named = jnp.sum(jnp.where(lanes == k, facts, 0.0), axis=1, keepdims=True)
        value = jnp.sum(jnp.where(named == expert, held, 0.0), axis=1, keepdims=True)
        result = jnp.where(lanes == k, value, result)
    out_ref[:, width:] = result.astype(bf16)


def call(kernel, outs, inputs, flops):
    scalar = inputs[0].shape == (1,)
    in_specs = [pl.BlockSpec(memory_space=pltpu.VMEM) for _ in inputs]
    if scalar:
        in_specs[0] = pl.BlockSpec(memory_space=pltpu.SMEM)
    moved = sum(a.size * a.dtype.itemsize for a in inputs) + sum(a.size * a.dtype.itemsize for a in outs)
    return pl.pallas_call(
        kernel,
        out_shape=outs,
        in_specs=in_specs,
        out_specs=[pl.BlockSpec(memory_space=pltpu.VMEM) for _ in outs],
        compiler_params=pltpu.CompilerParams(vmem_limit_bytes=VMEM_BYTES),
        cost_estimate=pl.CostEstimate(flops=flops, bytes_accessed=moved, transcendentals=0),
    )(*inputs)


def shards(grad_out, saved_pre, gates, routes, w_gate, w_up, w_down):
    tok, topk = routes.shape
    width = grad_out.shape[1]
    pre_width = saved_pre.shape[2]
    hidden_width = pre_width // 2
    me_y = lax.axis_index("y").astype(i32).reshape(1)
    out = jax.ShapeDtypeStruct
    per_col = RING_SIZE * CAP
    tokens = COLS * tok

    pre = saved_pre.reshape(tok * topk, pre_width)
    packed = out((COLS, per_col + 2 * tok, pre_width), bf16)
    (packed,) = call(pack_kernel, [packed], (routes, gates, grad_out, pre), 2 * SLOTS * tok * topk * pre_width)
    packed = lax.all_to_all(packed, "y", 0, 0, tiled=True)

    outs = [out((SLOTS, width + pre_width), bf16), out((tokens, SLOTS), bf16), out((tokens, FACTS), bf16)]
    deal = functools.partial(deal_kernel, tok=tok, topk=topk)
    rows, place, facts = call(deal, outs, (me_y, packed), 2 * SLOTS * SLOTS * pre_width)
    rows = rows.reshape(RING_SIZE, COLS * CAP, width + pre_width)
    rows = lax.all_to_all(rows, RING, 0, 0, tiled=True).reshape(SLOTS, width + pre_width)

    weight_rows = rows[:, :width]
    gate_pre = rows[:, width : width + hidden_width].astype(f32)
    up_pre = rows[:, width + hidden_width :].astype(f32)
    sigmoid_gate = jax.nn.sigmoid(gate_pre)
    activated = gate_pre * sigmoid_gate
    hidden = (activated * up_pre).astype(bf16)
    partial = dot(hidden, weight_rows, (0, 0)).astype(bf16)
    hidden_grad = dot(weight_rows, w_down[0], (1, 1))
    gate_dots = jnp.sum(hidden.astype(f32) * hidden_grad, axis=1, keepdims=True).astype(bf16)
    gate_grad = (hidden_grad * up_pre * sigmoid_gate * (1.0 + gate_pre * (1.0 - sigmoid_gate))).astype(bf16)
    up_grad = (hidden_grad * activated).astype(bf16)
    d_down = lax.psum_scatter(partial, "dp", scatter_dimension=0, tiled=True)
    route_grad = dot(gate_grad, w_gate[0], (1, 1)) + dot(up_grad, w_up[0], (1, 1))
    back = jnp.concatenate([route_grad.astype(bf16), jnp.pad(gate_dots, ((0, 0), (0, FACTS - 1)))], axis=1)
    back = lax.all_to_all(back.reshape(RING_SIZE, COLS * CAP, width + FACTS), RING, 0, 0, tiled=True)
    back = back.reshape(SLOTS, width + FACTS)

    join = functools.partial(join_kernel, topk=topk)
    home = [out((tokens, width + FACTS), bf16)]
    (home,) = call(join, home, (me_y, back, place, facts), 2 * tokens * SLOTS * width)
    home = lax.all_to_all(home.reshape(COLS, tok, width + FACTS), "y", 0, 0, tiled=True)
    total = jnp.sum(home.astype(f32), axis=0)
    d_tokens = total[:, :width].astype(bf16)
    d_gates = total[:, width : width + topk] / gates
    return (d_tokens, d_gates, d_down[None])


def solution(mesh):
    devices = mesh.devices
    dp, node, local = devices.shape
    split = Mesh(devices.reshape(dp, node, local // 2, 2), ("dp", "node", "y", "zh"))
    owner = ("dp", "node", "y", "zh")
    expert = ("node", "y", "zh")
    in_specs = (
        P(owner, None),
        P(owner, None, None),
        P(owner, None),
        P(owner, None),
        P(expert, None, None),
        P(expert, None, None),
        P(expert, None, None),
    )
    out_specs = (P(owner, None), P(owner, None), P(expert, "dp", None))
    return jax.shard_map(shards, mesh=split, in_specs=in_specs, out_specs=out_specs, check_vma=False)
```

time: 419 us -> 379 us (0.905)
  the two profiles are of different devices: /device:TPU:70 before, /device:TPU:64 now
where the time goes in v3:
time: 379 us
  blocking collectives  210 us (55%)
  waiting for transfers between devices  123 us (32%)
  between operations  14.1 us (4%)
  starting transfers between devices  10.8 us (3%)
  matrix products  7.64 us (2%)
  local copies, waits for them, and re-layouts  6.83 us (2%)
  Pallas kernels  4.72 us (1%)
    all_to_all x1, blocking collectives, shards(): lax.all_to_all(rows, RING, 0, 0, tiled=True)  201 us
    all_to_all x1, waiting for transfers between devices, shards(): lax.all_to_all(back.reshape(RING_SIZE, COLS * CAP, width + FACTS), RING,...  107 us
    all_to_all x1, waiting for transfers between devices, shards(): packed = lax.all_to_all(packed, 'y', 0, 0, tiled=True)  16.6 us
    all_to_all x1, blocking collectives, shards(): lax.all_to_all(home.reshape(COLS, tok, width + FACTS), 'y', 0, 0, tiled=T...  9.49 us
    dot_general x4, matrix products, dot(): return lax.dot_general(left, right, dims, preferred_element_type=f32)  7.64 us
  transfers between devices with their start and end apart: 3, of which 2 were waited for; matrix products, arithmetic and copies ran while one was open for 1% of the time, Pallas kernels for 0%

profile of v3, /device:TPU:64, one launch (start us, length us, event | category | flops | bytes accessed | tf_op | source)
XLA Modules:
  0.0 378.8 jit_solution(13024856010321935427)
XLA Ops:
  7.2 0.0 copy-start
  7.2 0.9 copy.18.gates_ref
  8.1 0.8 copy.17.routes_ref
  8.9 0.0 copy-start.2
  8.9 1.0 copy-done.2
  9.9 0.0 copy-start.3
  9.9 0.8 copy-done.3
  10.7 0.8 shard_map.94
  11.5 0.0 copy-start.1
  11.5 1.0 copy-done.1
  12.5 4.5 %all-to-all-start = ((bf16[4,96,1536]{2,1,0:T(8,128)(2,1)}), bf16[4,96,1536]{2,1,0:T(8,128)(2,1)}, u32[]{:S(2)}, u32[]{:S(2)}) async-start(bf16[4,96,1536]{2,1,0:T(8,128)(2,1)} %copy-done.1), calls=%async_computation | async-start | bytes 2359296 | tf_op jit(solution)/shard_map/all_to_all | solution.py:164
  17.0 16.6 %all-to-all-done.in_ref = bf16[4,96,1536]{2,1,0:T(8,128)(2,1)} async-done(((bf16[4,96,1536]{2,1,0:T(8,128)(2,1)}), bf16[4,96,1536]{2,1,0:T(8,128)(2,1)}, u32[]{:S(2)}, u32[]{:S(2)}) %all-to-all-start) | async-done | bytes 1179680 | tf_op jit(solution)/shard_map/all_to_all | solution.py:164
  33.6 2.3 shard_map.95
  35.9 0.0 copy-start.5
  35.9 200.8 %all_to_all.20 = bf16[32,8,3584]{2,1,0:T(8,128)(2,1)S(1)} all-to-all(bf16[32,8,3584]{2,1,0:T(8,128)(2,1)S(1)} %bitcast.24), channel_id=1, replica_groups=mesh['dp'=8,'node'=16,'y'=4,'zh'=2] {'node','zh'}, dimensions={0} | all-to-all | bytes 3670016 | tf_op jit(solution)/shard_map/all_to_all | solution.py:170
  236.7 0.0 copy-start.4
  236.7 0.0 copy-done.5
  236.7 1.2 multiply_reduce_fusion
  237.9 0.1 convert_element_type.55
  238.0 0.0 copy-done
  238.0 0.0 copy-start.6
  238.0 1.0 fusion
  239.1 0.0 copy-done.4
  239.1 0.8 copy-done.6
  239.9 1.2 fusion.9
  241.1 1.1 fusion.14
  242.2 6.3 %all-to-all-start.2 = ((bf16[32,8,2176]{2,1,0:T(8,128)(2,1)}), bf16[32,8,2176]{2,1,0:T(8,128)(2,1)}, u32[]{:S(2)}, u32[]{:S(2)}) async-start(bf16[32,8,2176]{2,1,0:T(8,128)(2,1)} %fusion.14), calls=%async_computation.2 | async-start | bytes 2228224 | tf_op jit(solution)/shard_map/all_to_all | solution.py:186
  248.5 0.0 reduce-scatter.2.cloned.1.call-start
  248.6 4.2 %convolution_convert_fusion = bf16[768,2048]{1,0:T(8,128)(2,1)} fusion(bf16[256,3584]{1,0:T(8,128)(2,1)} %bitcast.30), kind=kOutput, calls=%fused_computation | convolution fusion | flops 808452096 | bytes 4980736 | tf_op jit(solution)/shard_map/dot_general | solution.py:22
  252.8 0.0 reduce-scatter.2.cloned.1.call-update
  252.8 106.6 %all-to-all-done.2 = bf16[32,8,2176]{2,1,0:T(8,128)(2,1)} async-done(((bf16[32,8,2176]{2,1,0:T(8,128)(2,1)}), bf16[32,8,2176]{2,1,0:T(8,128)(2,1)}, u32[]{:S(2)}, u32[]{:S(2)}) %all-to-all-start.2) | async-done | bytes 1114144 | tf_op jit(solution)/shard_map/all_to_all | solution.py:186
  359.4 1.7 shard_map.96
  361.1 9.5 %all_to_all.21 = bf16[4,16,2176]{2,1,0:T(8,128)(2,1)S(1)} all-to-all(bf16[4,16,2176]{2,1,0:T(8,128)(2,1)S(1)} %bitcast.25), channel_id=1, replica_groups=mesh['dp'=8,'node'=16,'y'=4,'zh'=2] {'y'}, dimensions={0} | all-to-all | bytes 557056 | tf_op jit(solution)/shard_map/all_to_all | solution.py:192
  370.6 0.6 slice.53
  371.3 0.7 copy.21
  371.9 0.0 reduce-scatter.2.cloned.1.call-done
  (2 shorter events, 0.0 us)
Async XLA Ops:
  7.2 230.8 %copy-start = (bf16[1,2048,768]{2,1,0:T(8,128)(2,1)S(1)}, bf16[1,2048,768]{2,1,0:T(8,128)(2,1)}, u32[]{:S(2)}) copy-start(bf16[1,2048,768]{2,1,0:T(8,128)(2,1)} %param.12) | copy-start | bytes 9437188
  8.9 1.0 copy-start.2
  9.9 0.8 copy-start.3
  11.5 1.0 copy-start.1
  12.5 21.1 %all-to-all-start = ((bf16[4,96,1536]{2,1,0:T(8,128)(2,1)}), bf16[4,96,1536]{2,1,0:T(8,128)(2,1)}, u32[]{:S(2)}, u32[]{:S(2)}) async-start(bf16[4,96,1536]{2,1,0:T(8,128)(2,1)} %copy-done.1), calls=%async_computation | async-start | bytes 2359296 | tf_op jit(solution)/shard_map/all_to_all | solution.py:164
  35.9 200.8 %copy-start.5 = (bf16[1,768,2048]{2,1,0:T(8,128)(2,1)S(1)}, bf16[1,768,2048]{2,1,0:T(8,128)(2,1)}, u32[]{:S(2)}) copy-start(bf16[1,768,2048]{2,1,0:T(8,128)(2,1)} %param.13) | copy-start | bytes 9437188
  236.7 2.4 copy-start.4
  238.0 1.9 copy-start.6
  242.2 117.2 %all-to-all-start.2 = ((bf16[32,8,2176]{2,1,0:T(8,128)(2,1)}), bf16[32,8,2176]{2,1,0:T(8,128)(2,1)}, u32[]{:S(2)}, u32[]{:S(2)}) async-start(bf16[32,8,2176]{2,1,0:T(8,128)(2,1)} %fusion.14), calls=%async_computation.2 | async-start | bytes 2228224 | tf_op jit(solution)/shard_map/all_to_all | solution.py:186
  248.5 123.4 %reduce-scatter.2.cloned.1.call-start = ((), (), s32[]{:S(2)}) async-start(), calls=%async_computation.5 | async-start | bytes 3538944 | tf_op jit(solution)/shard_map/reduce_scatter | solution.py:183
Sparse Core Ops, SparseCore 0:
  253.3 52.5 reduce-scatter.1

commit v4 on v3

--- a/solution.py
+++ b/solution.py
@@ -7,10 +7,11 @@
 from jax.experimental.pallas import tpu as pltpu
 from jax.sharding import Mesh, PartitionSpec as P
 
-RING = ("node", "zh")
+RING = ("zh", "node")
 CAP = 2
 COLS = 4
 RING_SIZE = 32
+HALF = RING_SIZE // 2
 SLOTS = COLS * RING_SIZE * CAP
 FACTS = 128
 VMEM_BYTES = 24 * 1024 * 1024
@@ -27,7 +28,7 @@
 
 
 def expert_of(ring_index, column):
-    return (ring_index // 2) * 8 + column * 2 + ring_index % 2
+    return (ring_index % HALF) * 8 + column * 2 + ring_index // HALF
 
 
 def one_hot(mask):
@@ -35,12 +36,12 @@
 
 
 def pack_kernel(routes_ref, gates_ref, grad_ref, pre_ref, out_ref):
-    tok, topk = routes_ref.shape
+    topk, tok = routes_ref.shape
     routes_of, width = tok * topk, pre_ref.shape[1]
     per_col = RING_SIZE * CAP
     routes = routes_ref[...].astype(f32).astype(bf16)
     row_tok, row_k = iota((routes_of, tok), 0) // topk, iota((routes_of, topk), 0) % topk
-    spread = dot(one_hot(row_tok == iota((routes_of, tok), 1)), routes)
+    spread = dot(one_hot(row_tok == iota((routes_of, tok), 1)), routes, (1, 1))
     named = jnp.sum(jnp.where(row_k == iota((routes_of, topk), 1), spread, 0.0), axis=1, keepdims=True)
     slot = iota((routes_of, SLOTS), 1)
     wanted = expert_of(slot % per_col // CAP, slot // per_col).astype(f32)
@@ -58,7 +59,7 @@
     facts = jnp.zeros((tok, FACTS), f32)
     for at, part in enumerate((routes, high, middle, low)):
         seat = one_hot(iota((topk, FACTS), 1) == iota((topk, FACTS), 0) + at * topk)
-        facts = facts + dot(part, seat)
+        facts = facts + dot(part, seat, (0, 0))
     left = grad_ref.shape[1] - width
     for col in range(COLS):
         out_ref[col, :per_col, :] = rows[col * per_col : (col + 1) * per_col]
@@ -160,7 +161,7 @@
 
     pre = saved_pre.reshape(tok * topk, pre_width)
     packed = out((COLS, per_col + 2 * tok, pre_width), bf16)
-    (packed,) = call(pack_kernel, [packed], (routes, gates, grad_out, pre), 2 * SLOTS * tok * topk * pre_width)
+    (packed,) = call(pack_kernel, [packed], (routes.T, gates.T, grad_out, pre), 2 * SLOTS * tok * topk * pre_width)
     packed = lax.all_to_all(packed, "y", 0, 0, tiled=True)
 
     outs = [out((SLOTS, width + pre_width), bf16), out((tokens, SLOTS), bf16), out((tokens, FACTS), bf16)]

time: 379 us -> 387 us (1.021)
  the two profiles are of different devices: /device:TPU:64 before, /device:TPU:6 now
where the time goes in v4:
time: 387 us; the launch traced here: 386 us
  blocking collectives  204 us (53%)
  waiting for transfers between devices  134 us (35%)
  between operations  14.1 us (4%)
  starting transfers between devices  12.6 us (3%)
  matrix products  7.57 us (2%)
  local copies, waits for them, and re-layouts  6.73 us (2%)
  Pallas kernels  5.42 us (1%)
    all_to_all x1, blocking collectives, shards(): lax.all_to_all(rows, RING, 0, 0, tiled=True)  204 us
    all_to_all x1, waiting for transfers between devices, shards(): lax.all_to_all(back.reshape(RING_SIZE, COLS * CAP, width + FACTS), RING,...  111 us
    all_to_all x1, waiting for transfers between devices, shards(): packed = lax.all_to_all(packed, 'y', 0, 0, tiled=True)  16.7 us
  transfers between devices with their start and end apart: 4, of which 3 were waited for; matrix products, arithmetic and copies ran while one was open for 1% of the time, Pallas kernels for 1%

profile of v4, /device:TPU:6, one launch (start us, length us, event | category | flops | bytes accessed | tf_op | source)
XLA Modules:
  0.0 385.9 jit_solution(6930673980026503884)
XLA Ops:
  7.2 0.0 copy-start
  7.2 0.0 copy-start.2
  7.2 1.1 copy-done.2
  8.3 0.0 copy-start.3
  8.3 0.8 copy-done.3
  9.2 0.0 copy-start.4
  9.2 0.7 copy-done.4
  9.9 0.0 copy-start.6
  9.9 0.7 copy-done.6
  10.5 0.8 shard_map.94
  11.3 0.0 copy-start.1
  11.3 1.0 copy-done.1
  12.3 4.5 %all-to-all-start = ((bf16[4,96,1536]{2,1,0:T(8,128)(2,1)}), bf16[4,96,1536]{2,1,0:T(8,128)(2,1)}, u32[]{:S(2)}, u32[]{:S(2)}) async-start(bf16[4,96,1536]{2,1,0:T(8,128)(2,1)} %copy-done.1), calls=%async_computation | async-start | bytes 2359296 | tf_op jit(solution)/shard_map/all_to_all | solution.py:165
  16.8 16.7 %all-to-all-done.in_ref = bf16[4,96,1536]{2,1,0:T(8,128)(2,1)} async-done(((bf16[4,96,1536]{2,1,0:T(8,128)(2,1)}), bf16[4,96,1536]{2,1,0:T(8,128)(2,1)}, u32[]{:S(2)}, u32[]{:S(2)}) %all-to-all-start) | async-done | bytes 1179680 | tf_op jit(solution)/shard_map/all_to_all | solution.py:165
  33.5 2.3 shard_map.95
  35.7 0.0 copy-start.8
  35.7 204.4 %all_to_all.20 = bf16[32,8,3584]{2,1,0:T(8,128)(2,1)S(1)} all-to-all(bf16[32,8,3584]{2,1,0:T(8,128)(2,1)S(1)} %bitcast.26), channel_id=1, replica_groups=mesh['dp'=8,'node'=16,'y'=4,'zh'=2] {'zh','node'}, dimensions={0} | all-to-all | bytes 3670016 | tf_op jit(solution)/shard_map/all_to_all | solution.py:171
  240.1 0.0 copy-start.7
  240.1 0.0 copy-done.8
  240.1 1.2 multiply_reduce_fusion
  241.3 0.1 convert_element_type.55
  241.4 0.0 copy-done
  241.5 0.0 copy-start.9
  241.5 1.0 fusion
  242.5 0.0 copy-done.7
  242.5 0.8 copy-done.9
  243.3 1.1 fusion.9
  244.5 1.1 fusion.14
  245.6 4.7 %all-to-all-start.2 = ((bf16[32,8,2176]{2,1,0:T(8,128)(2,1)}), bf16[32,8,2176]{2,1,0:T(8,128)(2,1)}, u32[]{:S(2)}, u32[]{:S(2)}) async-start(bf16[32,8,2176]{2,1,0:T(8,128)(2,1)} %fusion.14), calls=%async_computation.2 | async-start | bytes 2228224 | tf_op jit(solution)/shard_map/all_to_all | solution.py:187
  250.3 0.0 reduce-scatter.2.cloned.1.call-start
  250.3 4.2 %convolution_convert_fusion = bf16[768,2048]{1,0:T(8,128)(2,1)} fusion(bf16[256,3584]{1,0:T(8,128)(2,1)} %bitcast.33), kind=kOutput, calls=%fused_computation | convolution fusion | flops 808452096 | bytes 4980736 | tf_op jit(solution)/shard_map/dot_general | solution.py:23
  254.5 0.0 copy-start.5
  254.5 0.0 reduce-scatter.2.cloned.1.call-update
  254.6 110.6 %all-to-all-done.2 = bf16[32,8,2176]{2,1,0:T(8,128)(2,1)} async-done(((bf16[32,8,2176]{2,1,0:T(8,128)(2,1)}), bf16[32,8,2176]{2,1,0:T(8,128)(2,1)}, u32[]{:S(2)}, u32[]{:S(2)}) %all-to-all-start.2) | async-done | bytes 1114144 | tf_op jit(solution)/shard_map/all_to_all | solution.py:187
  365.1 2.4 shard_map.96
  367.6 3.4 all-to-all-start.3
  371.0 0.0 copy-done.5
  371.0 0.1 copy.14
  371.1 6.6 %all-to-all-done.3 = bf16[4,16,2176]{2,1,0:T(8,128)(2,1)S(1)} async-done(((bf16[4,16,2176]{2,1,0:T(8,128)(2,1)}), bf16[4,16,2176]{2,1,0:T(8,128)(2,1)S(1)}, u32[]{:S(2)}, u32[]{:S(2)}) %all-to-all-start.3) | async-done | bytes 278560 | tf_op jit(solution)/shard_map/all_to_all | solution.py:193
  377.8 0.6 slice.53
  378.4 0.7 copy.15
  379.1 0.0 reduce-scatter.2.cloned.1.call-done
  (2 shorter events, 0.0 us)
Async XLA Ops:
  7.2 234.3 %copy-start = (bf16[1,2048,768]{2,1,0:T(8,128)(2,1)S(1)}, bf16[1,2048,768]{2,1,0:T(8,128)(2,1)}, u32[]{:S(2)}) copy-start(bf16[1,2048,768]{2,1,0:T(8,128)(2,1)} %param.12) | copy-start | bytes 9437188
  7.2 1.1 copy-start.2
  8.3 0.8 copy-start.3
  9.2 0.7 copy-start.4
  9.9 0.7 copy-start.6
  11.3 1.0 copy-start.1
  12.3 21.1 %all-to-all-start = ((bf16[4,96,1536]{2,1,0:T(8,128)(2,1)}), bf16[4,96,1536]{2,1,0:T(8,128)(2,1)}, u32[]{:S(2)}, u32[]{:S(2)}) async-start(bf16[4,96,1536]{2,1,0:T(8,128)(2,1)} %copy-done.1), calls=%async_computation | async-start | bytes 2359296 | tf_op jit(solution)/shard_map/all_to_all | solution.py:165
  35.7 204.4 %copy-start.8 = (bf16[1,768,2048]{2,1,0:T(8,128)(2,1)S(1)}, bf16[1,768,2048]{2,1,0:T(8,128)(2,1)}, u32[]{:S(2)}) copy-start(bf16[1,768,2048]{2,1,0:T(8,128)(2,1)} %param.13) | copy-start | bytes 9437188
  240.1 2.4 copy-start.7
  241.5 1.9 copy-start.9
  245.6 119.5 %all-to-all-start.2 = ((bf16[32,8,2176]{2,1,0:T(8,128)(2,1)}), bf16[32,8,2176]{2,1,0:T(8,128)(2,1)}, u32[]{:S(2)}, u32[]{:S(2)}) async-start(bf16[32,8,2176]{2,1,0:T(8,128)(2,1)} %fusion.14), calls=%async_computation.2 | async-start | bytes 2228224 | tf_op jit(solution)/shard_map/all_to_all | solution.py:187
  250.3 128.8 %reduce-scatter.2.cloned.1.call-start = ((), (), s32[]{:S(2)}) async-start(), calls=%async_computation.5 | async-start | bytes 3538944 | tf_op jit(solution)/shard_map/reduce_scatter | solution.py:184
  254.5 116.5 %copy-start.5 = (f32[16,8]{0,1:T(8,128)S(1)}, f32[16,8]{0,1:T(8,128)}, u32[]{:S(2)}) copy-start(f32[16,8]{0,1:T(8,128)} %param.9) | copy-start | bytes 1540
  367.6 10.2 %all-to-all-start.3 = ((bf16[4,16,2176]{2,1,0:T(8,128)(2,1)}), bf16[4,16,2176]{2,1,0:T(8,128)(2,1)S(1)}, u32[]{:S(2)}, u32[]{:S(2)}) async-start(bf16[4,16,2176]{2,1,0:T(8,128)(2,1)} %bitcast.11), calls=%async_computation.3 | async-start | bytes 557056 | tf_op jit(solution)/shard_map/all_to_all | solution.py:193
Sparse Core Ops, SparseCore 0:
  255.1 49.4 reduce-scatter.1

commit v5 on v4

--- a/solution.py
+++ b/solution.py
@@ -14,6 +14,9 @@
 HALF = RING_SIZE // 2
 SLOTS = COLS * RING_SIZE * CAP
 FACTS = 128
+RAISES = (64, 32, 8, 4, 2, 1)
+MIDDLE = 2.0**14
+LOW = 2.0**20
 VMEM_BYTES = 24 * 1024 * 1024
 f32, bf16, i32 = jnp.float32, jnp.bfloat16, jnp.int32
 
@@ -35,7 +38,7 @@
     return jnp.where(mask, 1.0, 0.0).astype(bf16)
 
 
-def pack_kernel(routes_ref, gates_ref, grad_ref, pre_ref, out_ref):
+def pack_kernel(routes_ref, gates_ref, grad_ref, pre_ref, out_ref, tokens_ref):
     topk, tok = routes_ref.shape
     routes_of, width = tok * topk, pre_ref.shape[1]
     per_col = RING_SIZE * CAP
@@ -56,59 +59,109 @@
     rest = gates - high.astype(f32)
     middle = rest.astype(bf16)
     low = (rest - middle.astype(f32)).astype(bf16)
-    facts = jnp.zeros((tok, FACTS), f32)
-    for at, part in enumerate((routes, high, middle, low)):
-        seat = one_hot(iota((topk, FACTS), 1) == iota((topk, FACTS), 0) + at * topk)
-        facts = facts + dot(part, seat, (0, 0))
-    left = grad_ref.shape[1] - width
+    seats = [one_hot(iota((topk, FACTS), 1) == iota((topk, FACTS), 0) + at * topk) for at in range(4)]
+    named = dot(routes, seats[0], (0, 0))
+    facts = named + dot(high, seats[1], (0, 0)) + dot(middle, seats[2], (0, 0)) * MIDDLE
+    facts = facts + dot(low, seats[3], (0, 0)) * LOW
+    grad = grad_ref[...].astype(f32)
+    top = jnp.max(jnp.abs(grad), axis=1, keepdims=True)
+    scale, raised = jnp.ones((tok, 1), f32), jnp.zeros((tok, 1), f32)
+    for step in RAISES:
+        fits = top * (scale * 2.0**step) <= 2.0**15
+        scale = jnp.where(fits, scale * 2.0**step, scale)
+        raised = jnp.where(fits, raised + step, raised)
+    facts = jnp.where(iota((tok, FACTS), 1) == 4 * topk, raised, facts)
+    tokens_ref[:, : grad.shape[1]] = grad * scale
+    tokens_ref[:, grad.shape[1] :] = facts
     for col in range(COLS):
         out_ref[col, :per_col, :] = rows[col * per_col : (col + 1) * per_col]
-        out_ref[col, per_col : per_col + tok, :] = grad_ref[:, :width]
-        out_ref[col, per_col + tok :, :left] = grad_ref[:, width:]
-        out_ref[col, per_col + tok :, left : left + FACTS] = facts.astype(bf16)
-        out_ref[col, per_col + tok :, left + FACTS :] = jnp.zeros((tok, width - left - FACTS), bf16)
+        out_ref[col, per_col:, :FACTS] = named.astype(bf16)
+        out_ref[col, per_col:, FACTS:] = jnp.zeros((tok, width - FACTS), bf16)
 
 
 def deal_kernel(col_ref, in_ref, out_ref, place_ref, facts_ref, *, tok, topk):
     width = in_ref.shape[2]
     per_col = RING_SIZE * CAP
-    left = out_ref.shape[1] - 2 * width
     tokens = COLS * tok
     me = col_ref[0]
-    facts = in_ref[:, per_col + tok :, left : left + FACTS].reshape(tokens, FACTS)
+    facts = in_ref[:, per_col:, :FACTS].reshape(tokens, FACTS)
     facts_ref[...] = facts
     square = (FACTS, FACTS)
     turned = dot(one_hot(iota(square, 0) == iota(square, 1)), facts, (1, 1))
-    gates = turned[topk : 2 * topk] + turned[2 * topk : 3 * topk] + turned[3 * topk : 4 * topk]
     shape = (SLOTS, tokens)
     slot, token = iota(shape, 0), iota(shape, 1)
     wanted = expert_of(slot // (COLS * CAP), me).astype(f32)
     hit = jnp.zeros(shape, f32)
-    gate = jnp.zeros(shape, f32)
     for k in range(topk):
-        match = turned[k : k + 1] == wanted
-        hit = jnp.where(match, 1.0, hit)
-        gate = jnp.where(match, gates[k : k + 1], gate)
+        hit = jnp.where(turned[k : k + 1] == wanted, 1.0, hit)
     pair = (tokens, tokens)
     first, second = iota(pair, 0), iota(pair, 1)
     earlier = jnp.where(first // tok == second // tok, jnp.where(first < second, 1.0, 0.0), 0.0).astype(bf16)
     before = dot(hit.astype(bf16), earlier)
     same = jnp.where(slot % (COLS * CAP) // CAP == token // tok, hit, 0.0)
-    place = jnp.where(before == (slot % CAP).astype(f32), same, 0.0)
-    scale = jnp.sum(place * gate, axis=1, keepdims=True)
-    place = place.astype(bf16)
+    place = jnp.where(before == (slot % CAP).astype(f32), same, 0.0).astype(bf16)
     eye = one_hot(first == second)
     place_ref[...] = dot(eye, place, (1, 1)).astype(bf16)
-    upper = in_ref[:, per_col : per_col + tok, :].reshape(tokens, width)
-    lower = in_ref[:, per_col + tok :, :left].reshape(tokens, left)
-    out_ref[:, :width] = (dot(place, upper) * scale).astype(bf16)
-    out_ref[:, width : width + left] = (dot(place, lower) * scale).astype(bf16)
     square = (SLOTS, SLOTS)
     slot = iota(square, 0)
     origin = slot % (COLS * CAP) // CAP * per_col + slot // (COLS * CAP) * CAP + slot % CAP
     swap = one_hot(origin == iota(square, 1))
-    pre = in_ref[:, :per_col, :].reshape(SLOTS, width)
-    out_ref[:, width + left :] = dot(swap, pre).astype(bf16)
+    out_ref[...] = dot(swap, in_ref[:, :per_col, :].reshape(SLOTS, width)).astype(bf16)
+
+
+def weigh_kernel(at_ref, in_ref, *out_refs, tok, topk):
+    tokens = in_ref.shape[0]
+    width = in_ref.shape[1] - FACTS
+    me, place_me = at_ref[0], at_ref[1]
+    square = (FACTS, FACTS)
+    turned = dot(one_hot(iota(square, 0) == iota(square, 1)), in_ref[:, width:], (1, 1))
+    routes = turned[:topk]
+    gates = turned[topk : 2 * topk] + turned[2 * topk : 3 * topk] * (1.0 / MIDDLE)
+    gates = gates + turned[3 * topk : 4 * topk] * (1.0 / LOW)
+    raised = turned[4 * topk : 4 * topk + 1]
+    lower = jnp.ones((1, tokens), f32)
+    for step in RAISES:
+        has = raised >= step
+        lower = jnp.where(has, lower * 2.0**-step, lower)
+        raised = jnp.where(has, raised - step, raised)
+    hits, gate = [], []
+    stack = jnp.zeros((8, tokens), f32)
+    row = iota((8, tokens), 0)
+    for col in range(COLS):
+        wanted = expert_of(place_me, (me + col) % COLS).astype(f32)
+        match = routes == wanted
+        hits.append(jnp.sum(jnp.where(match, 1.0, 0.0), axis=0, keepdims=True))
+        gate.append(jnp.sum(jnp.where(match, gates, 0.0), axis=0, keepdims=True))
+        stack = jnp.where(row == col, hits[col], stack)
+    pair = (tokens, tokens)
+    first, second = iota(pair, 0), iota(pair, 1)
+    earlier = jnp.where(first // tok == second // tok, jnp.where(first < second, 1.0, 0.0), 0.0).astype(bf16)
+    before = dot(stack.astype(bf16), earlier)
+    shape = (RING_SIZE * CAP, tokens)
+    slot, token = iota(shape, 0), iota(shape, 1)
+    for col in range(COLS):
+        place = jnp.where(slot // CAP == token // tok, hits[col], 0.0)
+        place = jnp.where(before[col : col + 1] == (slot % CAP).astype(f32), place, 0.0)
+        scale = jnp.sum(place * gate[col], axis=1, keepdims=True)
+        unit = jnp.sum(place * lower, axis=1, keepdims=True)
+        rows = dot(place.astype(bf16), in_ref[:, :width]) * unit
+        out_refs[col][...] = (rows * scale).astype(bf16)
+
+
+def gather_kernel(col_ref, *refs):
+    in_refs, out_ref = refs[:-1], refs[-1]
+    me = col_ref[0]
+    per_col = RING_SIZE * CAP
+    shape = (SLOTS, per_col)
+    slot = iota(shape, 0)
+    column = slot % (COLS * CAP) // CAP
+    origin = slot // (COLS * CAP) * CAP + slot % CAP
+    total = jnp.zeros(out_ref.shape, f32)
+    for hop, ref in enumerate(in_refs):
+        away = (me - hop + COLS) % COLS
+        picked = jnp.where(column == away, jnp.where(origin == iota(shape, 1), 1.0, 0.0), 0.0)
+        total = total + dot(picked.astype(bf16), ref[...])
+    out_ref[...] = total.astype(bf16)
 
 
 def join_kernel(col_ref, back_ref, place_ref, facts_ref, out_ref, *, topk):
@@ -134,7 +187,7 @@
 
 
 def call(kernel, outs, inputs, flops):
-    scalar = inputs[0].shape == (1,)
+    scalar = inputs[0].ndim == 1
     in_specs = [pl.BlockSpec(memory_space=pltpu.VMEM) for _ in inputs]
     if scalar:
         in_specs[0] = pl.BlockSpec(memory_space=pltpu.SMEM)
@@ -155,24 +208,37 @@
     pre_width = saved_pre.shape[2]
     hidden_width = pre_width // 2
     me_y = lax.axis_index("y").astype(i32).reshape(1)
+    me_z = (lax.axis_index("zh") * HALF + lax.axis_index("node")).astype(i32).reshape(1)
     out = jax.ShapeDtypeStruct
     per_col = RING_SIZE * CAP
     tokens = COLS * tok
 
     pre = saved_pre.reshape(tok * topk, pre_width)
-    packed = out((COLS, per_col + 2 * tok, pre_width), bf16)
-    (packed,) = call(pack_kernel, [packed], (routes.T, gates.T, grad_out, pre), 2 * SLOTS * tok * topk * pre_width)
+    outs = [out((COLS, per_col + tok, pre_width), bf16), out((tok, width + FACTS), f32)]
+    inputs = (routes.T, gates.T, grad_out, pre)
+    packed, own = call(pack_kernel, outs, inputs, 2 * SLOTS * tok * topk * pre_width)
     packed = lax.all_to_all(packed, "y", 0, 0, tiled=True)
 
-    outs = [out((SLOTS, width + pre_width), bf16), out((tokens, SLOTS), bf16), out((tokens, FACTS), bf16)]
+    ring_tokens = lax.all_gather(own.astype(jnp.float16), RING, axis=0, tiled=True)
+    outs = [out((SLOTS, pre_width), bf16), out((tokens, SLOTS), bf16), out((tokens, FACTS), bf16)]
     deal = functools.partial(deal_kernel, tok=tok, topk=topk)
-    rows, place, facts = call(deal, outs, (me_y, packed), 2 * SLOTS * SLOTS * pre_width)
-    rows = rows.reshape(RING_SIZE, COLS * CAP, width + pre_width)
-    rows = lax.all_to_all(rows, RING, 0, 0, tiled=True).reshape(SLOTS, width + pre_width)
-
-    weight_rows = rows[:, :width]
-    gate_pre = rows[:, width : width + hidden_width].astype(f32)
-    up_pre = rows[:, width + hidden_width :].astype(f32)
+    pre_rows, place, facts = call(deal, outs, (me_y, packed), 2 * SLOTS * SLOTS * pre_width)
+    pre_rows, ring_tokens = lax.optimization_barrier((pre_rows, ring_tokens))
+    pre_rows = lax.all_to_all(pre_rows.reshape(RING_SIZE, COLS * CAP, pre_width), RING, 0, 0, tiled=True)
+    pre_rows = pre_rows.reshape(SLOTS, pre_width)
+
+    weigh = functools.partial(weigh_kernel, tok=tok, topk=topk)
+    outs = [out((per_col, width), bf16)] * COLS
+    at = jnp.concatenate([me_y, me_z])
+    sent = call(weigh, outs, (at, ring_tokens.astype(bf16)), 2 * SLOTS * tok * RING_SIZE * width)
+    came = [sent[0]]
+    for hop in range(1, COLS):
+        came.append(lax.ppermute(sent[hop], "y", [(col, (col + hop) % COLS) for col in range(COLS)]))
+    outs = [out((SLOTS, width), bf16)]
+    (weight_rows,) = call(gather_kernel, outs, (me_y, *came), 2 * SLOTS * SLOTS * width)
+
+    gate_pre = pre_rows[:, :hidden_width].astype(f32)
+    up_pre = pre_rows[:, hidden_width:].astype(f32)
     sigmoid_gate = jax.nn.sigmoid(gate_pre)
     activated = gate_pre * sigmoid_gate
     hidden = (activated * up_pre).astype(bf16)

time: 387 us -> 334 us (0.86)
  blocking collectives: 204 us -> 86.7 us
  waiting for transfers between devices: 134 us -> 162 us
  starting transfers between devices: 12.6 us -> 38.2 us
  matrix products: 7.57 us -> 12.2 us
    all_to_all x1 -> x0, blocking collectives: 204 us -> none  [shards(): lax.all_to_all(rows, RING, 0, 0, tiled=True)]
    all_gather x0 -> x1, blocking collectives: none -> 86.7 us  [shards(): lax.all_gather(own.astype(jnp.float16), RING, axis=0, tiled=True)]
    all_to_all x0 -> x1, waiting for transfers between devices: none -> 51.8 us  [shards(): lax.all_to_all(pre_rows.reshape(RING_SIZE, COLS * CAP, pre_width), RING,...]
    all_to_all x1, waiting for transfers between devices: 16.7 us -> 0.01 us  [shards(): packed = lax.all_to_all(packed, 'y', 0, 0, tiled=True)]
    all_to_all x0 -> x1, starting transfers between devices: none -> 12.7 us  [shards(): lax.all_to_all(pre_rows.reshape(RING_SIZE, COLS * CAP, pre_width), RING,...]
    ppermute x0 -> x3, starting transfers between devices: none -> 12.2 us  [shards(): lax.ppermute(sent[hop], 'y', [(col, (col + hop) % COLS) for col in range(...]
    all_to_all x1, waiting for transfers between devices: 111 us -> 99.3 us  [shards(): lax.all_to_all(back.reshape(RING_SIZE, COLS * CAP, width + FACTS), RING,...]
    dot_general x4, matrix products: 7.57 us -> 12.2 us  [dot(): return lax.dot_general(left, right, dims, preferred_element_type=f32)]
  transfers between devices with their start and end apart: 4 -> 8, of which waited for: 3 -> 5; matrix products, arithmetic and copies ran while one was open for 1% -> 2% of each run, Pallas kernels for 1% -> 2%
where the time goes in v5:
time: 334 us; the launch traced here: 333 us
  waiting for transfers between devices  162 us (49%)
  blocking collectives  86.7 us (26%)
  starting transfers between devices  38.2 us (11%)
  between operations  14.2 us (4%)
  matrix products  12.2 us (4%)
  Pallas kernels  8.71 us (3%)
  local copies, waits for them, and re-layouts  7.65 us (2%)
    all_to_all x1, waiting for transfers between devices, shards(): lax.all_to_all(back.reshape(RING_SIZE, COLS * CAP, width + FACTS), RING,...  99.3 us
    all_gather x1, blocking collectives, shards(): lax.all_gather(own.astype(jnp.float16), RING, axis=0, tiled=True)  86.7 us
    all_to_all x1, waiting for transfers between devices, shards(): lax.all_to_all(pre_rows.reshape(RING_SIZE, COLS * CAP, pre_width), RING,...  51.8 us
    all_to_all x1, starting transfers between devices, shards(): lax.all_to_all(pre_rows.reshape(RING_SIZE, COLS * CAP, pre_width), RING,...  12.7 us
    dot_general x4, matrix products, dot(): return lax.dot_general(left, right, dims, preferred_element_type=f32)  12.2 us
    ppermute x3, starting transfers between devices, shards(): lax.ppermute(sent[hop], 'y', [(col, (col + hop) % COLS) for col in range(...  12.2 us
    pallas_call x5, Pallas kernels, call(): pl.pallas_call(kernel, out_shape=outs, in_specs=in_specs, out_specs=[pl.B...  8.71 us
    unnamed x22, local copies, waits for them, and re-layouts  6.91 us
  transfers between devices with their start and end apart: 8, of which 5 were waited for; matrix products, arithmetic and copies ran while one was open for 2% of the time, Pallas kernels for 2%

profile of v5, /device:TPU:6, one launch (start us, length us, event | category | flops | bytes accessed | tf_op | source)
XLA Modules:
  0.0 333.2 jit_solution(3977760771620958510)
XLA Ops:
  7.2 0.0 copy-start
  7.2 0.0 copy-start.4
  7.2 1.1 copy-done.4
  8.3 0.8 copy-done.5
  9.2 0.7 copy-done.6
  9.9 0.7 copy-done.8
  10.5 0.8 shard_map.94
  11.3 0.0 copy-start.2
  11.3 0.9 copy-done.2
  12.3 4.5 %all-to-all-start = ((bf16[4,80,1536]{2,1,0:T(8,128)(2,1)}), bf16[4,80,1536]{2,1,0:T(8,128)(2,1)}, u32[]{:S(2)}, u32[]{:S(2)}) async-start(bf16[4,80,1536]{2,1,0:T(8,128)(2,1)} %copy-done.2), calls=%async_computation | async-start | bytes 1966080 | tf_op jit(solution)/shard_map/all_to_all | solution.py:220
  16.7 86.7 %all-gather.1 = f16[512,2176]{1,0:T(8,128)(2,1)} all-gather(f16[16,2176]{1,0:T(8,128)(2,1)S(1)} %convert_element_type.50), channel_id=1, replica_groups=mesh['dp'=8,'node'=16,'y'=4,'zh'=2] {'zh','node'}, dimensions={0}, use_global_device_ids=true | all-gather | bytes 2297856 | tf_op jit(solution)/shard_map/all_gather | solution.py:222
  103.5 0.0 all-to-all-done.in_ref
  103.5 1.9 shard_map.95
  105.4 0.0 copy-start.3
  105.4 0.9 copy-done.3
  106.3 12.7 %all-to-all-start.1 = ((bf16[32,8,1536]{2,1,0:T(8,128)(2,1)}), bf16[32,8,1536]{2,1,0:T(8,128)(2,1)}, u32[]{:S(2)}, u32[]{:S(2)}) async-start(bf16[32,8,1536]{2,1,0:T(8,128)(2,1)} %bitcast.29), calls=%async_computation.1 | async-start | bytes 1572864 | tf_op jit(solution)/shard_map/all_to_all | solution.py:227
  118.9 0.1 pad_add_fusion.at_ref
  119.0 1.9 convert_element_type.51.in_ref
  120.9 2.4 shard_map.96
  123.3 4.0 %collective-permute-start = (bf16[64,2048]{1,0:T(8,128)(2,1)S(1)}, bf16[64,2048]{1,0:T(8,128)(2,1)S(1)}, u32[]{:S(2)}, u32[]{:S(2)}) collective-permute-start(bf16[64,2048]{1,0:T(8,128)(2,1)S(1)} %get-tuple-element.19), channel_id=1, source_target_pairs={{0,2},{2,4},{4,6},{6,0},{1,3},{3,5},{5,7},{7,1},{8,10},{10,12},{12... | collective-permute-start | bytes 786440 | tf_op jit(solution)/shard_map/ppermute | solution.py:236
  127.3 4.5 %collective-permute-start.1 = (bf16[64,2048]{1,0:T(8,128)(2,1)S(1)}, bf16[64,2048]{1,0:T(8,128)(2,1)S(1)}, u32[]{:S(2)}, u32[]{:S(2)}) collective-permute-start(bf16[64,2048]{1,0:T(8,128)(2,1)S(1)} %get-tuple-element.20), channel_id=1, source_target_pairs={{0,4},{2,6},{4,0},{6,2},{1,5},{3,7},{5,1},{7,3},{8,12},{10,14},{12... | collective-permute-start | bytes 786440 | tf_op jit(solution)/shard_map/ppermute | solution.py:236
  131.8 3.7 %collective-permute-start.2 = (bf16[64,2048]{1,0:T(8,128)(2,1)S(1)}, bf16[64,2048]{1,0:T(8,128)(2,1)S(1)}, u32[]{:S(2)}, u32[]{:S(2)}) collective-permute-start(bf16[64,2048]{1,0:T(8,128)(2,1)S(1)} %get-tuple-element.21), channel_id=1, source_target_pairs={{0,6},{2,0},{4,2},{6,4},{1,7},{3,1},{5,3},{7,5},{8,14},{10,8},{12,... | collective-permute-start | bytes 786440 | tf_op jit(solution)/shard_map/ppermute | solution.py:236
  135.5 0.0 collective-permute-done.refs_1_
  135.5 1.6 collective-permute-done.1.refs_2_
  137.1 3.0 collective-permute-done.2.refs_3_
  140.1 1.2 shard_map.97
  141.3 0.0 copy-start.1
  141.3 1.0 copy-done.1
  142.3 51.8 %all-to-all-done.1 = bf16[32,8,1536]{2,1,0:T(8,128)(2,1)} async-done(((bf16[32,8,1536]{2,1,0:T(8,128)(2,1)}), bf16[32,8,1536]{2,1,0:T(8,128)(2,1)}, u32[]{:S(2)}, u32[]{:S(2)}) %all-to-all-start.1) | async-done | bytes 786464 | tf_op jit(solution)/shard_map/all_to_all | solution.py:227
  194.1 3.5 %multiply_reduce_fusion = (bf16[256]{0:T(256)(128)(2,1)S(1)}, f32[256,768]{1,0:T(8,128)S(1)}) fusion(bf16[256,1536]{1,0:T(8,128)(2,1)} %bitcast.7, bf16[256,2048]{1,0:T(8,128)(2,1)} %copy-done.1, bf16[1,768,2048]{2,1,0:T(8,128)(2,1)} %param.13), kind=kOutput, calls=%fused_computation.26 | convolution fusion | flops 807468800 | bytes 5767680 | tf_op jit(solution)/shard_map/dot_general | solution.py:26
  197.6 0.1 convert_element_type.63
  197.7 0.0 copy-done
  197.7 0.0 copy-start.9
  197.7 2.2 fusion
  199.9 0.0 copy-done.9
  199.9 2.3 fusion.9
  202.2 1.1 fusion.14
  203.3 4.7 %all-to-all-start.2 = ((bf16[32,8,2176]{2,1,0:T(8,128)(2,1)}), bf16[32,8,2176]{2,1,0:T(8,128)(2,1)}, u32[]{:S(2)}, u32[]{:S(2)}) async-start(bf16[32,8,2176]{2,1,0:T(8,128)(2,1)} %fusion.14), calls=%async_computation.2 | async-start | bytes 2228224 | tf_op jit(solution)/shard_map/all_to_all | solution.py:253
  208.0 0.0 reduce-scatter.2.cloned.1.call-start
  208.0 4.2 %convolution_convert_fusion = bf16[768,2048]{1,0:T(8,128)(2,1)} fusion(bf16[256,2048]{1,0:T(8,128)(2,1)} %copy-done.1, bf16[256,1536]{1,0:T(8,128)(2,1)} %bitcast.7), kind=kOutput, calls=%fused_computation | convolution fusion | flops 808452096 | bytes 4980736 | tf_op jit(solution)/shard_map/dot_general | solution.py:26
  212.2 0.0 reduce-scatter.2.cloned.1.call-update
  212.3 99.3 %all-to-all-done.2 = bf16[32,8,2176]{2,1,0:T(8,128)(2,1)} async-done(((bf16[32,8,2176]{2,1,0:T(8,128)(2,1)}), bf16[32,8,2176]{2,1,0:T(8,128)(2,1)}, u32[]{:S(2)}, u32[]{:S(2)}) %all-to-all-start.2) | async-done | bytes 1114144 | tf_op jit(solution)/shard_map/all_to_all | solution.py:253
  311.6 2.4 shard_map.98
  314.0 4.2 %all-to-all-start.3 = ((bf16[4,16,2176]{2,1,0:T(8,128)(2,1)}), bf16[4,16,2176]{2,1,0:T(8,128)(2,1)S(1)}, u32[]{:S(2)}, u32[]{:S(2)}) async-start(bf16[4,16,2176]{2,1,0:T(8,128)(2,1)} %bitcast.12), calls=%async_computation.3 | async-start | bytes 557056 | tf_op jit(solution)/shard_map/all_to_all | solution.py:259
  318.2 0.1 copy.14
  318.3 6.7 %all-to-all-done.3 = bf16[4,16,2176]{2,1,0:T(8,128)(2,1)S(1)} async-done(((bf16[4,16,2176]{2,1,0:T(8,128)(2,1)}), bf16[4,16,2176]{2,1,0:T(8,128)(2,1)S(1)}, u32[]{:S(2)}, u32[]{:S(2)}) %all-to-all-start.3) | async-done | bytes 278560 | tf_op jit(solution)/shard_map/all_to_all | solution.py:259
  325.0 0.6 slice.44
  325.7 0.7 copy.15
  (9 shorter events, 0.1 us)
Async XLA Ops:
  7.2 190.6 %copy-start = (bf16[1,2048,768]{2,1,0:T(8,128)(2,1)S(1)}, bf16[1,2048,768]{2,1,0:T(8,128)(2,1)}, u32[]{:S(2)}) copy-start(bf16[1,2048,768]{2,1,0:T(8,128)(2,1)} %param.12) | copy-start | bytes 9437188
  7.2 1.1 copy-start.4
  8.3 0.8 copy-start.5
  9.2 0.7 copy-start.6
  9.9 0.7 copy-start.8
  11.3 1.0 copy-start.2
  12.3 91.2 %all-to-all-start = ((bf16[4,80,1536]{2,1,0:T(8,128)(2,1)}), bf16[4,80,1536]{2,1,0:T(8,128)(2,1)}, u32[]{:S(2)}, u32[]{:S(2)}) async-start(bf16[4,80,1536]{2,1,0:T(8,128)(2,1)} %copy-done.2), calls=%async_computation | async-start | bytes 1966080 | tf_op jit(solution)/shard_map/all_to_all | solution.py:220
  105.4 0.9 copy-start.3
  106.3 87.8 %all-to-all-start.1 = ((bf16[32,8,1536]{2,1,0:T(8,128)(2,1)}), bf16[32,8,1536]{2,1,0:T(8,128)(2,1)}, u32[]{:S(2)}, u32[]{:S(2)}) async-start(bf16[32,8,1536]{2,1,0:T(8,128)(2,1)} %bitcast.29), calls=%async_computation.1 | async-start | bytes 1572864 | tf_op jit(solution)/shard_map/all_to_all | solution.py:227
  123.3 12.2 %collective-permute-start = (bf16[64,2048]{1,0:T(8,128)(2,1)S(1)}, bf16[64,2048]{1,0:T(8,128)(2,1)S(1)}, u32[]{:S(2)}, u32[]{:S(2)}) collective-permute-start(bf16[64,2048]{1,0:T(8,128)(2,1)S(1)} %get-tuple-element.19), channel_id=1, source_target_pairs={{0,2},{2,4},{4,6},{6,0},{1,3},{3,5},{5,7},{7,1},{8,10},{10,12},{12... | collective-permute-start | bytes 786440 | tf_op jit(solution)/shard_map/ppermute | solution.py:236
  127.3 9.8 %collective-permute-start.1 = (bf16[64,2048]{1,0:T(8,128)(2,1)S(1)}, bf16[64,2048]{1,0:T(8,128)(2,1)S(1)}, u32[]{:S(2)}, u32[]{:S(2)}) collective-permute-start(bf16[64,2048]{1,0:T(8,128)(2,1)S(1)} %get-tuple-element.20), channel_id=1, source_target_pairs={{0,4},{2,6},{4,0},{6,2},{1,5},{3,7},{5,1},{7,3},{8,12},{10,14},{12... | collective-permute-start | bytes 786440 | tf_op jit(solution)/shard_map/ppermute | solution.py:236
  131.8 8.3 %collective-permute-start.2 = (bf16[64,2048]{1,0:T(8,128)(2,1)S(1)}, bf16[64,2048]{1,0:T(8,128)(2,1)S(1)}, u32[]{:S(2)}, u32[]{:S(2)}) collective-permute-start(bf16[64,2048]{1,0:T(8,128)(2,1)S(1)} %get-tuple-element.21), channel_id=1, source_target_pairs={{0,6},{2,0},{4,2},{6,4},{1,7},{3,1},{5,3},{7,5},{8,14},{10,8},{12,... | collective-permute-start | bytes 786440 | tf_op jit(solution)/shard_map/ppermute | solution.py:236
  141.3 1.0 copy-start.1
  197.7 2.2 copy-start.9
  203.3 108.3 %all-to-all-start.2 = ((bf16[32,8,2176]{2,1,0:T(8,128)(2,1)}), bf16[32,8,2176]{2,1,0:T(8,128)(2,1)}, u32[]{:S(2)}, u32[]{:S(2)}) async-start(bf16[32,8,2176]{2,1,0:T(8,128)(2,1)} %fusion.14), calls=%async_computation.2 | async-start | bytes 2228224 | tf_op jit(solution)/shard_map/all_to_all | solution.py:253
  208.0 118.4 %reduce-scatter.2.cloned.1.call-start = ((), (), s32[]{:S(2)}) async-start(), calls=%async_computation.5 | async-start | bytes 3538944 | tf_op jit(solution)/shard_map/reduce_scatter | solution.py:250
  212.2 106.0 %copy-start.7 = (f32[16,8]{0,1:T(8,128)S(1)}, f32[16,8]{0,1:T(8,128)}, u32[]{:S(2)}) copy-start(f32[16,8]{0,1:T(8,128)} %param.9) | copy-start | bytes 1540
  314.0 11.0 %all-to-all-start.3 = ((bf16[4,16,2176]{2,1,0:T(8,128)(2,1)}), bf16[4,16,2176]{2,1,0:T(8,128)(2,1)S(1)}, u32[]{:S(2)}, u32[]{:S(2)}) async-start(bf16[4,16,2176]{2,1,0:T(8,128)(2,1)} %bitcast.12), calls=%async_computation.3 | async-start | bytes 557056 | tf_op jit(solution)/shard_map/all_to_all | solution.py:259
Sparse Core Ops, SparseCore 0:
  212.8 51.4 reduce-scatter.1

commit v6 on v5

--- a/solution.py
+++ b/solution.py
@@ -186,6 +186,36 @@
     out_ref[:, width:] = result.astype(bf16)
 
 
+def expert_kernel(rows_ref, pre_ref, gate_ref, up_ref, down_ref, back_ref, hidden_ref):
+    hidden_width = down_ref.shape[0]
+    width = down_ref.shape[1]
+    gate_pre = pre_ref[:, :hidden_width].astype(f32)
+    up_pre = pre_ref[:, hidden_width:].astype(f32)
+    sigmoid_gate = jax.nn.sigmoid(gate_pre)
+    activated = gate_pre * sigmoid_gate
+    hidden = (activated * up_pre).astype(bf16)
+    hidden_ref[...] = hidden
+    hidden_grad = dot(rows_ref[...], down_ref[...], (1, 1))
+    dots = jnp.sum(hidden.astype(f32) * hidden_grad, axis=1, keepdims=True)
+    lanes = iota((rows_ref.shape[0], FACTS), 1)
+    back_ref[:, width:] = jnp.where(lanes == 0, dots, 0.0).astype(bf16)
+    gate_grad = (hidden_grad * up_pre * sigmoid_gate * (1.0 + gate_pre * (1.0 - sigmoid_gate))).astype(bf16)
+    up_grad = (hidden_grad * activated).astype(bf16)
+    route_grad = dot(gate_grad, gate_ref[...], (1, 1)) + dot(up_grad, up_ref[...], (1, 1))
+    back_ref[:, :width] = route_grad.astype(bf16)
+
+
+def finish_kernel(home_ref, gates_ref, tokens_ref, gates_out_ref):
+    width = tokens_ref.shape[1]
+    topk = gates_ref.shape[0]
+    total = home_ref[0].astype(f32)
+    for col in range(1, COLS):
+        total = total + home_ref[col].astype(f32)
+    tokens_ref[...] = total[:, :width].astype(bf16)
+    seat = one_hot(iota((topk, FACTS), 1) == iota((topk, FACTS), 0))
+    gates_out_ref[...] = dot(seat, total[:, width:].astype(bf16), (1, 1)) / gates_ref[...]
+
+
 def call(kernel, outs, inputs, flops):
     scalar = inputs[0].ndim == 1
     in_specs = [pl.BlockSpec(memory_space=pltpu.VMEM) for _ in inputs]
@@ -237,19 +267,11 @@
     outs = [out((SLOTS, width), bf16)]
     (weight_rows,) = call(gather_kernel, outs, (me_y, *came), 2 * SLOTS * SLOTS * width)
 
-    gate_pre = pre_rows[:, :hidden_width].astype(f32)
-    up_pre = pre_rows[:, hidden_width:].astype(f32)
-    sigmoid_gate = jax.nn.sigmoid(gate_pre)
-    activated = gate_pre * sigmoid_gate
-    hidden = (activated * up_pre).astype(bf16)
+    outs = [out((SLOTS, width + FACTS), bf16), out((SLOTS, hidden_width), bf16)]
+    inputs = (weight_rows, pre_rows, w_gate[0], w_up[0], w_down[0])
+    back, hidden = call(expert_kernel, outs, inputs, 6 * SLOTS * hidden_width * width)
     partial = dot(hidden, weight_rows, (0, 0)).astype(bf16)
-    hidden_grad = dot(weight_rows, w_down[0], (1, 1))
-    gate_dots = jnp.sum(hidden.astype(f32) * hidden_grad, axis=1, keepdims=True).astype(bf16)
-    gate_grad = (hidden_grad * up_pre * sigmoid_gate * (1.0 + gate_pre * (1.0 - sigmoid_gate))).astype(bf16)
-    up_grad = (hidden_grad * activated).astype(bf16)
     d_down = lax.psum_scatter(partial, "dp", scatter_dimension=0, tiled=True)
-    route_grad = dot(gate_grad, w_gate[0], (1, 1)) + dot(up_grad, w_up[0], (1, 1))
-    back = jnp.concatenate([route_grad.astype(bf16), jnp.pad(gate_dots, ((0, 0), (0, FACTS - 1)))], axis=1)
     back = lax.all_to_all(back.reshape(RING_SIZE, COLS * CAP, width + FACTS), RING, 0, 0, tiled=True)
     back = back.reshape(SLOTS, width + FACTS)
 
@@ -257,10 +279,9 @@
     home = [out((tokens, width + FACTS), bf16)]
     (home,) = call(join, home, (me_y, back, place, facts), 2 * tokens * SLOTS * width)
     home = lax.all_to_all(home.reshape(COLS, tok, width + FACTS), "y", 0, 0, tiled=True)
-    total = jnp.sum(home.astype(f32), axis=0)
-    d_tokens = total[:, :width].astype(bf16)
-    d_gates = total[:, width : width + topk] / gates
-    return (d_tokens, d_gates, d_down[None])
+    outs = [out((tok, width), bf16), out((topk, tok), f32)]
+    d_tokens, d_gates = call(finish_kernel, outs, (home, gates.T), COLS * tok * width)
+    return (d_tokens, d_gates.T, d_down[None])
 
 
 def solution(mesh):

time: 334 us -> 328 us (0.982)
  matrix products: 12.2 us -> 2.66 us
  blocking collectives: 86.7 us -> 92.9 us
  starting transfers between devices: 38.2 us -> 33.4 us
  Pallas kernels: 8.71 us -> 12.6 us
    all_to_all x0 -> x1, blocking collectives: none -> 11.2 us  [shards(): lax.all_to_all(home.reshape(COLS, tok, width + FACTS), 'y', 0, 0, tiled=T...]
    dot_general x4 -> x1, matrix products: 12.2 us -> 2.66 us  [dot(): return lax.dot_general(left, right, dims, preferred_element_type=f32)]
    all_to_all x1 -> x0, waiting for transfers between devices: 6.69 us -> none  [shards(): lax.all_to_all(home.reshape(COLS, tok, width + FACTS), 'y', 0, 0, tiled=T...]
    all_gather x1, blocking collectives: 86.7 us -> 81.7 us  [shards(): lax.all_gather(own.astype(jnp.float16), RING, axis=0, tiled=True)]
    all_to_all x1 -> x0, starting transfers between devices: 4.24 us -> none  [shards(): lax.all_to_all(home.reshape(COLS, tok, width + FACTS), 'y', 0, 0, tiled=T...]
    pallas_call x5 -> x7, Pallas kernels: 8.71 us -> 12.6 us  [call(): pl.pallas_call(kernel, out_shape=outs, in_specs=in_specs, out_specs=[pl.B...]
    all_to_all x1, waiting for transfers between devices: 99.3 us -> 103 us  [shards(): lax.all_to_all(back.reshape(RING_SIZE, COLS * CAP, width + FACTS), RING,...]
    unnamed x22 -> x16, local copies, waits for them, and re-layouts: 6.91 us -> 8.87 us
  transfers between devices with their start and end apart: 8 -> 7, of which waited for: 5 -> 4; matrix products, arithmetic and copies ran while one was open for 2% -> 1% of each run, Pallas kernels for 2% -> 1%
where the time goes in v6:
time: 328 us; the launch traced here: 327 us
  waiting for transfers between devices  162 us (49%)
  blocking collectives  92.9 us (28%)
  starting transfers between devices  33.4 us (10%)
  between operations  14.1 us (4%)
  Pallas kernels  12.6 us (4%)
  local copies, waits for them, and re-layouts  8.87 us (3%)
    all_to_all x1, waiting for transfers between devices, shards(): lax.all_to_all(back.reshape(RING_SIZE, COLS * CAP, width + FACTS), RING,...  103 us
    all_gather x1, blocking collectives, shards(): lax.all_gather(own.astype(jnp.float16), RING, axis=0, tiled=True)  81.7 us
    all_to_all x1, waiting for transfers between devices, shards(): lax.all_to_all(pre_rows.reshape(RING_SIZE, COLS * CAP, pre_width), RING,...  54.4 us
    all_to_all x1, starting transfers between devices, shards(): lax.all_to_all(pre_rows.reshape(RING_SIZE, COLS * CAP, pre_width), RING,...  13.3 us
    pallas_call x7, Pallas kernels, call(): pl.pallas_call(kernel, out_shape=outs, in_specs=in_specs, out_specs=[pl.B...  12.6 us
    ppermute x3, starting transfers between devices, shards(): lax.ppermute(sent[hop], 'y', [(col, (col + hop) % COLS) for col in range(...  11.7 us
    all_to_all x1, blocking collectives, shards(): lax.all_to_all(home.reshape(COLS, tok, width + FACTS), 'y', 0, 0, tiled=T...  11.2 us
    unnamed x16, local copies, waits for them, and re-layouts  8.87 us
  transfers between devices with their start and end apart: 7, of which 4 were waited for; matrix products, arithmetic and copies ran while one was open for 1% of the time, Pallas kernels for 1%

profile of v6, /device:TPU:6, one launch (start us, length us, event | category | flops | bytes accessed | tf_op | source)
XLA Modules:
  0.0 326.9 jit_solution(18414356481861582461)
XLA Ops:
  7.2 0.0 copy-start.3
  7.2 1.0 copy-done.3
  8.2 0.0 copy-start.4
  8.2 0.8 copy-done.4
  9.0 0.0 copy-start.5
  9.0 0.7 copy-done.5
  9.7 0.0 copy-start.7
  9.7 0.7 copy-done.7
  10.4 1.7 shard_map.94
  12.1 4.5 %all-to-all-start = ((bf16[4,80,1536]{2,1,0:T(8,128)(2,1)}), bf16[4,80,1536]{2,1,0:T(8,128)(2,1)S(1)}, u32[]{:S(2)}, u32[]{:S(2)}) async-start(bf16[4,80,1536]{2,1,0:T(8,128)(2,1)} %get-tuple-element.18), calls=%async_computation | async-start | bytes 1966080 | tf_op jit(solution)/shard_map/all_to_all | solution.py:250
  16.6 81.7 %all-gather.1 = f16[512,2176]{1,0:T(8,128)(2,1)S(1)} all-gather(f16[16,2176]{1,0:T(8,128)(2,1)S(1)} %convert_element_type.9), channel_id=1, replica_groups=mesh['dp'=8,'node'=16,'y'=4,'zh'=2] {'zh','node'}, dimensions={0}, use_global_device_ids=true | all-gather | bytes 2297856 | tf_op jit(solution)/shard_map/all_gather | solution.py:252
  98.3 0.0 all-to-all-done.in_ref
  98.3 1.6 shard_map.95
  99.9 13.3 %all-to-all-start.1 = ((bf16[32,8,1536]{2,1,0:T(8,128)(2,1)}), bf16[32,8,1536]{2,1,0:T(8,128)(2,1)S(1)}, u32[]{:S(2)}, u32[]{:S(2)}) async-start(bf16[32,8,1536]{2,1,0:T(8,128)(2,1)} %bitcast.5), calls=%async_computation.1 | async-start | bytes 1572864 | tf_op jit(solution)/shard_map/all_to_all | solution.py:257
  113.2 0.1 pad_add_fusion.at_ref
  113.2 0.3 convert_element_type.10.in_ref
  113.5 2.4 shard_map.96
  115.9 3.8 %collective-permute-start = (bf16[64,2048]{1,0:T(8,128)(2,1)S(1)}, bf16[64,2048]{1,0:T(8,128)(2,1)S(1)}, u32[]{:S(2)}, u32[]{:S(2)}) collective-permute-start(bf16[64,2048]{1,0:T(8,128)(2,1)S(1)} %get-tuple-element.23), channel_id=1, source_target_pairs={{0,2},{2,4},{4,6},{6,0},{1,3},{3,5},{5,7},{7,1},{8,10},{10,12},{12... | collective-permute-start | bytes 786440 | tf_op jit(solution)/shard_map/ppermute | solution.py:266
  119.8 4.4 %collective-permute-start.1 = (bf16[64,2048]{1,0:T(8,128)(2,1)S(1)}, bf16[64,2048]{1,0:T(8,128)(2,1)S(1)}, u32[]{:S(2)}, u32[]{:S(2)}) collective-permute-start(bf16[64,2048]{1,0:T(8,128)(2,1)S(1)} %get-tuple-element.24), channel_id=1, source_target_pairs={{0,4},{2,6},{4,0},{6,2},{1,5},{3,7},{5,1},{7,3},{8,12},{10,14},{12... | collective-permute-start | bytes 786440 | tf_op jit(solution)/shard_map/ppermute | solution.py:266
  124.2 3.4 %collective-permute-start.2 = (bf16[64,2048]{1,0:T(8,128)(2,1)S(1)}, bf16[64,2048]{1,0:T(8,128)(2,1)S(1)}, u32[]{:S(2)}, u32[]{:S(2)}) collective-permute-start(bf16[64,2048]{1,0:T(8,128)(2,1)S(1)} %get-tuple-element.25), channel_id=1, source_target_pairs={{0,6},{2,0},{4,2},{6,4},{1,7},{3,1},{5,3},{7,5},{8,14},{10,8},{12,... | collective-permute-start | bytes 786440 | tf_op jit(solution)/shard_map/ppermute | solution.py:266
  127.6 0.0 collective-permute-done.refs_1_
  127.6 1.9 collective-permute-done.1.refs_2_
  129.5 2.9 collective-permute-done.2.refs_3_
  132.5 1.2 shard_map.97.rows_ref
  133.7 54.4 %all-to-all-done.1 = bf16[32,8,1536]{2,1,0:T(8,128)(2,1)S(1)} async-done(((bf16[32,8,1536]{2,1,0:T(8,128)(2,1)}), bf16[32,8,1536]{2,1,0:T(8,128)(2,1)S(1)}, u32[]{:S(2)}, u32[]{:S(2)}) %all-to-all-start.1) | async-done | bytes 786464 | tf_op jit(solution)/shard_map/all_to_all | solution.py:257
  188.1 0.0 copy-start
  188.1 1.9 copy-done
  189.9 0.0 copy-start.1
  190.0 1.9 copy-done.1
  191.8 0.0 copy-start.2
  191.8 1.9 copy-done.2
  193.7 4.5 %shard_map.98 = (bf16[256,2176]{1,0:T(8,128)(2,1)}, bf16[256,768]{1,0:T(8,128)(2,1)S(1)}) custom-call(bf16[256,2048]{1,0:T(8,128)(2,1)S(1)} %shard_map.97.rows_ref, bf16[256,1536]{1,0:T(8,128)(2,1)S(1)} %bitcast.21, bf16[2048,768]{1,0:T(8,128)(2,1)S(1)} %bitcast.18, bf16[2048,768]{1,0:T(8,128)(2,1)S(1)} %bitcast.19, bf16[768,2048]{1,0:T(8,128)(2,1)S(1)} %bitcast.20), custom_call_target="tpu_custom_call" | custom-call | flops 2415919104 | bytes 12779520 | tf_op jit(solution)/shard_map/pallas_call | solution.py:225
  198.2 3.9 %all-to-all-start.2 = ((bf16[32,8,2176]{2,1,0:T(8,128)(2,1)}), bf16[32,8,2176]{2,1,0:T(8,128)(2,1)S(1)}, u32[]{:S(2)}, u32[]{:S(2)}) async-start(bf16[32,8,2176]{2,1,0:T(8,128)(2,1)} %bitcast.10), calls=%async_computation.2 | async-start | bytes 2228224 | tf_op jit(solution)/shard_map/all_to_all | solution.py:275
  202.2 0.0 reduce-scatter.2.cloned.1.call-start
  202.2 2.7 convolution_convert_fusion
  204.9 0.0 copy-start.6
  204.9 0.0 reduce-scatter.2.cloned.1.call-update
  204.9 102.7 %all-to-all-done.2 = bf16[32,8,2176]{2,1,0:T(8,128)(2,1)S(1)} async-done(((bf16[32,8,2176]{2,1,0:T(8,128)(2,1)}), bf16[32,8,2176]{2,1,0:T(8,128)(2,1)S(1)}, u32[]{:S(2)}, u32[]{:S(2)}) %all-to-all-start.2) | async-done | bytes 1114144 | tf_op jit(solution)/shard_map/all_to_all | solution.py:275
  307.6 0.4 shard_map.99
  308.1 11.2 %all_to_all.20.home_ref = bf16[4,16,2176]{2,1,0:T(8,128)(2,1)S(1)} all-to-all(bf16[4,16,2176]{2,1,0:T(8,128)(2,1)S(1)} %bitcast.22), channel_id=1, replica_groups=mesh['dp'=8,'node'=16,'y'=4,'zh'=2] {'y'}, dimensions={0} | all-to-all | bytes 557056 | tf_op jit(solution)/shard_map/all_to_all | solution.py:281
  319.3 0.0 copy-done.6
  319.3 0.7 shard_map.100
  320.0 0.0 reduce-scatter.2.cloned.1.call-done
  (1 shorter events, 0.0 us)
Async XLA Ops:
  7.2 1.0 copy-start.3
  8.2 0.8 copy-start.4
  9.0 0.7 copy-start.5
  9.7 0.7 copy-start.7
  12.1 86.2 %all-to-all-start = ((bf16[4,80,1536]{2,1,0:T(8,128)(2,1)}), bf16[4,80,1536]{2,1,0:T(8,128)(2,1)S(1)}, u32[]{:S(2)}, u32[]{:S(2)}) async-start(bf16[4,80,1536]{2,1,0:T(8,128)(2,1)} %get-tuple-element.18), calls=%async_computation | async-start | bytes 1966080 | tf_op jit(solution)/shard_map/all_to_all | solution.py:250
  99.9 88.2 %all-to-all-start.1 = ((bf16[32,8,1536]{2,1,0:T(8,128)(2,1)}), bf16[32,8,1536]{2,1,0:T(8,128)(2,1)S(1)}, u32[]{:S(2)}, u32[]{:S(2)}) async-start(bf16[32,8,1536]{2,1,0:T(8,128)(2,1)} %bitcast.5), calls=%async_computation.1 | async-start | bytes 1572864 | tf_op jit(solution)/shard_map/all_to_all | solution.py:257
  115.9 11.7 %collective-permute-start = (bf16[64,2048]{1,0:T(8,128)(2,1)S(1)}, bf16[64,2048]{1,0:T(8,128)(2,1)S(1)}, u32[]{:S(2)}, u32[]{:S(2)}) collective-permute-start(bf16[64,2048]{1,0:T(8,128)(2,1)S(1)} %get-tuple-element.23), channel_id=1, source_target_pairs={{0,2},{2,4},{4,6},{6,0},{1,3},{3,5},{5,7},{7,1},{8,10},{10,12},{12... | collective-permute-start | bytes 786440 | tf_op jit(solution)/shard_map/ppermute | solution.py:266
  119.8 9.8 %collective-permute-start.1 = (bf16[64,2048]{1,0:T(8,128)(2,1)S(1)}, bf16[64,2048]{1,0:T(8,128)(2,1)S(1)}, u32[]{:S(2)}, u32[]{:S(2)}) collective-permute-start(bf16[64,2048]{1,0:T(8,128)(2,1)S(1)} %get-tuple-element.24), channel_id=1, source_target_pairs={{0,4},{2,6},{4,0},{6,2},{1,5},{3,7},{5,1},{7,3},{8,12},{10,14},{12... | collective-permute-start | bytes 786440 | tf_op jit(solution)/shard_map/ppermute | solution.py:266
  124.2 8.3 %collective-permute-start.2 = (bf16[64,2048]{1,0:T(8,128)(2,1)S(1)}, bf16[64,2048]{1,0:T(8,128)(2,1)S(1)}, u32[]{:S(2)}, u32[]{:S(2)}) collective-permute-start(bf16[64,2048]{1,0:T(8,128)(2,1)S(1)} %get-tuple-element.25), channel_id=1, source_target_pairs={{0,6},{2,0},{4,2},{6,4},{1,7},{3,1},{5,3},{7,5},{8,14},{10,8},{12,... | collective-permute-start | bytes 786440 | tf_op jit(solution)/shard_map/ppermute | solution.py:266
  188.1 1.9 copy-start
  189.9 1.9 copy-start.1
  191.8 1.9 copy-start.2
  198.2 109.4 %all-to-all-start.2 = ((bf16[32,8,2176]{2,1,0:T(8,128)(2,1)}), bf16[32,8,2176]{2,1,0:T(8,128)(2,1)S(1)}, u32[]{:S(2)}, u32[]{:S(2)}) async-start(bf16[32,8,2176]{2,1,0:T(8,128)(2,1)} %bitcast.10), calls=%async_computation.2 | async-start | bytes 2228224 | tf_op jit(solution)/shard_map/all_to_all | solution.py:275
  202.2 117.8 %reduce-scatter.2.cloned.1.call-start = ((), (), s32[]{:S(2)}) async-start(), calls=%async_computation.5 | async-start | bytes 3538944 | tf_op jit(solution)/shard_map/reduce_scatter | solution.py:274
  204.9 114.4 %copy-start.6 = (f32[16,8]{0,1:T(8,128)S(1)}, f32[16,8]{0,1:T(8,128)}, u32[]{:S(2)}) copy-start(f32[16,8]{0,1:T(8,128)} %param.9) | copy-start | bytes 1540
Sparse Core Ops, SparseCore 0:
  207.0 50.6 reduce-scatter.1

commit v7 on v6

--- a/solution.py
+++ b/solution.py
@@ -17,7 +17,7 @@
 RAISES = (64, 32, 8, 4, 2, 1)
 MIDDLE = 2.0**14
 LOW = 2.0**20
-VMEM_BYTES = 24 * 1024 * 1024
+VMEM_BYTES = 32 * 1024 * 1024
 f32, bf16, i32 = jnp.float32, jnp.bfloat16, jnp.int32
 
 
@@ -186,7 +186,11 @@
     out_ref[:, width:] = result.astype(bf16)
 
 
-def expert_kernel(rows_ref, pre_ref, gate_ref, up_ref, down_ref, back_ref, hidden_ref):
+def expert_kernel(rows_ref, pre_ref, gate_hbm, up_hbm, down_hbm, back_ref, hidden_ref, gate_ref, up_ref, down_ref, sems):
+    moves = []
+    for at, (source, target) in enumerate(((down_hbm, down_ref), (gate_hbm, gate_ref), (up_hbm, up_ref))):
+        moves.append(pltpu.make_async_copy(source, target, sems.at[at]))
+        moves[at].start()
     hidden_width = down_ref.shape[0]
     width = down_ref.shape[1]
     gate_pre = pre_ref[:, :hidden_width].astype(f32)
@@ -195,13 +199,17 @@
     activated = gate_pre * sigmoid_gate
     hidden = (activated * up_pre).astype(bf16)
     hidden_ref[...] = hidden
+    moves[0].wait()
     hidden_grad = dot(rows_ref[...], down_ref[...], (1, 1))
     dots = jnp.sum(hidden.astype(f32) * hidden_grad, axis=1, keepdims=True)
     lanes = iota((rows_ref.shape[0], FACTS), 1)
     back_ref[:, width:] = jnp.where(lanes == 0, dots, 0.0).astype(bf16)
     gate_grad = (hidden_grad * up_pre * sigmoid_gate * (1.0 + gate_pre * (1.0 - sigmoid_gate))).astype(bf16)
     up_grad = (hidden_grad * activated).astype(bf16)
-    route_grad = dot(gate_grad, gate_ref[...], (1, 1)) + dot(up_grad, up_ref[...], (1, 1))
+    moves[1].wait()
+    route_grad = dot(gate_grad, gate_ref[...], (1, 1))
+    moves[2].wait()
+    route_grad = route_grad + dot(up_grad, up_ref[...], (1, 1))
     back_ref[:, :width] = route_grad.astype(bf16)
 
 
@@ -216,17 +224,20 @@
     gates_out_ref[...] = dot(seat, total[:, width:].astype(bf16), (1, 1)) / gates_ref[...]
 
 
-def call(kernel, outs, inputs, flops):
+def call(kernel, outs, inputs, flops, far=0, scratch=()):
     scalar = inputs[0].ndim == 1
     in_specs = [pl.BlockSpec(memory_space=pltpu.VMEM) for _ in inputs]
     if scalar:
         in_specs[0] = pl.BlockSpec(memory_space=pltpu.SMEM)
+    for at in range(len(inputs) - far, len(inputs)):
+        in_specs[at] = pl.BlockSpec(memory_space=pl.ANY)
     moved = sum(a.size * a.dtype.itemsize for a in inputs) + sum(a.size * a.dtype.itemsize for a in outs)
     return pl.pallas_call(
         kernel,
         out_shape=outs,
         in_specs=in_specs,
         out_specs=[pl.BlockSpec(memory_space=pltpu.VMEM) for _ in outs],
+        scratch_shapes=list(scratch),
         compiler_params=pltpu.CompilerParams(vmem_limit_bytes=VMEM_BYTES),
         cost_estimate=pl.CostEstimate(flops=flops, bytes_accessed=moved, transcendentals=0),
     )(*inputs)
@@ -269,7 +280,8 @@
 
     outs = [out((SLOTS, width + FACTS), bf16), out((SLOTS, hidden_width), bf16)]
     inputs = (weight_rows, pre_rows, w_gate[0], w_up[0], w_down[0])
-    back, hidden = call(expert_kernel, outs, inputs, 6 * SLOTS * hidden_width * width)
+    scratch = [pltpu.VMEM(w.shape, bf16) for w in inputs[2:]] + [pltpu.SemaphoreType.DMA((3,))]
+    back, hidden = call(expert_kernel, outs, inputs, 6 * SLOTS * hidden_width * width, 3, scratch)
     partial = dot(hidden, weight_rows, (0, 0)).astype(bf16)
     d_down = lax.psum_scatter(partial, "dp", scatter_dimension=0, tiled=True)
     back = lax.all_to_all(back.reshape(RING_SIZE, COLS * CAP, width + FACTS), RING, 0, 0, tiled=True)

time: 328 us -> 329 us (level)
  no operation moved by 1% of the time
where the time goes in v7:
time: 329 us; the launch traced here: 328 us
  waiting for transfers between devices  162 us (49%)
  blocking collectives  92.9 us (28%)
  starting transfers between devices  33.4 us (10%)
  between operations  14.1 us (4%)
  Pallas kernels  14 us (4%)
  local copies, waits for them, and re-layouts  8.87 us (3%)
    all_to_all x1, waiting for transfers between devices, shards(): lax.all_to_all(back.reshape(RING_SIZE, COLS * CAP, width + FACTS), RING,...  103 us
    all_gather x1, blocking collectives, shards(): lax.all_gather(own.astype(jnp.float16), RING, axis=0, tiled=True)  81.7 us
    all_to_all x1, waiting for transfers between devices, shards(): lax.all_to_all(pre_rows.reshape(RING_SIZE, COLS * CAP, pre_width), RING,...  54.4 us
    pallas_call x7, Pallas kernels, call(): pl.pallas_call(kernel, out_shape=outs, in_specs=in_specs, out_specs=[pl.B...  14 us
    all_to_all x1, starting transfers between devices, shards(): lax.all_to_all(pre_rows.reshape(RING_SIZE, COLS * CAP, pre_width), RING,...  13.3 us
    ppermute x3, starting transfers between devices, shards(): lax.ppermute(sent[hop], 'y', [(col, (col + hop) % COLS) for col in range(...  11.7 us
    all_to_all x1, blocking collectives, shards(): lax.all_to_all(home.reshape(COLS, tok, width + FACTS), 'y', 0, 0, tiled=T...  11.2 us
    unnamed x16, local copies, waits for them, and re-layouts  8.87 us
  transfers between devices with their start and end apart: 7, of which 4 were waited for; matrix products, arithmetic and copies ran while one was open for 1% of the time, Pallas kernels for 1%

profile of v7, /device:TPU:6, one launch (start us, length us, event | category | flops | bytes accessed | tf_op | source)
XLA Modules:
  0.0 328.3 jit_solution(1533330010144976313)
XLA Ops:
  7.2 0.0 copy-start.3
  7.2 1.0 copy-done.3
  8.2 0.0 copy-start.4
  8.2 0.8 copy-done.4
  9.0 0.0 copy-start.5
  9.0 0.7 copy-done.5
  9.7 0.0 copy-start.7
  9.7 0.7 copy-done.7
  10.4 1.7 shard_map.94
  12.1 4.5 %all-to-all-start = ((bf16[4,80,1536]{2,1,0:T(8,128)(2,1)}), bf16[4,80,1536]{2,1,0:T(8,128)(2,1)S(1)}, u32[]{:S(2)}, u32[]{:S(2)}) async-start(bf16[4,80,1536]{2,1,0:T(8,128)(2,1)} %get-tuple-element.18), calls=%async_computation | async-start | bytes 1966080 | tf_op jit(solution)/shard_map/all_to_all | solution.py:261
  16.6 81.7 %all-gather.1 = f16[512,2176]{1,0:T(8,128)(2,1)S(1)} all-gather(f16[16,2176]{1,0:T(8,128)(2,1)S(1)} %convert_element_type.9), channel_id=1, replica_groups=mesh['dp'=8,'node'=16,'y'=4,'zh'=2] {'zh','node'}, dimensions={0}, use_global_device_ids=true | all-gather | bytes 2297856 | tf_op jit(solution)/shard_map/all_gather | solution.py:263
  98.3 0.0 all-to-all-done.in_ref
  98.3 1.6 shard_map.95
  99.9 13.3 %all-to-all-start.1 = ((bf16[32,8,1536]{2,1,0:T(8,128)(2,1)}), bf16[32,8,1536]{2,1,0:T(8,128)(2,1)S(1)}, u32[]{:S(2)}, u32[]{:S(2)}) async-start(bf16[32,8,1536]{2,1,0:T(8,128)(2,1)} %bitcast.5), calls=%async_computation.1 | async-start | bytes 1572864 | tf_op jit(solution)/shard_map/all_to_all | solution.py:268
  113.2 0.1 pad_add_fusion.at_ref
  113.2 0.3 convert_element_type.10.in_ref
  113.5 2.4 shard_map.96
  115.9 3.8 %collective-permute-start = (bf16[64,2048]{1,0:T(8,128)(2,1)S(1)}, bf16[64,2048]{1,0:T(8,128)(2,1)S(1)}, u32[]{:S(2)}, u32[]{:S(2)}) collective-permute-start(bf16[64,2048]{1,0:T(8,128)(2,1)S(1)} %get-tuple-element.23), channel_id=1, source_target_pairs={{0,2},{2,4},{4,6},{6,0},{1,3},{3,5},{5,7},{7,1},{8,10},{10,12},{12... | collective-permute-start | bytes 786440 | tf_op jit(solution)/shard_map/ppermute | solution.py:277
  119.8 4.4 %collective-permute-start.1 = (bf16[64,2048]{1,0:T(8,128)(2,1)S(1)}, bf16[64,2048]{1,0:T(8,128)(2,1)S(1)}, u32[]{:S(2)}, u32[]{:S(2)}) collective-permute-start(bf16[64,2048]{1,0:T(8,128)(2,1)S(1)} %get-tuple-element.24), channel_id=1, source_target_pairs={{0,4},{2,6},{4,0},{6,2},{1,5},{3,7},{5,1},{7,3},{8,12},{10,14},{12... | collective-permute-start | bytes 786440 | tf_op jit(solution)/shard_map/ppermute | solution.py:277
  124.2 3.4 %collective-permute-start.2 = (bf16[64,2048]{1,0:T(8,128)(2,1)S(1)}, bf16[64,2048]{1,0:T(8,128)(2,1)S(1)}, u32[]{:S(2)}, u32[]{:S(2)}) collective-permute-start(bf16[64,2048]{1,0:T(8,128)(2,1)S(1)} %get-tuple-element.25), channel_id=1, source_target_pairs={{0,6},{2,0},{4,2},{6,4},{1,7},{3,1},{5,3},{7,5},{8,14},{10,8},{12,... | collective-permute-start | bytes 786440 | tf_op jit(solution)/shard_map/ppermute | solution.py:277
  127.6 0.0 collective-permute-done.refs_1_
  127.6 1.9 collective-permute-done.1.refs_2_
  129.5 2.9 collective-permute-done.2.refs_3_
  132.5 1.2 shard_map.97.rows_ref
  133.7 54.4 %all-to-all-done.1 = bf16[32,8,1536]{2,1,0:T(8,128)(2,1)S(1)} async-done(((bf16[32,8,1536]{2,1,0:T(8,128)(2,1)}), bf16[32,8,1536]{2,1,0:T(8,128)(2,1)S(1)}, u32[]{:S(2)}, u32[]{:S(2)}) %all-to-all-start.1) | async-done | bytes 786464 | tf_op jit(solution)/shard_map/all_to_all | solution.py:268
  188.1 0.0 copy-start
  188.1 1.9 copy-done
  189.9 0.0 copy-start.1
  190.0 1.9 copy-done.1
  191.8 0.0 copy-start.2
  191.8 1.9 copy-done.2
  193.7 5.9 %shard_map.98 = (bf16[256,2176]{1,0:T(8,128)(2,1)}, bf16[256,768]{1,0:T(8,128)(2,1)S(1)}) custom-call(bf16[256,2048]{1,0:T(8,128)(2,1)S(1)} %shard_map.97.rows_ref, bf16[256,1536]{1,0:T(8,128)(2,1)S(1)} %bitcast.21, bf16[2048,768]{1,0:T(8,128)(2,1)S(1)} %bitcast.18, bf16[2048,768]{1,0:T(8,128)(2,1)S(1)} %bitcast.19, bf16[768,2048]{1,0:T(8,128)(2,1)S(1)} %bitcast.20), custom_call_target="tpu_custom_call" | custom-call | flops 2415919104 | bytes 12779520 | tf_op jit(solution)/shard_map/pallas_call | solution.py:235
  199.6 3.9 %all-to-all-start.2 = ((bf16[32,8,2176]{2,1,0:T(8,128)(2,1)}), bf16[32,8,2176]{2,1,0:T(8,128)(2,1)S(1)}, u32[]{:S(2)}, u32[]{:S(2)}) async-start(bf16[32,8,2176]{2,1,0:T(8,128)(2,1)} %bitcast.10), calls=%async_computation.2 | async-start | bytes 2228224 | tf_op jit(solution)/shard_map/all_to_all | solution.py:287
  203.6 0.0 reduce-scatter.2.cloned.1.call-start
  203.6 2.7 convolution_convert_fusion
  206.3 0.0 copy-start.6
  206.3 0.0 reduce-scatter.2.cloned.1.call-update
  206.3 102.7 %all-to-all-done.2 = bf16[32,8,2176]{2,1,0:T(8,128)(2,1)S(1)} async-done(((bf16[32,8,2176]{2,1,0:T(8,128)(2,1)}), bf16[32,8,2176]{2,1,0:T(8,128)(2,1)S(1)}, u32[]{:S(2)}, u32[]{:S(2)}) %all-to-all-start.2) | async-done | bytes 1114144 | tf_op jit(solution)/shard_map/all_to_all | solution.py:287
  309.0 0.4 shard_map.99
  309.5 11.2 %all_to_all.20.home_ref = bf16[4,16,2176]{2,1,0:T(8,128)(2,1)S(1)} all-to-all(bf16[4,16,2176]{2,1,0:T(8,128)(2,1)S(1)} %bitcast.22), channel_id=1, replica_groups=mesh['dp'=8,'node'=16,'y'=4,'zh'=2] {'y'}, dimensions={0} | all-to-all | bytes 557056 | tf_op jit(solution)/shard_map/all_to_all | solution.py:293
  320.7 0.0 copy-done.6
  320.7 0.7 shard_map.100
  321.4 0.0 reduce-scatter.2.cloned.1.call-done
  (1 shorter events, 0.0 us)
Async XLA Ops:
  7.2 1.0 copy-start.3
  8.2 0.8 copy-start.4
  9.0 0.7 copy-start.5
  9.7 0.7 copy-start.7
  12.1 86.2 %all-to-all-start = ((bf16[4,80,1536]{2,1,0:T(8,128)(2,1)}), bf16[4,80,1536]{2,1,0:T(8,128)(2,1)S(1)}, u32[]{:S(2)}, u32[]{:S(2)}) async-start(bf16[4,80,1536]{2,1,0:T(8,128)(2,1)} %get-tuple-element.18), calls=%async_computation | async-start | bytes 1966080 | tf_op jit(solution)/shard_map/all_to_all | solution.py:261
  99.9 88.2 %all-to-all-start.1 = ((bf16[32,8,1536]{2,1,0:T(8,128)(2,1)}), bf16[32,8,1536]{2,1,0:T(8,128)(2,1)S(1)}, u32[]{:S(2)}, u32[]{:S(2)}) async-start(bf16[32,8,1536]{2,1,0:T(8,128)(2,1)} %bitcast.5), calls=%async_computation.1 | async-start | bytes 1572864 | tf_op jit(solution)/shard_map/all_to_all | solution.py:268
  115.9 11.7 %collective-permute-start = (bf16[64,2048]{1,0:T(8,128)(2,1)S(1)}, bf16[64,2048]{1,0:T(8,128)(2,1)S(1)}, u32[]{:S(2)}, u32[]{:S(2)}) collective-permute-start(bf16[64,2048]{1,0:T(8,128)(2,1)S(1)} %get-tuple-element.23), channel_id=1, source_target_pairs={{0,2},{2,4},{4,6},{6,0},{1,3},{3,5},{5,7},{7,1},{8,10},{10,12},{12... | collective-permute-start | bytes 786440 | tf_op jit(solution)/shard_map/ppermute | solution.py:277
  119.8 9.8 %collective-permute-start.1 = (bf16[64,2048]{1,0:T(8,128)(2,1)S(1)}, bf16[64,2048]{1,0:T(8,128)(2,1)S(1)}, u32[]{:S(2)}, u32[]{:S(2)}) collective-permute-start(bf16[64,2048]{1,0:T(8,128)(2,1)S(1)} %get-tuple-element.24), channel_id=1, source_target_pairs={{0,4},{2,6},{4,0},{6,2},{1,5},{3,7},{5,1},{7,3},{8,12},{10,14},{12... | collective-permute-start | bytes 786440 | tf_op jit(solution)/shard_map/ppermute | solution.py:277
  124.2 8.3 %collective-permute-start.2 = (bf16[64,2048]{1,0:T(8,128)(2,1)S(1)}, bf16[64,2048]{1,0:T(8,128)(2,1)S(1)}, u32[]{:S(2)}, u32[]{:S(2)}) collective-permute-start(bf16[64,2048]{1,0:T(8,128)(2,1)S(1)} %get-tuple-element.25), channel_id=1, source_target_pairs={{0,6},{2,0},{4,2},{6,4},{1,7},{3,1},{5,3},{7,5},{8,14},{10,8},{12,... | collective-permute-start | bytes 786440 | tf_op jit(solution)/shard_map/ppermute | solution.py:277
  188.1 1.9 copy-start
  189.9 1.9 copy-start.1
  191.8 1.9 copy-start.2
  199.6 109.4 %all-to-all-start.2 = ((bf16[32,8,2176]{2,1,0:T(8,128)(2,1)}), bf16[32,8,2176]{2,1,0:T(8,128)(2,1)S(1)}, u32[]{:S(2)}, u32[]{:S(2)}) async-start(bf16[32,8,2176]{2,1,0:T(8,128)(2,1)} %bitcast.10), calls=%async_computation.2 | async-start | bytes 2228224 | tf_op jit(solution)/shard_map/all_to_all | solution.py:287
  203.6 117.8 %reduce-scatter.2.cloned.1.call-start = ((), (), s32[]{:S(2)}) async-start(), calls=%async_computation.5 | async-start | bytes 3538944 | tf_op jit(solution)/shard_map/reduce_scatter | solution.py:286
  206.3 114.4 %copy-start.6 = (f32[16,8]{0,1:T(8,128)S(1)}, f32[16,8]{0,1:T(8,128)}, u32[]{:S(2)}) copy-start(f32[16,8]{0,1:T(8,128)} %param.9) | copy-start | bytes 1540
Sparse Core Ops, SparseCore 0:
  208.4 50.5 reduce-scatter.1

commit v8 on v7

--- a/solution.py
+++ b/solution.py
@@ -230,7 +230,7 @@
     if scalar:
         in_specs[0] = pl.BlockSpec(memory_space=pltpu.SMEM)
     for at in range(len(inputs) - far, len(inputs)):
-        in_specs[at] = pl.BlockSpec(memory_space=pl.ANY)
+        in_specs[at] = pl.BlockSpec(memory_space=pltpu.HBM)
     moved = sum(a.size * a.dtype.itemsize for a in inputs) + sum(a.size * a.dtype.itemsize for a in outs)
     return pl.pallas_call(
         kernel,

time: 329 us -> 329 us (level)
  no operation moved by 1% of the time
where the time goes in v8:
time: 329 us; the launch traced here: 328 us
  waiting for transfers between devices  162 us (49%)
  blocking collectives  92.9 us (28%)
  starting transfers between devices  33.4 us (10%)
  between operations  14.1 us (4%)
  Pallas kernels  14 us (4%)
  local copies, waits for them, and re-layouts  8.87 us (3%)
    all_to_all x1, waiting for transfers between devices, shards(): lax.all_to_all(back.reshape(RING_SIZE, COLS * CAP, width + FACTS), RING,...  103 us
    all_gather x1, blocking collectives, shards(): lax.all_gather(own.astype(jnp.float16), RING, axis=0, tiled=True)  81.7 us
    all_to_all x1, waiting for transfers between devices, shards(): lax.all_to_all(pre_rows.reshape(RING_SIZE, COLS * CAP, pre_width), RING,...  54.4 us
    pallas_call x7, Pallas kernels, call(): pl.pallas_call(kernel, out_shape=outs, in_specs=in_specs, out_specs=[pl.B...  14 us
    all_to_all x1, starting transfers between devices, shards(): lax.all_to_all(pre_rows.reshape(RING_SIZE, COLS * CAP, pre_width), RING,...  13.3 us
    ppermute x3, starting transfers between devices, shards(): lax.ppermute(sent[hop], 'y', [(col, (col + hop) % COLS) for col in range(...  11.7 us
    all_to_all x1, blocking collectives, shards(): lax.all_to_all(home.reshape(COLS, tok, width + FACTS), 'y', 0, 0, tiled=T...  11.2 us
    unnamed x16, local copies, waits for them, and re-layouts  8.87 us
  transfers between devices with their start and end apart: 7, of which 4 were waited for; matrix products, arithmetic and copies ran while one was open for 1% of the time, Pallas kernels for 1%

profile of v8, /device:TPU:6, one launch (start us, length us, event | category | flops | bytes accessed | tf_op | source)
XLA Modules:
  0.0 328.3 jit_solution(1533330010144976313)
XLA Ops:
  7.2 0.0 copy-start.3
  7.2 1.0 copy-done.3
  8.2 0.0 copy-start.4
  8.2 0.8 copy-done.4
  9.0 0.0 copy-start.5
  9.0 0.7 copy-done.5
  9.7 0.0 copy-start.7
  9.7 0.7 copy-done.7
  10.4 1.7 shard_map.94
  12.1 4.5 %all-to-all-start = ((bf16[4,80,1536]{2,1,0:T(8,128)(2,1)}), bf16[4,80,1536]{2,1,0:T(8,128)(2,1)S(1)}, u32[]{:S(2)}, u32[]{:S(2)}) async-start(bf16[4,80,1536]{2,1,0:T(8,128)(2,1)} %get-tuple-element.18), calls=%async_computation | async-start | bytes 1966080 | tf_op jit(solution)/shard_map/all_to_all | solution.py:261
  16.6 81.7 %all-gather.1 = f16[512,2176]{1,0:T(8,128)(2,1)S(1)} all-gather(f16[16,2176]{1,0:T(8,128)(2,1)S(1)} %convert_element_type.9), channel_id=1, replica_groups=mesh['dp'=8,'node'=16,'y'=4,'zh'=2] {'zh','node'}, dimensions={0}, use_global_device_ids=true | all-gather | bytes 2297856 | tf_op jit(solution)/shard_map/all_gather | solution.py:263
  98.3 0.0 all-to-all-done.in_ref
  98.3 1.6 shard_map.95
  99.9 13.3 %all-to-all-start.1 = ((bf16[32,8,1536]{2,1,0:T(8,128)(2,1)}), bf16[32,8,1536]{2,1,0:T(8,128)(2,1)S(1)}, u32[]{:S(2)}, u32[]{:S(2)}) async-start(bf16[32,8,1536]{2,1,0:T(8,128)(2,1)} %bitcast.5), calls=%async_computation.1 | async-start | bytes 1572864 | tf_op jit(solution)/shard_map/all_to_all | solution.py:268
  113.2 0.1 pad_add_fusion.at_ref
  113.2 0.3 convert_element_type.10.in_ref
  113.5 2.4 shard_map.96
  115.9 3.8 %collective-permute-start = (bf16[64,2048]{1,0:T(8,128)(2,1)S(1)}, bf16[64,2048]{1,0:T(8,128)(2,1)S(1)}, u32[]{:S(2)}, u32[]{:S(2)}) collective-permute-start(bf16[64,2048]{1,0:T(8,128)(2,1)S(1)} %get-tuple-element.23), channel_id=1, source_target_pairs={{0,2},{2,4},{4,6},{6,0},{1,3},{3,5},{5,7},{7,1},{8,10},{10,12},{12... | collective-permute-start | bytes 786440 | tf_op jit(solution)/shard_map/ppermute | solution.py:277
  119.8 4.4 %collective-permute-start.1 = (bf16[64,2048]{1,0:T(8,128)(2,1)S(1)}, bf16[64,2048]{1,0:T(8,128)(2,1)S(1)}, u32[]{:S(2)}, u32[]{:S(2)}) collective-permute-start(bf16[64,2048]{1,0:T(8,128)(2,1)S(1)} %get-tuple-element.24), channel_id=1, source_target_pairs={{0,4},{2,6},{4,0},{6,2},{1,5},{3,7},{5,1},{7,3},{8,12},{10,14},{12... | collective-permute-start | bytes 786440 | tf_op jit(solution)/shard_map/ppermute | solution.py:277
  124.2 3.4 %collective-permute-start.2 = (bf16[64,2048]{1,0:T(8,128)(2,1)S(1)}, bf16[64,2048]{1,0:T(8,128)(2,1)S(1)}, u32[]{:S(2)}, u32[]{:S(2)}) collective-permute-start(bf16[64,2048]{1,0:T(8,128)(2,1)S(1)} %get-tuple-element.25), channel_id=1, source_target_pairs={{0,6},{2,0},{4,2},{6,4},{1,7},{3,1},{5,3},{7,5},{8,14},{10,8},{12,... | collective-permute-start | bytes 786440 | tf_op jit(solution)/shard_map/ppermute | solution.py:277
  127.6 0.0 collective-permute-done.refs_1_
  127.6 1.9 collective-permute-done.1.refs_2_
  129.5 2.9 collective-permute-done.2.refs_3_
  132.5 1.2 shard_map.97.rows_ref
  133.7 54.4 %all-to-all-done.1 = bf16[32,8,1536]{2,1,0:T(8,128)(2,1)S(1)} async-done(((bf16[32,8,1536]{2,1,0:T(8,128)(2,1)}), bf16[32,8,1536]{2,1,0:T(8,128)(2,1)S(1)}, u32[]{:S(2)}, u32[]{:S(2)}) %all-to-all-start.1) | async-done | bytes 786464 | tf_op jit(solution)/shard_map/all_to_all | solution.py:268
  188.1 0.0 copy-start
  188.1 1.9 copy-done
  189.9 0.0 copy-start.1
  190.0 1.9 copy-done.1
  191.8 0.0 copy-start.2
  191.8 1.9 copy-done.2
  193.7 5.9 %shard_map.98 = (bf16[256,2176]{1,0:T(8,128)(2,1)}, bf16[256,768]{1,0:T(8,128)(2,1)S(1)}) custom-call(bf16[256,2048]{1,0:T(8,128)(2,1)S(1)} %shard_map.97.rows_ref, bf16[256,1536]{1,0:T(8,128)(2,1)S(1)} %bitcast.21, bf16[2048,768]{1,0:T(8,128)(2,1)S(1)} %bitcast.18, bf16[2048,768]{1,0:T(8,128)(2,1)S(1)} %bitcast.19, bf16[768,2048]{1,0:T(8,128)(2,1)S(1)} %bitcast.20), custom_call_target="tpu_custom_call" | custom-call | flops 2415919104 | bytes 12779520 | tf_op jit(solution)/shard_map/pallas_call | solution.py:235
  199.6 3.9 %all-to-all-start.2 = ((bf16[32,8,2176]{2,1,0:T(8,128)(2,1)}), bf16[32,8,2176]{2,1,0:T(8,128)(2,1)S(1)}, u32[]{:S(2)}, u32[]{:S(2)}) async-start(bf16[32,8,2176]{2,1,0:T(8,128)(2,1)} %bitcast.10), calls=%async_computation.2 | async-start | bytes 2228224 | tf_op jit(solution)/shard_map/all_to_all | solution.py:287
  203.6 0.0 reduce-scatter.2.cloned.1.call-start
  203.6 2.7 convolution_convert_fusion
  206.3 0.0 copy-start.6
  206.3 0.0 reduce-scatter.2.cloned.1.call-update
  206.3 102.7 %all-to-all-done.2 = bf16[32,8,2176]{2,1,0:T(8,128)(2,1)S(1)} async-done(((bf16[32,8,2176]{2,1,0:T(8,128)(2,1)}), bf16[32,8,2176]{2,1,0:T(8,128)(2,1)S(1)}, u32[]{:S(2)}, u32[]{:S(2)}) %all-to-all-start.2) | async-done | bytes 1114144 | tf_op jit(solution)/shard_map/all_to_all | solution.py:287
  309.0 0.4 shard_map.99
  309.5 11.2 %all_to_all.20.home_ref = bf16[4,16,2176]{2,1,0:T(8,128)(2,1)S(1)} all-to-all(bf16[4,16,2176]{2,1,0:T(8,128)(2,1)S(1)} %bitcast.22), channel_id=1, replica_groups=mesh['dp'=8,'node'=16,'y'=4,'zh'=2] {'y'}, dimensions={0} | all-to-all | bytes 557056 | tf_op jit(solution)/shard_map/all_to_all | solution.py:293
  320.7 0.0 copy-done.6
  320.7 0.7 shard_map.100
  321.4 0.0 reduce-scatter.2.cloned.1.call-done
  (1 shorter events, 0.0 us)
Async XLA Ops:
  7.2 1.0 copy-start.3
  8.2 0.8 copy-start.4
  9.0 0.7 copy-start.5
  9.7 0.7 copy-start.7
  12.1 86.2 %all-to-all-start = ((bf16[4,80,1536]{2,1,0:T(8,128)(2,1)}), bf16[4,80,1536]{2,1,0:T(8,128)(2,1)S(1)}, u32[]{:S(2)}, u32[]{:S(2)}) async-start(bf16[4,80,1536]{2,1,0:T(8,128)(2,1)} %get-tuple-element.18), calls=%async_computation | async-start | bytes 1966080 | tf_op jit(solution)/shard_map/all_to_all | solution.py:261
  99.9 88.2 %all-to-all-start.1 = ((bf16[32,8,1536]{2,1,0:T(8,128)(2,1)}), bf16[32,8,1536]{2,1,0:T(8,128)(2,1)S(1)}, u32[]{:S(2)}, u32[]{:S(2)}) async-start(bf16[32,8,1536]{2,1,0:T(8,128)(2,1)} %bitcast.5), calls=%async_computation.1 | async-start | bytes 1572864 | tf_op jit(solution)/shard_map/all_to_all | solution.py:268
  115.9 11.7 %collective-permute-start = (bf16[64,2048]{1,0:T(8,128)(2,1)S(1)}, bf16[64,2048]{1,0:T(8,128)(2,1)S(1)}, u32[]{:S(2)}, u32[]{:S(2)}) collective-permute-start(bf16[64,2048]{1,0:T(8,128)(2,1)S(1)} %get-tuple-element.23), channel_id=1, source_target_pairs={{0,2},{2,4},{4,6},{6,0},{1,3},{3,5},{5,7},{7,1},{8,10},{10,12},{12... | collective-permute-start | bytes 786440 | tf_op jit(solution)/shard_map/ppermute | solution.py:277
  119.8 9.8 %collective-permute-start.1 = (bf16[64,2048]{1,0:T(8,128)(2,1)S(1)}, bf16[64,2048]{1,0:T(8,128)(2,1)S(1)}, u32[]{:S(2)}, u32[]{:S(2)}) collective-permute-start(bf16[64,2048]{1,0:T(8,128)(2,1)S(1)} %get-tuple-element.24), channel_id=1, source_target_pairs={{0,4},{2,6},{4,0},{6,2},{1,5},{3,7},{5,1},{7,3},{8,12},{10,14},{12... | collective-permute-start | bytes 786440 | tf_op jit(solution)/shard_map/ppermute | solution.py:277
  124.2 8.3 %collective-permute-start.2 = (bf16[64,2048]{1,0:T(8,128)(2,1)S(1)}, bf16[64,2048]{1,0:T(8,128)(2,1)S(1)}, u32[]{:S(2)}, u32[]{:S(2)}) collective-permute-start(bf16[64,2048]{1,0:T(8,128)(2,1)S(1)} %get-tuple-element.25), channel_id=1, source_target_pairs={{0,6},{2,0},{4,2},{6,4},{1,7},{3,1},{5,3},{7,5},{8,14},{10,8},{12,... | collective-permute-start | bytes 786440 | tf_op jit(solution)/shard_map/ppermute | solution.py:277
  188.1 1.9 copy-start
  189.9 1.9 copy-start.1
  191.8 1.9 copy-start.2
  199.6 109.4 %all-to-all-start.2 = ((bf16[32,8,2176]{2,1,0:T(8,128)(2,1)}), bf16[32,8,2176]{2,1,0:T(8,128)(2,1)S(1)}, u32[]{:S(2)}, u32[]{:S(2)}) async-start(bf16[32,8,2176]{2,1,0:T(8,128)(2,1)} %bitcast.10), calls=%async_computation.2 | async-start | bytes 2228224 | tf_op jit(solution)/shard_map/all_to_all | solution.py:287
  203.6 117.8 %reduce-scatter.2.cloned.1.call-start = ((), (), s32[]{:S(2)}) async-start(), calls=%async_computation.5 | async-start | bytes 3538944 | tf_op jit(solution)/shard_map/reduce_scatter | solution.py:286
  206.3 114.4 %copy-start.6 = (f32[16,8]{0,1:T(8,128)S(1)}, f32[16,8]{0,1:T(8,128)}, u32[]{:S(2)}) copy-start(f32[16,8]{0,1:T(8,128)} %param.9) | copy-start | bytes 1540
Sparse Core Ops, SparseCore 0:
  208.4 50.5 reduce-scatter.1
